TPU v7x, 32 devices: a whole 2x2x4 slice. The times are simulated.
32 devices in a mesh: grp: 2 (over y), ep: 16 (over z, x, core), tp: 1.
Axes of the slice: x: 2, y: 2, z: 4, core: 2. Of those that a mesh axis runs over, the one named last changes fastest.
Arguments:
- tokens: bfloat16 [2048, 3584], P(('grp', 'ep'), 'tp'), parts along dimension 0, may hold values from -6 to 6
- gate_scores: float32 [2048, 8], P(('grp', 'ep')), parts along dimension 0, may hold values from 0.05 to 1
- route_ids: int32 [2048, 8], P(('grp', 'ep')), parts along dimension 0, may hold values from 0 to 15, all different within a row; in each aligned block of 64 rows (0 to 63, 64 to 127, ...) at most 40 rows name the same one
- gate_codes: float32 [16, 896, 1024], P('ep', None, 'tp'), may hold values from 0 to 65535, as said below
- up_codes: float32 [16, 896, 1024], P('ep', None, 'tp'), may hold values from 0 to 65535, as said below
- down_codes: float32 [16, 256, 3584], P('ep', None, 'tp'), may hold values from 0 to 65535, as said below
- gate_scale: bfloat16 [16, 28, 1024], P('ep', None, 'tp'), may hold values from 0.0019989014 to 0.007507324
- up_scale: bfloat16 [16, 28, 1024], P('ep', None, 'tp'), may hold values from 0.0019989014 to 0.007507324
- down_scale: bfloat16 [16, 8, 3584], P('ep', None, 'tp'), may hold values from 0.0037384033 to 0.014038086
- gate_zero: bfloat16 [16, 28, 1024], P('ep', None, 'tp'), may hold values from 6 to 9
- up_zero: bfloat16 [16, 28, 1024], P('ep', None, 'tp'), may hold values from 6 to 9
- down_zero: bfloat16 [16, 8, 3584], P('ep', None, 'tp'), may hold values from 6 to 9
Outputs:
- mixed: bfloat16 [2048, 3584], P(('grp', 'ep'), 'tp'), parts along dimension 0
There are 2 independent parts, one for each index of `grp`. A program takes and returns all parts, laid end to end along the dimension named above; an argument that names none is the same for every part. Nothing has to cross between parts.
Inputs may be any that keep to these rules, and one draw needn't show every extreme that they name: `route_ids`: each row names 8 different experts; within each aligned block of 64 rows no expert is named by more than 40 rows, a bound that some block reaches. `gate_codes`: every entry is a whole number. `up_codes`: every entry is a whole number. `down_codes`: every entry is a whole number.
All inputs are finite; a program needn't handle non-finite values.
Results may differ from a plain program's by a relative error of at most 0.0076.
Values may be sent and summed in bfloat16 or wider, within the bound.
No kernel may reach another device: no remote copies, remote signals or barrier semaphores. Data moves between devices by JAX's collectives and lax.ppermute only.
A program may use at most 192 MiB of HBM per device.

v0:
```python
import jax
import jax.numpy as jnp
from jax import lax
from jax.sharding import PartitionSpec as P

route_scale = 2.5


def dequantize(words, scales, zeros):
    groups = scales.shape[0]
    packed = words.reshape(groups, words.shape[0] // groups, 1, words.shape[1])
    powers = jnp.array([1.0, 16.0, 256.0, 4096.0], jnp.float32)[None, None, :, None]
    lower = jnp.floor(packed / powers)
    higher = jnp.floor(packed / (16.0 * powers))
    codes = lower - 16.0 * higher
    values = (codes - zeros.astype(jnp.float32)[:, None, None, :]) * scales.astype(jnp.float32)[
        :, None, None, :
    ]
    return values.reshape(-1, words.shape[1]).astype(jnp.bfloat16)


def on_device(
    tokens,
    gate_scores,
    route_ids,
    gate_codes,
    up_codes,
    down_codes,
    gate_scale,
    up_scale,
    down_scale,
    gate_zero,
    up_zero,
    down_zero,
):
    experts = lax.axis_size("ep")
    tok_rows, half_width = tokens.shape
    topk = route_ids.shape[1]
    capacity = min(tok_rows, max(2, 5 * tok_rows * topk // (4 * experts)))
    w_gate = dequantize(gate_codes[0], gate_scale[0], gate_zero[0])
    w_up = dequantize(up_codes[0], up_scale[0], up_zero[0])
    w_down = dequantize(down_codes[0], down_scale[0], down_zero[0])
    flat_ids = route_ids.reshape(-1)
    onehot = (flat_ids[:, None] == jnp.arange(experts, dtype=jnp.int32)[None, :]).astype(jnp.int32)
    earlier = jnp.cumsum(onehot, axis=0) - onehot
    slot = jnp.sum(earlier * onehot, axis=1)
    target = (flat_ids * capacity + slot).reshape(tok_rows, topk)
    places = jnp.arange(experts * capacity, dtype=jnp.int32)
    selector = jnp.sum(
        (places[:, None, None] == target[None, :, :]).astype(jnp.float32), axis=2
    ).astype(jnp.bfloat16)
    outgoing = jnp.dot(selector, tokens, preferred_element_type=jnp.float32).astype(jnp.bfloat16)
    outgoing = outgoing.reshape(experts, capacity, half_width)
    whole = lax.all_gather(
        lax.all_to_all(outgoing, "ep", split_axis=0, concat_axis=0, tiled=True),
        "tp",
        axis=2,
        tiled=True,
    )
    count = whole.shape[1]
    flat_rows = whole.reshape(-1, whole.shape[2])
    gate = jnp.dot(flat_rows, w_gate, preferred_element_type=jnp.float32)
    up = jnp.dot(flat_rows, w_up, preferred_element_type=jnp.float32)
    hidden = (jax.nn.silu(gate) * up).astype(jnp.bfloat16)
    summed = jnp.dot(
        lax.all_gather(hidden, "tp", axis=1, tiled=True), w_down, preferred_element_type=jnp.float32
    )
    answer = summed.astype(jnp.bfloat16).reshape(experts, count, w_down.shape[1])
    returned = lax.all_to_all(answer, "ep", split_axis=0, concat_axis=0, tiled=True)
    weights = route_scale * gate_scores / jnp.sum(gate_scores, axis=1, keepdims=True)
    weighting = jnp.sum(
        jnp.where(places[None, None, :] == target[:, :, None], weights[:, :, None], 0.0), axis=1
    )
    answers = returned.reshape(experts * capacity, half_width).astype(jnp.float32)
    combined = jnp.dot(weighting, answers, precision=lax.Precision.HIGHEST)
    return combined.astype(jnp.bfloat16)


def solution(mesh):
    in_specs = (
        P(("grp", "ep"), "tp"),
        P(("grp", "ep"), None),
        P(("grp", "ep"), None),
        P("ep", None, "tp"),
        P("ep", None, "tp"),
        P("ep", None, "tp"),
        P("ep", None, "tp"),
        P("ep", None, "tp"),
        P("ep", None, "tp"),
        P("ep", None, "tp"),
        P("ep", None, "tp"),
        P("ep", None, "tp"),
    )
    out_specs = P(("grp", "ep"), "tp")
    return jax.shard_map(
        on_device, mesh=mesh, in_specs=in_specs, out_specs=out_specs, check_vma=False
    )
```

profile of v0, /device:TPU:11, one launch (start us, length us, event | category | flops | bytes accessed | tf_op | source)
XLA Modules:
  0.0 285.3 jit_solution(6158303330354679578)
XLA Ops:
  0.0 0.8 copy.31
  1.0 1.2 reduce-window.6
  2.2 0.2 slice_reduce_fusion
  2.7 0.7 multiply_add_fusion
  3.5 0.5 convert_reduce_fusion
  4.0 3.6 %convolution_convert_fusion = bf16[640,3584]{1,0:T(8,128)(2,1)} fusion(bf16[64,3584]{1,0:T(8,128)(2,1)S(1)} %copy-done, bf16[640,64]{0,1:T(8,128)(2,1)S(1)} %convert_reduce_fusion), kind=kOutput, calls=%fused_computation.17 | convolution fusion | flops 295895040 | bytes 5128192 | tf_op jit(solution)/shard_map/dot_general | solution.py:52
  7.7 6.6 %all-to-all-start = ((bf16[16,40,3584]{2,1,0:T(8,128)(2,1)}), bf16[16,40,3584]{2,1,0:T(8,128)(2,1)}, u32[]{:S(2)}, u32[]{:S(2)}) async-start(bf16[16,40,3584]{2,1,0:T(8,128)(2,1)} %bitcast.74), calls=%async_computation | async-start | bytes 9175040 | tf_op jit(solution)/shard_map/all_to_all | solution.py:55
  14.3 23.0 %fusion.4 = (bf16[28,32,4,1024]{3,2,1,0:T(4,128)(2,1)}, bf16[28,32,4,1024]{3,2,1,0:T(4,128)(2,1)}) fusion(f32[4]{0:T(128)S(1)} %copy-done.12, f32[4]{0:T(128)S(1)} %copy-done.11, f32[28,1024]{1,0:T(8,128)S(1)} %get-tuple-element.7, f32[28,1024]{1,0:T(8,128)S(1)} %get-tuple-element.8, f32[28,32,1024]{2,1,0:T(8,128)} %bitcast.76, ...), kind=kLoop, calls=%fused_computation.5 | loop fusion | flops 66060288 | bytes 22478880 | tf_op jit(solution)/shard_map/convert_element_type | solution.py:19
  37.3 11.1 %convert_element_type.123 = bf16[3584,1024]{1,0:T(8,128)(2,1)} reshape(bf16[28,32,4,1024]{3,2,1,0:T(4,128)(2,1)} %get-tuple-element.6) | data formatting | bytes 14680064 | tf_op jit(solution)/shard_map/convert_element_type | solution.py:19
  48.4 11.1 %convert_element_type.129 = bf16[3584,1024]{1,0:T(8,128)(2,1)} reshape(bf16[28,32,4,1024]{3,2,1,0:T(4,128)(2,1)} %get-tuple-element.5) | data formatting | bytes 14680064 | tf_op jit(solution)/shard_map/convert_element_type | solution.py:19
  59.5 7.4 %mul.128 = f32[8,32,4,3584]{3,2,1,0:T(4,128)} broadcast(f32[8,3584]{1,0:T(8,128)S(1)} %bitcast_convert_fusion.4), dimensions={0,3} | broadcast | bytes 14794752 | tf_op jit(solution)/shard_map/mul | solution.py:16
  66.9 17.3 %mul.129 = f32[1024,3584]{1,0:T(8,128)} reshape(f32[8,32,4,3584]{3,2,1,0:T(4,128)} %mul.128) | data formatting | bytes 29360128 | tf_op jit(solution)/shard_map/mul | solution.py:16
  84.3 7.4 %sub.80 = f32[8,32,4,3584]{3,2,1,0:T(4,128)} broadcast(f32[8,3584]{1,0:T(8,128)S(1)} %bitcast_convert_fusion.5), dimensions={0,3} | broadcast | bytes 14794752 | tf_op jit(solution)/shard_map/sub | solution.py:16
  91.7 17.3 %sub.81 = f32[1024,3584]{1,0:T(8,128)} reshape(f32[8,32,4,3584]{3,2,1,0:T(4,128)} %sub.80) | data formatting | bytes 29360128 | tf_op jit(solution)/shard_map/sub | solution.py:16
  109.0 8.8 %div.150 = f32[8,32,4,3584]{3,2,1,0:T(4,128)} broadcast(f32[8,32,3584]{2,1,0:T(8,128)} %bitcast.78), dimensions={0,1,3} | broadcast | bytes 18350080 | tf_op jit(solution)/shard_map/div | solution.py:13
  117.8 17.4 %div.151 = f32[1024,3584]{1,0:T(8,128)} reshape(f32[8,32,4,3584]{3,2,1,0:T(4,128)} %div.150) | data formatting | bytes 29360128 | tf_op jit(solution)/shard_map/div | solution.py:13
  135.2 0.1 div.153
  135.5 8.7 %fusion.18 = f32[640,1024]{1,0:T(8,128)S(1)} fusion(bf16[640,3584]{1,0:T(8,128)(2,1)} %bitcast.2, bf16[3584,1024]{1,0:T(8,128)(2,1)} %convert_element_type.123), kind=kOutput, calls=%fused_computation.43 | convolution fusion | flops 4697620480 | bytes 14548992 | tf_op jit(solution)/shard_map/dot_general | solution.py:62
  144.2 9.6 %fusion.47 = bf16[640,1024]{1,0:T(8,128)(2,1)S(1)} fusion(bf16[3584,1024]{1,0:T(8,128)(2,1)} %convert_element_type.129, bf16[640,3584]{1,0:T(8,128)(2,1)} %bitcast.2, f32[640,1024]{1,0:T(8,128)S(1)} %fusion.18), kind=kOutput, calls=%bitcast_fusion.clone.2 | convolution fusion | flops 4701552640 | bytes 15859712 | tf_op jit(solution)/shard_map/dot_general | solution.py:63
  153.8 18.9 %fusion.11 = bf16[640,3584]{1,0:T(8,128)(2,1)} fusion(f32[1024,3584]{1,0:T(8,128)} %mul.129, f32[1024,3584]{1,0:T(8,128)} %sub.81, f32[1024,3584]{1,0:T(8,128)} %div.151, f32[1024]{0:T(1024)S(1)} %div.157, f32[1024]{0:T(1024)S(1)} %div.153, bf16[640,1024]{1,0:T(8,128)(2,1)S(1)} %fusion.47), kind=kOutput, calls=%fused_computation.16 | convolution fusion | flops 4732944384 | bytes 49946624 | tf_op jit(solution)/shard_map/dot_general | solution.py:65
  172.8 6.1 %all-to-all-start.1 = ((bf16[16,40,3584]{2,1,0:T(8,128)(2,1)}), bf16[16,40,3584]{2,1,0:T(8,128)(2,1)}, u32[]{:S(2)}, u32[]{:S(2)}) async-start(bf16[16,40,3584]{2,1,0:T(8,128)(2,1)} %bitcast.75), calls=%async_computation.1 | async-start | bytes 9175040 | tf_op jit(solution)/shard_map/all_to_all | solution.py:69
  179.0 0.5 select_reduce_fusion
  179.5 100.3 %all-to-all-done.1 = bf16[16,40,3584]{2,1,0:T(8,128)(2,1)} async-done(((bf16[16,40,3584]{2,1,0:T(8,128)(2,1)}), bf16[16,40,3584]{2,1,0:T(8,128)(2,1)}, u32[]{:S(2)}, u32[]{:S(2)}) %all-to-all-start.1) | async-done | bytes 4587552 | tf_op jit(solution)/shard_map/all_to_all | solution.py:69
  279.8 5.5 %convolution_convert_fusion.1 = bf16[64,3584]{1,0:T(8,128)(2,1)} fusion(f32[64,640]{1,0:T(8,128)S(1)} %select_reduce_fusion, bf16[640,3584]{1,0:T(8,128)(2,1)} %bitcast.13), kind=kOutput, calls=%fused_computation.18 | convolution fusion | flops 1761837056 | bytes 5210112 | tf_op jit(solution)/shard_map/dot_general | solution.py:75
  (46 shorter events, 0.9 us)
Async XLA Ops:
  0.0 3.9 %copy-start = (bf16[64,3584]{1,0:T(8,128)(2,1)S(1)}, bf16[64,3584]{1,0:T(8,128)(2,1)}, u32[]{:S(2)}) copy-start(bf16[64,3584]{1,0:T(8,128)(2,1)} %param.15) | copy-start | bytes 1376260
  4.0 10.3 %copy-start.2 = (bf16[1,28,1024]{2,1,0:T(8,128)(2,1)S(1)}, bf16[1,28,1024]{2,1,0:T(8,128)(2,1)}, u32[]{:S(2)}) copy-start(bf16[1,28,1024]{2,1,0:T(8,128)(2,1)} %param.21) | copy-start | bytes 172036
  4.0 10.3 %copy-start.3 = (bf16[1,28,1024]{2,1,0:T(8,128)(2,1)S(1)}, bf16[1,28,1024]{2,1,0:T(8,128)(2,1)}, u32[]{:S(2)}) copy-start(bf16[1,28,1024]{2,1,0:T(8,128)(2,1)} %param.24) | copy-start | bytes 172036
  4.0 10.3 %copy-start.4 = (bf16[1,28,1024]{2,1,0:T(8,128)(2,1)S(1)}, bf16[1,28,1024]{2,1,0:T(8,128)(2,1)}, u32[]{:S(2)}) copy-start(bf16[1,28,1024]{2,1,0:T(8,128)(2,1)} %param.22) | copy-start | bytes 172036
  4.0 10.3 %copy-start.5 = (bf16[1,28,1024]{2,1,0:T(8,128)(2,1)S(1)}, bf16[1,28,1024]{2,1,0:T(8,128)(2,1)}, u32[]{:S(2)}) copy-start(bf16[1,28,1024]{2,1,0:T(8,128)(2,1)} %param.25) | copy-start | bytes 172036
  4.0 10.3 %copy-start.11 = (f32[4]{0:T(128)S(1)}, f32[4]{0:T(128)}, u32[]{:S(2)}) copy-start(f32[4]{0:T(128)} %constant.31) | copy-start | bytes 52
  4.0 10.3 %copy-start.12 = (f32[4]{0:T(128)S(1)}, f32[4]{0:T(128)}, u32[]{:S(2)}) copy-start(f32[4]{0:T(128)} %constant.34) | copy-start | bytes 52
  7.7 127.8 %all-to-all-start = ((bf16[16,40,3584]{2,1,0:T(8,128)(2,1)}), bf16[16,40,3584]{2,1,0:T(8,128)(2,1)}, u32[]{:S(2)}, u32[]{:S(2)}) async-start(bf16[16,40,3584]{2,1,0:T(8,128)(2,1)} %bitcast.74), calls=%async_computation | async-start | bytes 9175040 | tf_op jit(solution)/shard_map/all_to_all | solution.py:55
  48.4 11.1 %copy-start.6 = (bf16[1,8,3584]{2,1,0:T(8,128)(2,1)S(1)}, bf16[1,8,3584]{2,1,0:T(8,128)(2,1)}, u32[]{:S(2)}) copy-start(bf16[1,8,3584]{2,1,0:T(8,128)(2,1)} %param.23) | copy-start | bytes 172036
  66.9 17.3 %copy-start.7 = (bf16[1,8,3584]{2,1,0:T(8,128)(2,1)S(1)}, bf16[1,8,3584]{2,1,0:T(8,128)(2,1)}, u32[]{:S(2)}) copy-start(bf16[1,8,3584]{2,1,0:T(8,128)(2,1)} %param.26) | copy-start | bytes 172036
  117.8 17.4 %copy-start.10 = (f32[4]{0:T(128)S(1)}, f32[4]{0:T(128)}, u32[]{:S(2)}) copy-start(f32[4]{0:T(128)} %constant.21.clone) | copy-start | bytes 52
  117.8 17.5 %copy-start.9 = (f32[4]{0:T(128)S(1)}, f32[4]{0:T(128)}, u32[]{:S(2)}) copy-start(f32[4]{0:T(128)} %constant.33) | copy-start | bytes 52
  153.8 131.5 %copy-start.1 = (bf16[64,3584]{1,0:T(8,128)(2,1)S(1)}, bf16[64,3584]{1,0:T(8,128)(2,1)}, u32[]{:S(2)}) copy-start(bf16[64,3584]{1,0:T(8,128)(2,1)} %param.15) | copy-start | bytes 1376260
  172.8 6.2 %copy-start.8 = (f32[64,8]{0,1:T(8,128)S(1)}, f32[64,8]{0,1:T(8,128)}, u32[]{:S(2)}) copy-start(f32[64,8]{0,1:T(8,128)} %param.16) | copy-start | bytes 6148
  172.8 107.0 %all-to-all-start.1 = ((bf16[16,40,3584]{2,1,0:T(8,128)(2,1)}), bf16[16,40,3584]{2,1,0:T(8,128)(2,1)}, u32[]{:S(2)}, u32[]{:S(2)}) async-start(bf16[16,40,3584]{2,1,0:T(8,128)(2,1)} %bitcast.75), calls=%async_computation.1 | async-start | bytes 9175040 | tf_op jit(solution)/shard_map/all_to_all | solution.py:69
where the time goes:
time: 288 us; the launch traced here: 285 us
  waiting for transfers between devices  100 us (35%)
  local copies, waits for them, and re-layouts  99.7 us (35%)
  matrix products  46.4 us (16%)
  other arithmetic  26 us (9%)
  starting transfers between devices  12.7 us (4%)
    all_to_all x1, waiting for transfers between devices, on_device(): lax.all_to_all(answer, 'ep', split_axis=0, concat_axis=0, tiled=True)  100 us
    div x4, local copies, waits for them, and re-layouts, dequantize(): lower = jnp.floor(packed / powers)  26.3 us
    mul x2, local copies, waits for them, and re-layouts, dequantize(): (codes - zeros.astype(jnp.float32)[:, None, None, :]) * scales.astype(jnp...  24.7 us
    sub x2, local copies, waits for them, and re-layouts, dequantize(): codes - zeros.astype(jnp.float32)[:, None, None, :]  24.7 us
    convert_element_type x1, other arithmetic, dequantize(): return values.reshape(-1, words.shape[1]).astype(jnp.bfloat16)  23 us
    convert_element_type x2, local copies, waits for them, and re-layouts, dequantize(): return values.reshape(-1, words.shape[1]).astype(jnp.bfloat16)  22.2 us
    dot_general x1, matrix products, on_device(): jnp.dot(lax.all_gather(hidden, 'tp', axis=1, tiled=True), w_down, preferr...  18.9 us
    dot_general x1, matrix products, on_device(): up = jnp.dot(flat_rows, w_up, preferred_element_type=jnp.float32)  9.57 us
  transfers between devices with their start and end apart: 2, of which 1 were waited for; matrix products, arithmetic and copies ran while one was open for 43% of the time, Pallas kernels for 0%

commit v1 on v0

--- a/solution.py
+++ b/solution.py
@@ -1,9 +1,19 @@
+import functools
+
 import jax
 import jax.numpy as jnp
 from jax import lax
+from jax.experimental import pallas as pl
+from jax.experimental.pallas import tpu as pltpu
 from jax.sharding import PartitionSpec as P
 
 route_scale = 2.5
+GROUP = 128
+WORD = 4
+CHUNK = GROUP * WORD
+EXTRA = 128
+F32 = jnp.float32
+BF16 = jnp.bfloat16
 
 
 def dequantize(words, scales, zeros):
@@ -19,7 +29,7 @@
     return values.reshape(-1, words.shape[1]).astype(jnp.bfloat16)
 
 
-def on_device(
+def routed(
     tokens,
     gate_scores,
     route_ids,
@@ -76,6 +86,225 @@
     return combined.astype(jnp.bfloat16)
 
 
+def prepare_kernel(experts, tokens, scores, ids, rows, perm):
+    source = lax.broadcasted_iota(jnp.int32, (CHUNK, CHUNK), 0)
+    place = lax.broadcasted_iota(jnp.int32, (CHUNK, CHUNK), 1)
+    perm[...] = jnp.where((source & 3) * GROUP + (source >> 2) == place, 1.0, 0.0).astype(BF16)
+    width = tokens.shape[1]
+    for at in range(0, width, CHUNK):
+        rows[:, at : at + CHUNK] = jnp.dot(
+            tokens[:, at : at + CHUNK], perm[...], preferred_element_type=F32
+        ).astype(BF16)
+    weights = route_scale * scores[...] / jnp.sum(scores[...], axis=1, keepdims=True)
+    lane = lax.broadcasted_iota(jnp.int32, (tokens.shape[0], EXTRA), 1)
+    spread = jnp.zeros((tokens.shape[0], EXTRA), F32)
+    for k in range(ids.shape[1]):
+        spread += jnp.where(lane % experts == ids[:, k : k + 1], weights[:, k : k + 1], 0.0)
+    high = spread.astype(BF16).astype(F32)
+    mid = (spread - high).astype(BF16).astype(F32)
+    low = spread - high - mid
+    part = lane // experts
+    rows[:, width:] = jnp.where(
+        part == 0, high, jnp.where(part == 1, mid, jnp.where(part == 2, low, 0.0))
+    ).astype(BF16)
+
+
+def prepare(tokens, scores, ids, experts):
+    n, width = tokens.shape
+    return pl.pallas_call(
+        functools.partial(prepare_kernel, experts),
+        out_shape=(
+            jax.ShapeDtypeStruct((n, width + EXTRA), BF16),
+            jax.ShapeDtypeStruct((CHUNK, CHUNK), BF16),
+        ),
+        name="prepare",
+    )(tokens, scores, ids)
+
+
+def unpack_chunk(words, scale, zero, at, out, tiles, tile):
+    sub = GROUP // WORD
+    for t in range(tiles):
+        cols = slice(t * tile, (t + 1) * tile)
+        for g in range(WORD):
+            s = scale[pl.ds(at * WORD + g, 1), cols]
+            z = zero[pl.ds(at * WORD + g, 1), cols]
+            w = words[g * sub : (g + 1) * sub, cols].astype(jnp.int32)
+            for j in range(WORD):
+                code = ((w >> (4 * j)) & 15).astype(F32)
+                out[t, j * GROUP + g * sub : j * GROUP + (g + 1) * sub, :] = (
+                    (code - z) * s
+                ).astype(BF16)
+
+
+def unpack_kernel(pairs, tiles, tile, *refs):
+    ins, outs, scratch = refs[: 3 * pairs], refs[3 * pairs : 4 * pairs], refs[4 * pairs :]
+    at = pl.program_id(0)
+
+    @pl.when(at == 0)
+    def _():
+        for p in range(pairs):
+            scratch[2 * p][...] = ins[3 * p + 1][...].astype(F32)
+            scratch[2 * p + 1][...] = ins[3 * p + 2][...].astype(F32)
+
+    for p in range(pairs):
+        unpack_chunk(
+            ins[3 * p], scratch[2 * p], scratch[2 * p + 1], at, outs[p], tiles, tile
+        )
+
+
+def unpack(triples, tile):
+    words, scale, _ = triples[0]
+    n, cols = words.shape
+    tiles = cols // tile
+    steps = n // GROUP
+    in_specs, args, scratch = [], [], []
+    for w, s, z in triples:
+        in_specs += [
+            pl.BlockSpec((GROUP, cols), lambda i: (i, 0)),
+            pl.BlockSpec(s.shape, lambda i: (0, 0)),
+            pl.BlockSpec(z.shape, lambda i: (0, 0)),
+        ]
+        args += [w, s, z]
+        scratch += [pltpu.VMEM(s.shape, F32), pltpu.VMEM(z.shape, F32)]
+    return pl.pallas_call(
+        functools.partial(unpack_kernel, len(triples), tiles, tile),
+        grid=(steps,),
+        in_specs=in_specs,
+        out_specs=[pl.BlockSpec((tiles, CHUNK, tile), lambda i: (0, i, 0)) for _ in triples],
+        out_shape=[jax.ShapeDtypeStruct((tiles, n * WORD, tile), BF16) for _ in triples],
+        scratch_shapes=scratch,
+        compiler_params=pltpu.CompilerParams(vmem_limit_bytes=40 * 1024 * 1024),
+        cost_estimate=pl.CostEstimate(
+            flops=n * cols * 24 * len(triples),
+            bytes_accessed=n * cols * 12 * len(triples),
+            transcendentals=0,
+        ),
+        name="unpack",
+    )(*args)
+
+
+def expert_kernel(
+    experts, first, mine, x0, x1, x2, x3, perm, wg, wu, wd, keep, send, xs, hs, hp, col
+):
+    i = pl.program_id(0)
+    n, width = x0.shape[0], x0.shape[1] - EXTRA
+    half = first // 2
+
+    @pl.when(i == 0)
+    def _():
+        for at, x in enumerate((x0, x1, x2, x3)):
+            xs[at * n : (at + 1) * n, :] = x[:, :width]
+            parts = x[:, width:].astype(F32)
+            lane = lax.broadcasted_iota(jnp.int32, parts.shape, 1)
+            parts = jnp.where(lane % experts == mine[0], parts, 0.0)
+            col[at * n : (at + 1) * n, :] = jnp.sum(parts, axis=1, keepdims=True)
+
+    @pl.when(i < first)
+    def _():
+        gate = jnp.dot(xs[...], wg[0], preferred_element_type=F32)
+        up = jnp.dot(xs[...], wu[0], preferred_element_type=F32)
+        hs[i] = (gate / (1.0 + jnp.exp(-gate)) * up).astype(BF16)
+
+    @pl.when(i == first)
+    def _():
+        tile = hs.shape[2]
+        each = CHUNK // tile
+        for c in range(first // each):
+            total = None
+            for b in range(each):
+                part = jnp.dot(
+                    hs[c * each + b], perm[b * tile : (b + 1) * tile, :], preferred_element_type=F32
+                )
+                total = part if total is None else total + part
+            hp[:, c * CHUNK : (c + 1) * CHUNK] = total.astype(BF16)
+
+    @pl.when(i >= first)
+    def _():
+        answer = jnp.dot(hp[...], wd[0], preferred_element_type=F32) * col[...]
+        keep[...] = answer[: 2 * n].astype(BF16)
+        send[...] = answer[2 * n :].astype(BF16)
+
+
+def expert_block(mine, shards, perm, wg, wu, wd, experts):
+    n, wide = shards[0].shape
+    width = wide - EXTRA
+    first, _, tile = wg.shape
+    second, hidden, otile = wd.shape
+    whole = lambda a: pl.BlockSpec(a.shape, lambda i: (0,) * a.ndim)
+    flops = 2 * 4 * n * width * hidden * 3
+    return pl.pallas_call(
+        functools.partial(expert_kernel, experts, first),
+        grid=(first + second,),
+        in_specs=[pl.BlockSpec(memory_space=pltpu.SMEM)]
+        + [whole(s) for s in shards]
+        + [
+            whole(perm),
+            pl.BlockSpec((1, width, tile), lambda i: (jnp.minimum(i, first - 1), 0, 0)),
+            pl.BlockSpec((1, width, tile), lambda i: (jnp.minimum(i, first - 1), 0, 0)),
+            pl.BlockSpec((1, hidden, otile), lambda i: (jnp.maximum(i - first, 0), 0, 0)),
+        ],
+        out_specs=[
+            pl.BlockSpec((2 * n, otile), lambda i: (0, jnp.maximum(i - first, 0))),
+            pl.BlockSpec((2 * n, otile), lambda i: (0, jnp.maximum(i - first, 0))),
+        ],
+        out_shape=[jax.ShapeDtypeStruct((2 * n, width), BF16)] * 2,
+        scratch_shapes=[
+            pltpu.VMEM((4 * n, width), BF16),
+            pltpu.VMEM((first, 4 * n, tile), BF16),
+            pltpu.VMEM((4 * n, hidden), BF16),
+            pltpu.VMEM((4 * n, 1), F32),
+        ],
+        compiler_params=pltpu.CompilerParams(vmem_limit_bytes=40 * 1024 * 1024),
+        cost_estimate=pl.CostEstimate(
+            flops=flops,
+            bytes_accessed=3 * width * hidden * 2,
+            transcendentals=4 * n * hidden,
+        ),
+        name="expert_block",
+    )(mine, *shards, perm, wg, wu, wd)
+
+
+def dense(
+    tokens,
+    gate_scores,
+    route_ids,
+    gate_codes,
+    up_codes,
+    down_codes,
+    gate_scale,
+    up_scale,
+    down_scale,
+    gate_zero,
+    up_zero,
+    down_zero,
+):
+    experts = lax.axis_size("ep")
+    planes = experts // 4
+    n = tokens.shape[0]
+    mine = lax.axis_index("ep").astype(jnp.int32).reshape(1)
+
+    def swap(value, bits):
+        return lax.ppermute(value, "ep", [(i, i ^ bits) for i in range(experts)])
+
+    rows, perm = prepare(tokens, gate_scores, route_ids, experts)
+    w_gate, w_up = unpack(
+        [(gate_codes[0], gate_scale[0], gate_zero[0]), (up_codes[0], up_scale[0], up_zero[0])], 256
+    )
+    (w_down,) = unpack([(down_codes[0], down_scale[0], down_zero[0])], 512)
+
+    total = None
+    for k in range(planes):
+        here = rows if k == 0 else swap(rows, 4 * k)
+        across = swap(here, 2)
+        shards = [here, across, swap(here, 1), swap(across, 1)]
+        keep, send = expert_block(mine, shards, perm, w_gate, w_up, w_down, experts)
+        pair = keep.astype(F32) + swap(send, 1).astype(F32)
+        plane = pair[:n] + swap(pair[n:].astype(BF16), 2).astype(F32)
+        back = plane if k == 0 else swap(plane.astype(BF16), 4 * k).astype(F32)
+        total = back if total is None else total + back
+    return total.astype(BF16)
+
+
 def solution(mesh):
     in_specs = (
         P(("grp", "ep"), "tp"),
@@ -92,6 +321,12 @@
         P("ep", None, "tp"),
     )
     out_specs = P(("grp", "ep"), "tp")
+    experts = mesh.shape["ep"]
+    few = mesh.shape["tp"] == 1 and experts % 4 == 0 and 3 * experts <= EXTRA
     return jax.shard_map(
-        on_device, mesh=mesh, in_specs=in_specs, out_specs=out_specs, check_vma=False
-    )
+        dense if few and experts & (experts - 1) == 0 else routed,
+        mesh=mesh,
+        in_specs=in_specs,
+        out_specs=out_specs,
+        check_vma=False,
+    )

time: 288 us -> 192 us (0.67)
  the two profiles are of different devices: /device:TPU:11 before, /device:TPU:8 now
where the time goes in v1:
time: 192 us; the launch traced here: 191 us
  waiting for transfers between devices  87.1 us (45%)
  Pallas kernels  69.2 us (36%)
  starting transfers between devices  18.1 us (9%)
  local copies, waits for them, and re-layouts  14.5 us (8%)
  other arithmetic  2.23 us (1%)
    ppermute x26, waiting for transfers between devices, swap(): return lax.ppermute(value, 'ep', [(i, i ^ bits) for i in range(experts)])  87.1 us
    pallas_call x4, Pallas kernels, expert_block(): pl.pallas_call(functools.partial(expert_kernel, experts, first), grid=(fi...  54.6 us
    ppermute x26, starting transfers between devices, swap(): return lax.ppermute(value, 'ep', [(i, i ^ bits) for i in range(experts)])  18.1 us
    unnamed x34, local copies, waits for them, and re-layouts  14.3 us
    pallas_call x2, Pallas kernels, unpack(): pl.pallas_call(functools.partial(unpack_kernel, len(triples), tiles, tile...  11.9 us
  transfers between devices with their start and end apart: 26, of which 8 were waited for; matrix products, arithmetic and copies ran while one was open for 1% of the time, Pallas kernels for 35%

profile of v1, /device:TPU:8, one launch (start us, length us, event | category | flops | bytes accessed | tf_op | source)
XLA Modules:
  0.0 191.3 jit_solution(14761220227286674328)
XLA Ops:
  2.8 2.7 %prepare.1 = (bf16[64,3712]{1,0:T(8,128)(2,1)}, bf16[512,512]{1,0:T(8,128)(2,1)}) custom-call(bf16[64,3584]{1,0:T(8,128)(2,1)} %tokens.1, f32[64,8]{1,0:T(8,128)} %copy.13.scores, s32[64,8]{1,0:T(8,128)} %copy.14.ids), custom_call_target="tpu_custom_call" | custom-call | tf_op jit(solution)/shard_map/prepare/pallas_call | solution.py:114
  5.4 1.9 %collective-permute-start = (bf16[64,3712]{1,0:T(8,128)(2,1)}, bf16[64,3712]{1,0:T(8,128)(2,1)S(1)}, u32[]{:S(2)}, u32[]{:S(2)}) collective-permute-start(bf16[64,3712]{1,0:T(8,128)(2,1)} %get-tuple-element.17.x0), channel_id=1, source_target_pairs={{0,2},{1,3},{2,0},{3,1},{4,6},{5,7},{6,4},{7,5},{8,10},{9,11},{10,... | collective-permute-start | bytes 1425416 | tf_op jit(solution)/shard_map/ppermute | solution.py:287
  7.4 2.6 %collective-permute-start.12 = (bf16[64,3712]{1,0:T(8,128)(2,1)}, bf16[64,3712]{1,0:T(8,128)(2,1)S(1)}, u32[]{:S(2)}, u32[]{:S(2)}) collective-permute-start(bf16[64,3712]{1,0:T(8,128)(2,1)} %get-tuple-element.17.x0), channel_id=1, source_target_pairs={{0,8},{1,9},{2,10},{3,11},{4,12},{5,13},{6,14},{7,15},{8,0},{9,1},... | collective-permute-start | bytes 1425416 | tf_op jit(solution)/shard_map/ppermute | solution.py:287
  10.4 14.4 %collective-permute-done.5.x0 = bf16[64,3712]{1,0:T(8,128)(2,1)S(1)} collective-permute-done((bf16[64,3712]{1,0:T(8,128)(2,1)}, bf16[64,3712]{1,0:T(8,128)(2,1)S(1)}, u32[]{:S(2)}, u32[]{:S(2)}) %collective-permute-start.5) | collective-permute-done | bytes 475168 | tf_op jit(solution)/shard_map/ppermute | solution.py:287
  24.8 2.1 %collective-permute-start.6 = (bf16[64,3712]{1,0:T(8,128)(2,1)S(1)}, bf16[64,3712]{1,0:T(8,128)(2,1)S(1)}, u32[]{:S(2)}, u32[]{:S(2)}) collective-permute-start(bf16[64,3712]{1,0:T(8,128)(2,1)S(1)} %collective-permute-done.5.x0), channel_id=1, source_target_pairs={{0,2},{1,3},{2,0},{3,1},{4,6},{5,7},{6,4},{7,5},{8,10},{9,11},{10,... | collective-permute-start | bytes 1425416 | tf_op jit(solution)/shard_map/ppermute | solution.py:287
  27.0 2.0 %copy-done.6 = f32[1,256,3584]{2,1,0:T(8,128)S(1)} copy-done((f32[1,256,3584]{2,1,0:T(8,128)S(1)}, f32[1,256,3584]{2,1,0:T(8,128)}, u32[]{:S(2)}) %copy-start.6) | copy-done | bytes 3670040
  30.7 3.3 %unpack.3.wd = bf16[7,1024,512]{2,1,0:T(8,128)(2,1)S(1)} custom-call(f32[256,3584]{1,0:T(8,128)S(1)} %bitcast.12, bf16[8,3584]{1,0:T(8,128)(2,1)S(1)} %bitcast.17, bf16[8,3584]{1,0:T(8,128)(2,1)S(1)} %bitcast.18), custom_call_target="tpu_custom_call" | custom-call | flops 22020096 | bytes 11010048 | tf_op jit(solution)/shard_map/unpack/pallas_call | solution.py:169
  33.9 2.9 %copy-done = bf16[7,1024,512]{2,1,0:T(8,128)(2,1)} copy-done((bf16[7,1024,512]{2,1,0:T(8,128)(2,1)}, bf16[7,1024,512]{2,1,0:T(8,128)(2,1)S(1)}, u32[]{:S(2)}) %copy-start) | copy-done | bytes 7340056
  36.9 8.6 %unpack.2 = (bf16[4,3584,256]{2,1,0:T(8,128)(2,1)}, bf16[4,3584,256]{2,1,0:T(8,128)(2,1)}) custom-call(f32[896,1024]{1,0:T(8,128)S(1)} %bitcast.10, bf16[28,1024]{1,0:T(8,128)(2,1)S(1)} %bitcast.13, bf16[28,1024]{1,0:T(8,128)(2,1)S(1)} %bitcast.14, f32[896,1024]{1,0:T(8,128)S(1)} %bitcast.11, bf16[28,1024]{1,0:T(8,128)(2,1)S(1)} %bitcast.15, ...), custom_call_target="tpu_custom_call" | custom-call | flops 44040192 | bytes 22020096 | tf_op jit(solution)/shard_map/unpack/pallas_call | solution.py:169
  46.0 5.2 %collective-permute-done.19.x0 = bf16[64,3712]{1,0:T(8,128)(2,1)S(1)} collective-permute-done((bf16[64,3712]{1,0:T(8,128)(2,1)}, bf16[64,3712]{1,0:T(8,128)(2,1)S(1)}, u32[]{:S(2)}, u32[]{:S(2)}) %collective-permute-start.19) | collective-permute-done | bytes 475168 | tf_op jit(solution)/shard_map/ppermute | solution.py:287
  51.8 1.6 collective-permute-start.20
  53.5 3.1 %copy-done.1 = bf16[4,3584,256]{2,1,0:T(8,128)(2,1)S(1)} copy-done((bf16[4,3584,256]{2,1,0:T(8,128)(2,1)S(1)}, bf16[4,3584,256]{2,1,0:T(8,128)(2,1)}, u32[]{:S(2)}) %copy-start.1) | copy-done | bytes 7340056
  56.6 14.5 %expert_block.4 = (bf16[128,3584]{1,0:T(8,128)(2,1)S(1)}, bf16[128,3584]{1,0:T(8,128)(2,1)}) custom-call(s32[1]{0:T(128)} %bitcast.mine, bf16[64,3712]{1,0:T(8,128)(2,1)S(1)} %copy-done.7, bf16[64,3712]{1,0:T(8,128)(2,1)S(1)} %collective-permute-done.x1, bf16[64,3712]{1,0:T(8,128)(2,1)S(1)} %collective-permute-done.1.x2, ...), custom_call_target="tpu_custom_call" | custom-call | flops 5637144576 | bytes 22020096 | tf_op jit(solution)/shard_map/expert_block/pallas_call | solution.py:235
  74.9 13.4 %expert_block.5 = (bf16[128,3584]{1,0:T(8,128)(2,1)S(1)}, bf16[128,3584]{1,0:T(8,128)(2,1)S(1)}) custom-call(s32[1]{0:T(128)} %bitcast.mine, bf16[64,3712]{1,0:T(8,128)(2,1)S(1)} %collective-permute-done.5.x0, bf16[64,3712]{1,0:T(8,128)(2,1)S(1)} %collective-permute-done.6.x1, bf16[64,3712]{1,0:T(8,128)(2,1)S(1)} %collective-permute-done.7.x2, ...), custom_call_target="tpu_custom_call" | custom-call | flops 5637144576 | bytes 22020096 | tf_op jit(solution)/shard_map/expert_block/pallas_call | solution.py:235
  88.4 13.4 %expert_block.6 = (bf16[128,3584]{1,0:T(8,128)(2,1)S(1)}, bf16[128,3584]{1,0:T(8,128)(2,1)S(1)}) custom-call(s32[1]{0:T(128)} %bitcast.mine, bf16[64,3712]{1,0:T(8,128)(2,1)S(1)} %collective-permute-done.12.x0, bf16[64,3712]{1,0:T(8,128)(2,1)S(1)} %collective-permute-done.13.x1, bf16[64,3712]{1,0:T(8,128)(2,1)S(1)} %collective-permute-done.14.x2, ...), custom_call_target="tpu_custom_call" | custom-call | flops 5637144576 | bytes 22020096 | tf_op jit(solution)/shard_map/expert_block/pallas_call | solution.py:235
  102.3 13.4 %expert_block.7 = (bf16[128,3584]{1,0:T(8,128)(2,1)S(1)}, bf16[128,3584]{1,0:T(8,128)(2,1)S(1)}) custom-call(s32[1]{0:T(128)} %bitcast.mine, bf16[64,3712]{1,0:T(8,128)(2,1)S(1)} %collective-permute-done.19.x0, bf16[64,3712]{1,0:T(8,128)(2,1)S(1)} %collective-permute-done.20.x1, bf16[64,3712]{1,0:T(8,128)(2,1)S(1)} %collective-permute-done.21.x2, ...), custom_call_target="tpu_custom_call" | custom-call | flops 5637144576 | bytes 22020096 | tf_op jit(solution)/shard_map/expert_block/pallas_call | solution.py:235
  117.0 1.6 collective-permute-start.10
  119.8 1.6 collective-permute-start.24
  121.3 18.0 %collective-permute-done.10 = bf16[64,3584]{1,0:T(8,128)(2,1)S(1)} collective-permute-done((bf16[64,3584]{1,0:T(8,128)(2,1)S(1)}, bf16[64,3584]{1,0:T(8,128)(2,1)S(1)}, u32[]{:S(2)}, u32[]{:S(2)}) %collective-permute-start.10) | collective-permute-done | bytes 458784 | tf_op jit(solution)/shard_map/ppermute | solution.py:287
  139.5 9.6 %collective-permute-done.17 = bf16[64,3584]{1,0:T(8,128)(2,1)S(1)} collective-permute-done((bf16[64,3584]{1,0:T(8,128)(2,1)S(1)}, bf16[64,3584]{1,0:T(8,128)(2,1)S(1)}, u32[]{:S(2)}, u32[]{:S(2)}) %collective-permute-start.17) | collective-permute-done | bytes 458784 | tf_op jit(solution)/shard_map/ppermute | solution.py:287
  149.7 8.8 %collective-permute-done.24 = bf16[64,3584]{1,0:T(8,128)(2,1)S(1)} collective-permute-done((bf16[64,3584]{1,0:T(8,128)(2,1)S(1)}, bf16[64,3584]{1,0:T(8,128)(2,1)S(1)}, u32[]{:S(2)}, u32[]{:S(2)}) %collective-permute-start.24) | collective-permute-done | bytes 458784 | tf_op jit(solution)/shard_map/ppermute | solution.py:287
  158.6 1.6 collective-permute-start.25
  160.3 20.1 %collective-permute-done.18 = bf16[64,3584]{1,0:T(8,128)(2,1)S(1)} collective-permute-done((bf16[64,3584]{1,0:T(8,128)(2,1)S(1)}, bf16[64,3584]{1,0:T(8,128)(2,1)S(1)}, u32[]{:S(2)}, u32[]{:S(2)}) %collective-permute-start.18) | collective-permute-done | bytes 458784 | tf_op jit(solution)/shard_map/ppermute | solution.py:287
  180.4 9.9 %collective-permute-done.25 = bf16[64,3584]{1,0:T(8,128)(2,1)S(1)} collective-permute-done((bf16[64,3584]{1,0:T(8,128)(2,1)S(1)}, bf16[64,3584]{1,0:T(8,128)(2,1)S(1)}, u32[]{:S(2)}, u32[]{:S(2)}) %collective-permute-start.25) | collective-permute-done | bytes 458784 | tf_op jit(solution)/shard_map/ppermute | solution.py:287
  (81 shorter events, 14.8 us)
Async XLA Ops:
  5.4 19.4 %collective-permute-start.5 = (bf16[64,3712]{1,0:T(8,128)(2,1)}, bf16[64,3712]{1,0:T(8,128)(2,1)S(1)}, u32[]{:S(2)}, u32[]{:S(2)}) collective-permute-start(bf16[64,3712]{1,0:T(8,128)(2,1)} %get-tuple-element.17.x0), channel_id=1, source_target_pairs={{0,4},{1,5},{2,6},{3,7},{4,0},{5,1},{6,2},{7,3},{8,12},{9,13},{10,... | collective-permute-start | bytes 1425416 | tf_op jit(solution)/shard_map/ppermute | solution.py:287
  5.4 21.5 %collective-permute-start = (bf16[64,3712]{1,0:T(8,128)(2,1)}, bf16[64,3712]{1,0:T(8,128)(2,1)S(1)}, u32[]{:S(2)}, u32[]{:S(2)}) collective-permute-start(bf16[64,3712]{1,0:T(8,128)(2,1)} %get-tuple-element.17.x0), channel_id=1, source_target_pairs={{0,2},{1,3},{2,0},{3,1},{4,6},{5,7},{6,4},{7,5},{8,10},{9,11},{10,... | collective-permute-start | bytes 1425416 | tf_op jit(solution)/shard_map/ppermute | solution.py:287
  7.4 38.2 %collective-permute-start.12 = (bf16[64,3712]{1,0:T(8,128)(2,1)}, bf16[64,3712]{1,0:T(8,128)(2,1)S(1)}, u32[]{:S(2)}, u32[]{:S(2)}) collective-permute-start(bf16[64,3712]{1,0:T(8,128)(2,1)} %get-tuple-element.17.x0), channel_id=1, source_target_pairs={{0,8},{1,9},{2,10},{3,11},{4,12},{5,13},{6,14},{7,15},{8,0},{9,1},... | collective-permute-start | bytes 1425416 | tf_op jit(solution)/shard_map/ppermute | solution.py:287
  9.9 41.3 %collective-permute-start.19 = (bf16[64,3712]{1,0:T(8,128)(2,1)}, bf16[64,3712]{1,0:T(8,128)(2,1)S(1)}, u32[]{:S(2)}, u32[]{:S(2)}) collective-permute-start(bf16[64,3712]{1,0:T(8,128)(2,1)} %get-tuple-element.17.x0), channel_id=1, source_target_pairs={{0,12},{1,13},{2,14},{3,15},{4,8},{5,9},{6,10},{7,11},{8,4},{9,5},... | collective-permute-start | bytes 1425416 | tf_op jit(solution)/shard_map/ppermute | solution.py:287
  10.4 41.4 %collective-permute-start.1 = (bf16[64,3712]{1,0:T(8,128)(2,1)}, bf16[64,3712]{1,0:T(8,128)(2,1)S(1)}, u32[]{:S(2)}, u32[]{:S(2)}) collective-permute-start(bf16[64,3712]{1,0:T(8,128)(2,1)} %get-tuple-element.17.x0), channel_id=1, source_target_pairs={{0,1},{1,0},{2,3},{3,2},{4,5},{5,4},{6,7},{7,6},{8,9},{9,8},{10,11... | collective-permute-start | bytes 1425416 | tf_op jit(solution)/shard_map/ppermute | solution.py:287
  24.8 27.0 %collective-permute-start.6 = (bf16[64,3712]{1,0:T(8,128)(2,1)S(1)}, bf16[64,3712]{1,0:T(8,128)(2,1)S(1)}, u32[]{:S(2)}, u32[]{:S(2)}) collective-permute-start(bf16[64,3712]{1,0:T(8,128)(2,1)S(1)} %collective-permute-done.5.x0), channel_id=1, source_target_pairs={{0,2},{1,3},{2,0},{3,1},{4,6},{5,7},{6,4},{7,5},{8,10},{9,11},{10,... | collective-permute-start | bytes 1425416 | tf_op jit(solution)/shard_map/ppermute | solution.py:287
  26.9 26.4 %collective-permute-start.2 = (bf16[64,3712]{1,0:T(8,128)(2,1)S(1)}, bf16[64,3712]{1,0:T(8,128)(2,1)}, u32[]{:S(2)}, u32[]{:S(2)}) collective-permute-start(bf16[64,3712]{1,0:T(8,128)(2,1)S(1)} %collective-permute-done.x1), channel_id=1, source_target_pairs={{0,1},{1,0},{2,3},{3,2},{4,5},{5,4},{6,7},{7,6},{8,9},{9,8},{10,11... | collective-permute-start | bytes 1425416 | tf_op jit(solution)/shard_map/ppermute | solution.py:287
  45.5 25.6 %collective-permute-start.7 = (bf16[64,3712]{1,0:T(8,128)(2,1)S(1)}, bf16[64,3712]{1,0:T(8,128)(2,1)S(1)}, u32[]{:S(2)}, u32[]{:S(2)}) collective-permute-start(bf16[64,3712]{1,0:T(8,128)(2,1)S(1)} %collective-permute-done.5.x0), channel_id=1, source_target_pairs={{0,1},{1,0},{2,3},{3,2},{4,5},{5,4},{6,7},{7,6},{8,9},{9,8},{10,11... | collective-permute-start | bytes 1425416 | tf_op jit(solution)/shard_map/ppermute | solution.py:287
  51.2 20.3 %collective-permute-start.13 = (bf16[64,3712]{1,0:T(8,128)(2,1)S(1)}, bf16[64,3712]{1,0:T(8,128)(2,1)S(1)}, u32[]{:S(2)}, u32[]{:S(2)}) collective-permute-start(bf16[64,3712]{1,0:T(8,128)(2,1)S(1)} %collective-permute-done.12.x0), channel_id=1, source_target_pairs={{0,2},{1,3},{2,0},{3,1},{4,6},{5,7},{6,4},{7,5},{8,10},{9,11},{10,... | collective-permute-start | bytes 1425416 | tf_op jit(solution)/shard_map/ppermute | solution.py:287
  51.8 36.5 %collective-permute-start.14 = (bf16[64,3712]{1,0:T(8,128)(2,1)S(1)}, bf16[64,3712]{1,0:T(8,128)(2,1)S(1)}, u32[]{:S(2)}, u32[]{:S(2)}) collective-permute-start(bf16[64,3712]{1,0:T(8,128)(2,1)S(1)} %collective-permute-done.12.x0), channel_id=1, source_target_pairs={{0,1},{1,0},{2,3},{3,2},{4,5},{5,4},{6,7},{7,6},{8,9},{9,8},{10,11... | collective-permute-start | bytes 1425416 | tf_op jit(solution)/shard_map/ppermute | solution.py:287
  51.8 20.8 %collective-permute-start.20 = (bf16[64,3712]{1,0:T(8,128)(2,1)S(1)}, bf16[64,3712]{1,0:T(8,128)(2,1)S(1)}, u32[]{:S(2)}, u32[]{:S(2)}) collective-permute-start(bf16[64,3712]{1,0:T(8,128)(2,1)S(1)} %collective-permute-done.19.x0), channel_id=1, source_target_pairs={{0,2},{1,3},{2,0},{3,1},{4,6},{5,7},{6,4},{7,5},{8,10},{9,11},{10,... | collective-permute-start | bytes 1425416 | tf_op jit(solution)/shard_map/ppermute | solution.py:287
  53.3 19.3 %collective-permute-start.8 = (bf16[64,3712]{1,0:T(8,128)(2,1)S(1)}, bf16[64,3712]{1,0:T(8,128)(2,1)S(1)}, u32[]{:S(2)}, u32[]{:S(2)}) collective-permute-start(bf16[64,3712]{1,0:T(8,128)(2,1)S(1)} %collective-permute-done.6.x1), channel_id=1, source_target_pairs={{0,1},{1,0},{2,3},{3,2},{4,5},{5,4},{6,7},{7,6},{8,9},{9,8},{10,11... | collective-permute-start | bytes 1425416 | tf_op jit(solution)/shard_map/ppermute | solution.py:287
  71.2 31.2 %collective-permute-start.21 = (bf16[64,3712]{1,0:T(8,128)(2,1)S(1)}, bf16[64,3712]{1,0:T(8,128)(2,1)S(1)}, u32[]{:S(2)}, u32[]{:S(2)}) collective-permute-start(bf16[64,3712]{1,0:T(8,128)(2,1)S(1)} %collective-permute-done.19.x0), channel_id=1, source_target_pairs={{0,1},{1,0},{2,3},{3,2},{4,5},{5,4},{6,7},{7,6},{8,9},{9,8},{10,11... | collective-permute-start | bytes 1425416 | tf_op jit(solution)/shard_map/ppermute | solution.py:287
  71.5 44.3 %collective-permute-start.3 = (bf16[128,3584]{1,0:T(8,128)(2,1)}, bf16[128,3584]{1,0:T(8,128)(2,1)S(1)}, u32[]{:S(2)}, u32[]{:S(2)}) collective-permute-start(bf16[128,3584]{1,0:T(8,128)(2,1)} %get-tuple-element.22), channel_id=1, source_target_pairs={{0,1},{1,0},{2,3},{3,2},{4,5},{5,4},{6,7},{7,6},{8,9},{9,8},{10,11... | collective-permute-start | bytes 2752520 | tf_op jit(solution)/shard_map/ppermute | solution.py:287
  73.4 28.9 %collective-permute-start.22 = (bf16[64,3712]{1,0:T(8,128)(2,1)S(1)}, bf16[64,3712]{1,0:T(8,128)(2,1)S(1)}, u32[]{:S(2)}, u32[]{:S(2)}) collective-permute-start(bf16[64,3712]{1,0:T(8,128)(2,1)S(1)} %collective-permute-done.20.x1), channel_id=1, source_target_pairs={{0,1},{1,0},{2,3},{3,2},{4,5},{5,4},{6,7},{7,6},{8,9},{9,8},{10,11... | collective-permute-start | bytes 1425416 | tf_op jit(solution)/shard_map/ppermute | solution.py:287
  88.3 28.4 %collective-permute-start.9 = (bf16[128,3584]{1,0:T(8,128)(2,1)S(1)}, bf16[128,3584]{1,0:T(8,128)(2,1)S(1)}, u32[]{:S(2)}, u32[]{:S(2)}) collective-permute-start(bf16[128,3584]{1,0:T(8,128)(2,1)S(1)} %get-tuple-element.24), channel_id=1, source_target_pairs={{0,1},{1,0},{2,3},{3,2},{4,5},{5,4},{6,7},{7,6},{8,9},{9,8},{10,11... | collective-permute-start | bytes 2752520 | tf_op jit(solution)/shard_map/ppermute | solution.py:287
  101.8 16.8 %collective-permute-start.16 = (bf16[128,3584]{1,0:T(8,128)(2,1)S(1)}, bf16[128,3584]{1,0:T(8,128)(2,1)S(1)}, u32[]{:S(2)}, u32[]{:S(2)}) collective-permute-start(bf16[128,3584]{1,0:T(8,128)(2,1)S(1)} %get-tuple-element.26), channel_id=1, source_target_pairs={{0,1},{1,0},{2,3},{3,2},{4,5},{5,4},{6,7},{7,6},{8,9},{9,8},{10,11... | collective-permute-start | bytes 2752520 | tf_op jit(solution)/shard_map/ppermute | solution.py:287
  116.1 44.2 %collective-permute-start.4 = (bf16[64,3584]{1,0:T(8,128)(2,1)S(1)}, bf16[64,3584]{1,0:T(8,128)(2,1)S(1)}, u32[]{:S(2)}, u32[]{:S(2)}) collective-permute-start(bf16[64,3584]{1,0:T(8,128)(2,1)S(1)} %slice.69), channel_id=1, source_target_pairs={{0,2},{1,3},{2,0},{3,1},{4,6},{5,7},{6,4},{7,5},{8,10},{9,11},{10,... | collective-permute-start | bytes 1376264 | tf_op jit(solution)/shard_map/ppermute | solution.py:287
  117.0 22.3 %collective-permute-start.10 = (bf16[64,3584]{1,0:T(8,128)(2,1)S(1)}, bf16[64,3584]{1,0:T(8,128)(2,1)S(1)}, u32[]{:S(2)}, u32[]{:S(2)}) collective-permute-start(bf16[64,3584]{1,0:T(8,128)(2,1)S(1)} %slice.68), channel_id=1, source_target_pairs={{0,2},{1,3},{2,0},{3,1},{4,6},{5,7},{6,4},{7,5},{8,10},{9,11},{10,... | collective-permute-start | bytes 1376264 | tf_op jit(solution)/shard_map/ppermute | solution.py:287
  118.9 30.3 %collective-permute-start.17 = (bf16[64,3584]{1,0:T(8,128)(2,1)S(1)}, bf16[64,3584]{1,0:T(8,128)(2,1)S(1)}, u32[]{:S(2)}, u32[]{:S(2)}) collective-permute-start(bf16[64,3584]{1,0:T(8,128)(2,1)S(1)} %slice.67), channel_id=1, source_target_pairs={{0,2},{1,3},{2,0},{3,1},{4,6},{5,7},{6,4},{7,5},{8,10},{9,11},{10,... | collective-permute-start | bytes 1376264 | tf_op jit(solution)/shard_map/ppermute | solution.py:287
  119.8 38.8 %collective-permute-start.24 = (bf16[64,3584]{1,0:T(8,128)(2,1)S(1)}, bf16[64,3584]{1,0:T(8,128)(2,1)S(1)}, u32[]{:S(2)}, u32[]{:S(2)}) collective-permute-start(bf16[64,3584]{1,0:T(8,128)(2,1)S(1)} %slice.66), channel_id=1, source_target_pairs={{0,2},{1,3},{2,0},{3,1},{4,6},{5,7},{6,4},{7,5},{8,10},{9,11},{10,... | collective-permute-start | bytes 1376264 | tf_op jit(solution)/shard_map/ppermute | solution.py:287
  139.4 20.8 %collective-permute-start.11 = (bf16[64,3584]{1,0:T(8,128)(2,1)S(1)}, bf16[64,3584]{1,0:T(8,128)(2,1)S(1)}, u32[]{:S(2)}, u32[]{:S(2)}) collective-permute-start(bf16[64,3584]{1,0:T(8,128)(2,1)S(1)} %fusion.2), channel_id=1, source_target_pairs={{0,4},{1,5},{2,6},{3,7},{4,0},{5,1},{6,2},{7,3},{8,12},{9,13},{10,... | collective-permute-start | bytes 1376264 | tf_op jit(solution)/shard_map/ppermute | solution.py:287
  149.3 31.1 %collective-permute-start.18 = (bf16[64,3584]{1,0:T(8,128)(2,1)S(1)}, bf16[64,3584]{1,0:T(8,128)(2,1)S(1)}, u32[]{:S(2)}, u32[]{:S(2)}) collective-permute-start(bf16[64,3584]{1,0:T(8,128)(2,1)S(1)} %fusion.1), channel_id=1, source_target_pairs={{0,8},{1,9},{2,10},{3,11},{4,12},{5,13},{6,14},{7,15},{8,0},{9,1},... | collective-permute-start | bytes 1376264 | tf_op jit(solution)/shard_map/ppermute | solution.py:287
  158.6 31.7 %collective-permute-start.25 = (bf16[64,3584]{1,0:T(8,128)(2,1)S(1)}, bf16[64,3584]{1,0:T(8,128)(2,1)S(1)}, u32[]{:S(2)}, u32[]{:S(2)}) collective-permute-start(bf16[64,3584]{1,0:T(8,128)(2,1)S(1)} %fusion), channel_id=1, source_target_pairs={{0,12},{1,13},{2,14},{3,15},{4,8},{5,9},{6,10},{7,11},{8,4},{9,5},... | collective-permute-start | bytes 1376264 | tf_op jit(solution)/shard_map/ppermute | solution.py:287
  (18 other events, 118.8 us)

commit v2 on v1

--- a/solution.py
+++ b/solution.py
@@ -12,6 +12,7 @@
 WORD = 4
 CHUNK = GROUP * WORD
 EXTRA = 128
+QUARTERS = 4
 F32 = jnp.float32
 BF16 = jnp.bfloat16
 
@@ -117,6 +118,7 @@
             jax.ShapeDtypeStruct((n, width + EXTRA), BF16),
             jax.ShapeDtypeStruct((CHUNK, CHUNK), BF16),
         ),
+        compiler_params=pltpu.CompilerParams(vmem_limit_bytes=8 * 1024 * 1024),
         name="prepare",
     )(tokens, scores, ids)
 
@@ -131,13 +133,14 @@
             w = words[g * sub : (g + 1) * sub, cols].astype(jnp.int32)
             for j in range(WORD):
                 code = ((w >> (4 * j)) & 15).astype(F32)
-                out[t, j * GROUP + g * sub : j * GROUP + (g + 1) * sub, :] = (
+                out[t, pl.ds(pl.multiple_of(at * CHUNK + j * GROUP + g * sub, sub), sub), :] = (
                     (code - z) * s
                 ).astype(BF16)
 
 
 def unpack_kernel(pairs, tiles, tile, *refs):
-    ins, outs, scratch = refs[: 3 * pairs], refs[3 * pairs : 4 * pairs], refs[4 * pairs :]
+    ins, outs, scratch = refs[: 3 * pairs], refs[3 * pairs : 4 * pairs], refs[4 * pairs + 1 :]
+    refs[4 * pairs][...] = jnp.zeros(refs[4 * pairs].shape, F32)
     at = pl.program_id(0)
 
     @pl.when(at == 0)
@@ -170,13 +173,15 @@
         functools.partial(unpack_kernel, len(triples), tiles, tile),
         grid=(steps,),
         in_specs=in_specs,
-        out_specs=[pl.BlockSpec((tiles, CHUNK, tile), lambda i: (0, i, 0)) for _ in triples],
-        out_shape=[jax.ShapeDtypeStruct((tiles, n * WORD, tile), BF16) for _ in triples],
+        out_specs=[pl.BlockSpec(memory_space=pltpu.VMEM) for _ in triples]
+        + [pl.BlockSpec((8, 128), lambda i: (0, 0))],
+        out_shape=[pltpu.VMEM((tiles, n * WORD, tile), BF16) for _ in triples]
+        + [jax.ShapeDtypeStruct((8, 128), F32)],
         scratch_shapes=scratch,
-        compiler_params=pltpu.CompilerParams(vmem_limit_bytes=40 * 1024 * 1024),
+        compiler_params=pltpu.CompilerParams(vmem_limit_bytes=20 * 1024 * 1024),
         cost_estimate=pl.CostEstimate(
             flops=n * cols * 24 * len(triples),
-            bytes_accessed=n * cols * 12 * len(triples),
+            bytes_accessed=n * cols * 4 * len(triples),
             transcendentals=0,
         ),
         name="unpack",
@@ -184,25 +189,40 @@
 
 
 def expert_kernel(
-    experts, first, mine, x0, x1, x2, x3, perm, wg, wu, wd, keep, send, xs, hs, hp, col
+    experts, quarter, first, mine, near, cross, other, z, x, c, perm, wg, wu, wd,
+    keep_near, keep_far, send_near, send_far, done, xs, hs, hp, col,
 ):
     i = pl.program_id(0)
-    n, width = x0.shape[0], x0.shape[1] - EXTRA
-    half = first // 2
+    width = near.shape[1] - EXTRA
+    far = z.shape[0]
+    u = far // 3
 
     @pl.when(i == 0)
     def _():
-        for at, x in enumerate((x0, x1, x2, x3)):
-            xs[at * n : (at + 1) * n, :] = x[:, :width]
-            parts = x[:, width:].astype(F32)
+        done[...] = jnp.zeros(done.shape, F32)
+        mine_at = quarter * u
+        n = near.shape[0]
+        at = 0
+        for ref, begin, count in (
+            (near, mine_at, u),
+            (cross, mine_at, u),
+            (z, 0, far),
+            (x, 0, far),
+            (other, mine_at, u),
+            (other, n + mine_at, u),
+            (c, 0, 2 * far),
+        ):
+            xs[at : at + count, :] = ref[begin : begin + count, :width]
+            parts = ref[begin : begin + count, width:].astype(F32)
             lane = lax.broadcasted_iota(jnp.int32, parts.shape, 1)
             parts = jnp.where(lane % experts == mine[0], parts, 0.0)
-            col[at * n : (at + 1) * n, :] = jnp.sum(parts, axis=1, keepdims=True)
+            col[at : at + count, :] = jnp.sum(parts, axis=1, keepdims=True)
+            at += count
 
     @pl.when(i < first)
     def _():
-        gate = jnp.dot(xs[...], wg[0], preferred_element_type=F32)
-        up = jnp.dot(xs[...], wu[0], preferred_element_type=F32)
+        gate = jnp.dot(xs[...], wg[i], preferred_element_type=F32)
+        up = jnp.dot(xs[...], wu[i], preferred_element_type=F32)
         hs[i] = (gate / (1.0 + jnp.exp(-gate)) * up).astype(BF16)
 
     @pl.when(i == first)
@@ -220,48 +240,44 @@
 
     @pl.when(i >= first)
     def _():
-        answer = jnp.dot(hp[...], wd[0], preferred_element_type=F32) * col[...]
-        keep[...] = answer[: 2 * n].astype(BF16)
-        send[...] = answer[2 * n :].astype(BF16)
-
-
-def expert_block(mine, shards, perm, wg, wu, wd, experts):
-    n, wide = shards[0].shape
+        answer = (jnp.dot(hp[...], wd[i - first], preferred_element_type=F32) * col[...]).astype(BF16)
+        at = 0
+        for ref in (keep_near, keep_far, send_near, send_far):
+            ref[...] = answer[at : at + ref.shape[0]]
+            at += ref.shape[0]
+
+
+def expert_block(quarter, mine, near, cross, other, z, x, c, perm, wg, wu, wd, experts):
+    far, wide = z.shape
+    u = far // 3
     width = wide - EXTRA
     first, _, tile = wg.shape
     second, hidden, otile = wd.shape
-    whole = lambda a: pl.BlockSpec(a.shape, lambda i: (0,) * a.ndim)
-    flops = 2 * 4 * n * width * hidden * 3
+    rows = 16 * u
+    resident = pl.BlockSpec(memory_space=pltpu.VMEM)
+    out = lambda n: pl.BlockSpec((n, otile), lambda i: (0, jnp.maximum(i - first, 0)))
     return pl.pallas_call(
-        functools.partial(expert_kernel, experts, first),
+        functools.partial(expert_kernel, experts, quarter, first),
         grid=(first + second,),
-        in_specs=[pl.BlockSpec(memory_space=pltpu.SMEM)]
-        + [whole(s) for s in shards]
-        + [
-            whole(perm),
-            pl.BlockSpec((1, width, tile), lambda i: (jnp.minimum(i, first - 1), 0, 0)),
-            pl.BlockSpec((1, width, tile), lambda i: (jnp.minimum(i, first - 1), 0, 0)),
-            pl.BlockSpec((1, hidden, otile), lambda i: (jnp.maximum(i - first, 0), 0, 0)),
+        in_specs=[pl.BlockSpec(memory_space=pltpu.SMEM)] + [resident] * 10,
+        out_specs=[out(2 * u), out(6 * u), out(2 * u), out(6 * u)]
+        + [pl.BlockSpec((8, 128), lambda i: (0, 0))],
+        out_shape=[jax.ShapeDtypeStruct((n * u, width), BF16) for n in (2, 6, 2, 6)]
+        + [jax.ShapeDtypeStruct((8, 128), F32)],
+        scratch_shapes=[
+            pltpu.VMEM((rows, width), BF16),
+            pltpu.VMEM((first, rows, tile), BF16),
+            pltpu.VMEM((rows, hidden), BF16),
+            pltpu.VMEM((rows, 1), F32),
         ],
-        out_specs=[
-            pl.BlockSpec((2 * n, otile), lambda i: (0, jnp.maximum(i - first, 0))),
-            pl.BlockSpec((2 * n, otile), lambda i: (0, jnp.maximum(i - first, 0))),
-        ],
-        out_shape=[jax.ShapeDtypeStruct((2 * n, width), BF16)] * 2,
-        scratch_shapes=[
-            pltpu.VMEM((4 * n, width), BF16),
-            pltpu.VMEM((first, 4 * n, tile), BF16),
-            pltpu.VMEM((4 * n, hidden), BF16),
-            pltpu.VMEM((4 * n, 1), F32),
-        ],
-        compiler_params=pltpu.CompilerParams(vmem_limit_bytes=40 * 1024 * 1024),
+        compiler_params=pltpu.CompilerParams(vmem_limit_bytes=16 * 1024 * 1024),
         cost_estimate=pl.CostEstimate(
-            flops=flops,
-            bytes_accessed=3 * width * hidden * 2,
-            transcendentals=4 * n * hidden,
+            flops=2 * rows * width * hidden * 3,
+            bytes_accessed=rows * width * 4,
+            transcendentals=rows * hidden,
         ),
         name="expert_block",
-    )(mine, *shards, perm, wg, wu, wd)
+    )(mine, near, cross, other, z, x, c, perm, wg, wu, wd)
 
 
 def dense(
@@ -279,29 +295,85 @@
     down_zero,
 ):
     experts = lax.axis_size("ep")
-    planes = experts // 4
     n = tokens.shape[0]
+    u = n // QUARTERS
     mine = lax.axis_index("ep").astype(jnp.int32).reshape(1)
 
     def swap(value, bits):
         return lax.ppermute(value, "ep", [(i, i ^ bits) for i in range(experts)])
 
+    def after(values, *others):
+        return lax.optimization_barrier((values, others))[0]
+
+    quarters = range(QUARTERS)
     rows, perm = prepare(tokens, gate_scores, route_ids, experts)
-    w_gate, w_up = unpack(
+    w_gate, w_up, done_in = unpack(
         [(gate_codes[0], gate_scale[0], gate_zero[0]), (up_codes[0], up_scale[0], up_zero[0])], 256
     )
-    (w_down,) = unpack([(down_codes[0], down_scale[0], down_zero[0])], 512)
-
-    total = None
-    for k in range(planes):
-        here = rows if k == 0 else swap(rows, 4 * k)
-        across = swap(here, 2)
-        shards = [here, across, swap(here, 1), swap(across, 1)]
-        keep, send = expert_block(mine, shards, perm, w_gate, w_up, w_down, experts)
-        pair = keep.astype(F32) + swap(send, 1).astype(F32)
-        plane = pair[:n] + swap(pair[n:].astype(BF16), 2).astype(F32)
-        back = plane if k == 0 else swap(plane.astype(BF16), 4 * k).astype(F32)
-        total = back if total is None else total + back
+    w_down, done_out = unpack([(down_codes[0], down_scale[0], down_zero[0])], 512)
+
+    mids = [rows[q * u : (q + 1) * u] for q in quarters]
+    twos = [swap(mids[q], 8) for q in quarters]
+    cross = swap(rows, 2)
+    twos, cross = after((twos, cross), done_in, done_out)
+    ones = [swap(jnp.concatenate([mids[q], twos[q]]), 4) for q in quarters]
+    other = swap(jnp.concatenate([rows, cross]), 1)
+    z = [jnp.concatenate([ones[q], twos[q]]) for q in quarters]
+    x = [swap(z[q], 2) for q in quarters]
+
+    near, pairs, crossed, planes, back_one = [], [], [], [], []
+    sums = [None] * QUARTERS
+
+    def after_core(q):
+        keep, send = sent[q]
+        pair = keep.astype(F32) + send.astype(F32)
+        crossing = pair[3 * u :].astype(BF16)
+        pairs.append(pair[: 3 * u])
+        crossed.append(swap(crossing, 2))
+        return crossing
+
+    def after_x(q):
+        plane = pairs[q] + crossed[q].astype(F32)
+        leaving = plane[: 2 * u].astype(BF16)
+        planes.append(plane[2 * u :])
+        back_one.append(swap(leaving, 4))
+        return leaving
+
+    def after_one(q):
+        got = back_one[q].astype(F32)
+        leaving = (planes[q] + got[u:]).astype(BF16)
+        sums[q] = got[:u] + swap(leaving, 8).astype(F32)
+        return leaving
+
+    sent, done = [], None
+    for q in quarters:
+        zq, xq = (z[q], x[q]) if done is None else after((z[q], x[q]), done)
+        c = swap(jnp.concatenate([zq, xq]), 1)
+        due = [x[q + 1]] if q + 1 < QUARTERS else []
+        if q == 0:
+            due += [z[i] for i in quarters]
+        if q >= 2:
+            due.append(after_core(q - 2))
+        if q >= 3:
+            due.append(after_x(q - 3))
+        if due:
+            c = after(c, *due)
+        keep_near, keep_far, send_near, send_far, done = expert_block(
+            q, mine, rows, cross, other, zq, xq, c, perm, w_gate, w_up, w_down, experts
+        )
+        near.append((keep_near, send_near))
+        sent.append((keep_far, swap(send_far, 1)))
+    for q in range(max(QUARTERS - 2, 0), QUARTERS):
+        after_core(q)
+    for q in range(max(QUARTERS - 3, 0), QUARTERS):
+        after_x(q)
+    for q in quarters:
+        after_one(q)
+    sends = [s for _, s in near]
+    got = swap(jnp.concatenate([s[:u] for s in sends] + [s[u:] for s in sends]), 1)
+    kept = [k for k, _ in near]
+    pair = jnp.concatenate([k[:u] for k in kept] + [k[u:] for k in kept]).astype(F32) + got.astype(F32)
+    total = pair[:n] + swap(pair[n:].astype(BF16), 2).astype(F32) + jnp.concatenate(sums)
     return total.astype(BF16)
 
 
@@ -322,9 +394,9 @@
     )
     out_specs = P(("grp", "ep"), "tp")
     experts = mesh.shape["ep"]
-    few = mesh.shape["tp"] == 1 and experts % 4 == 0 and 3 * experts <= EXTRA
+    few = mesh.shape["tp"] == 1 and experts == 16
     return jax.shard_map(
-        dense if few and experts & (experts - 1) == 0 else routed,
+        dense if few else routed,
         mesh=mesh,
         in_specs=in_specs,
         out_specs=out_specs,

time: 192 us -> 160 us (0.83)
  the two profiles are of different devices: /device:TPU:8 before, /device:TPU:0 now
where the time goes in v2:
time: 160 us
  waiting for transfers between devices  71.5 us (45%)
  Pallas kernels  48.1 us (30%)
  starting transfers between devices  29.7 us (19%)
  local copies, waits for them, and re-layouts  7.29 us (5%)
  other arithmetic  2.8 us (2%)
    ppermute x36, waiting for transfers between devices, swap(): return lax.ppermute(value, 'ep', [(i, i ^ bits) for i in range(experts)])  71.5 us
    pallas_call x4, Pallas kernels, expert_block(): pl.pallas_call(functools.partial(expert_kernel, experts, quarter, first),...  37.7 us
    ppermute x36, starting transfers between devices, swap(): return lax.ppermute(value, 'ep', [(i, i ^ bits) for i in range(experts)])  29.7 us
    pallas_call x2, Pallas kernels, unpack(): pl.pallas_call(functools.partial(unpack_kernel, len(triples), tiles, tile...  9.61 us
    unnamed x39, local copies, waits for them, and re-layouts  6.87 us
  transfers between devices with their start and end apart: 36, of which 17 were waited for; matrix products, arithmetic and copies ran while one was open for 2% of the time, Pallas kernels for 30%

profile of v2, /device:TPU:0, one launch (start us, length us, event | category | flops | bytes accessed | tf_op | source)
XLA Modules:
  0.0 159.9 jit_solution(16468608359596803244)
XLA Ops:
  3.4 3.0 %collective-permute-start.4 = (bf16[64,3712]{1,0:T(8,128)(2,1)S(1)}, bf16[64,3712]{1,0:T(8,128)(2,1)S(1)}, u32[]{:S(2)}, u32[]{:S(2)}) collective-permute-start(bf16[64,3712]{1,0:T(8,128)(2,1)S(1)} %get-tuple-element.41.near), channel_id=1, source_target_pairs={{0,2},{1,3},{2,0},{3,1},{4,6},{5,7},{6,4},{7,5},{8,10},{9,11},{10,... | collective-permute-start | bytes 1425416 | tf_op jit(solution)/shard_map/ppermute | solution.py:303
  6.4 2.7 %collective-permute-start = (bf16[16,3712]{1,0:T(8,128)(2,1)S(1)}, bf16[16,3712]{1,0:T(8,128)(2,1)S(1)}, u32[]{:S(2)}, u32[]{:S(2)}) collective-permute-start(bf16[16,3712]{1,0:T(8,128)(2,1)S(1)} %get-tuple-element.80), channel_id=1, source_target_pairs={{0,8},{1,9},{2,10},{3,11},{4,12},{5,13},{6,14},{7,15},{8,0},{9,1},... | collective-permute-start | bytes 356360 | tf_op jit(solution)/shard_map/ppermute | solution.py:303
  9.4 2.6 %collective-permute-start.2 = (bf16[16,3712]{1,0:T(8,128)(2,1)S(1)}, bf16[16,3712]{1,0:T(8,128)(2,1)S(1)}, u32[]{:S(2)}, u32[]{:S(2)}) collective-permute-start(bf16[16,3712]{1,0:T(8,128)(2,1)S(1)} %get-tuple-element.78), channel_id=1, source_target_pairs={{0,8},{1,9},{2,10},{3,11},{4,12},{5,13},{6,14},{7,15},{8,0},{9,1},... | collective-permute-start | bytes 356360 | tf_op jit(solution)/shard_map/ppermute | solution.py:303
  14.4 3.2 %unpack.3 = (bf16[7,1024,512]{2,1,0:T(8,128)(2,1)S(1)}, f32[8,128]{1,0:T(8,128)}) custom-call(f32[256,3584]{1,0:T(8,128)S(1)} %bitcast.10, bf16[8,3584]{1,0:T(8,128)(2,1)S(1)} %bitcast.17, bf16[8,3584]{1,0:T(8,128)(2,1)S(1)} %bitcast.18), custom_call_target="tpu_custom_call" | custom-call | flops 22020096 | bytes 3670016 | tf_op jit(solution)/shard_map/unpack/pallas_call | solution.py:172
  19.7 6.5 %unpack.2 = (bf16[4,3584,256]{2,1,0:T(8,128)(2,1)S(1)}, bf16[4,3584,256]{2,1,0:T(8,128)(2,1)S(1)}, f32[8,128]{1,0:T(8,128)}) custom-call(f32[896,1024]{1,0:T(8,128)S(1)} %bitcast.11, bf16[28,1024]{1,0:T(8,128)(2,1)S(1)} %bitcast.13, bf16[28,1024]{1,0:T(8,128)(2,1)S(1)} %bitcast.14, f32[896,1024]{1,0:T(8,128)S(1)} %bitcast.12, bf16[28,1024]{1,0:T(8,128)(2,1)S(1)} %bitcast.15, ...), custom_call_target="tpu_custom_call" | custom-call | flops 44040192 | bytes 7340032 | tf_op jit(solution)/shard_map/unpack/pallas_call | solution.py:172
  26.1 2.4 %collective-permute-done.2 = bf16[16,3712]{1,0:T(8,128)(2,1)S(1)} collective-permute-done((bf16[16,3712]{1,0:T(8,128)(2,1)S(1)}, bf16[16,3712]{1,0:T(8,128)(2,1)S(1)}, u32[]{:S(2)}, u32[]{:S(2)}) %collective-permute-start.2) | collective-permute-done | bytes 118816 | tf_op jit(solution)/shard_map/ppermute | solution.py:303
  34.5 4.3 %collective-permute-done.6 = bf16[32,3712]{1,0:T(8,128)(2,1)S(1)} collective-permute-done((bf16[32,3712]{1,0:T(8,128)(2,1)S(1)}, bf16[32,3712]{1,0:T(8,128)(2,1)S(1)}, u32[]{:S(2)}, u32[]{:S(2)}) %collective-permute-start.6) | collective-permute-done | bytes 237600 | tf_op jit(solution)/shard_map/ppermute | solution.py:303
  39.3 4.5 %collective-permute-done.9 = bf16[32,3712]{1,0:T(8,128)(2,1)S(1)} collective-permute-done((bf16[32,3712]{1,0:T(8,128)(2,1)S(1)}, bf16[32,3712]{1,0:T(8,128)(2,1)S(1)}, u32[]{:S(2)}, u32[]{:S(2)}) %collective-permute-start.9) | collective-permute-done | bytes 237600 | tf_op jit(solution)/shard_map/ppermute | solution.py:303
  44.4 4.5 %collective-permute-done.11 = bf16[32,3712]{1,0:T(8,128)(2,1)S(1)} collective-permute-done((bf16[32,3712]{1,0:T(8,128)(2,1)S(1)}, bf16[32,3712]{1,0:T(8,128)(2,1)S(1)}, u32[]{:S(2)}, u32[]{:S(2)}) %collective-permute-start.11) | collective-permute-done | bytes 237600 | tf_op jit(solution)/shard_map/ppermute | solution.py:303
  49.5 2.4 %collective-permute-done.12 = bf16[32,3712]{1,0:T(8,128)(2,1)S(1)} collective-permute-done((bf16[32,3712]{1,0:T(8,128)(2,1)S(1)}, bf16[32,3712]{1,0:T(8,128)(2,1)S(1)}, u32[]{:S(2)}, u32[]{:S(2)}) %collective-permute-start.12) | collective-permute-done | bytes 237600 | tf_op jit(solution)/shard_map/ppermute | solution.py:303
  52.7 4.6 %collective-permute-done.10.x = bf16[48,3712]{1,0:T(8,128)(2,1)S(1)} collective-permute-done((bf16[48,3712]{1,0:T(8,128)(2,1)S(1)}, bf16[48,3712]{1,0:T(8,128)(2,1)S(1)}, u32[]{:S(2)}, u32[]{:S(2)}) %collective-permute-start.10) | collective-permute-done | bytes 356384 | tf_op jit(solution)/shard_map/ppermute | solution.py:303
  57.4 7.5 %collective-permute-done.14.x = bf16[48,3712]{1,0:T(8,128)(2,1)S(1)} collective-permute-done((bf16[48,3712]{1,0:T(8,128)(2,1)S(1)}, bf16[48,3712]{1,0:T(8,128)(2,1)S(1)}, u32[]{:S(2)}, u32[]{:S(2)}) %collective-permute-start.14) | collective-permute-done | bytes 356384 | tf_op jit(solution)/shard_map/ppermute | solution.py:303
  65.0 4.1 %collective-permute-done.16.x = bf16[48,3712]{1,0:T(8,128)(2,1)S(1)} collective-permute-done((bf16[48,3712]{1,0:T(8,128)(2,1)S(1)}, bf16[48,3712]{1,0:T(8,128)(2,1)S(1)}, u32[]{:S(2)}, u32[]{:S(2)}) %collective-permute-start.16) | collective-permute-done | bytes 356384 | tf_op jit(solution)/shard_map/ppermute | solution.py:303
  69.3 9.4 %expert_block.4 = (bf16[32,3584]{1,0:T(8,128)(2,1)S(1)}, bf16[96,3584]{1,0:T(8,128)(2,1)S(1)}, bf16[32,3584]{1,0:T(8,128)(2,1)S(1)}, bf16[96,3584]{1,0:T(8,128)(2,1)S(1)}, f32[8,128]{1,0:T(8,128)}) custom-call(s32[1]{0:T(128)} %bitcast.mine, bf16[64,3712]{1,0:T(8,128)(2,1)S(1)} %get-tuple-element.41.near, bf16[64,3712]{1,0:T(8,128)(2,1)S(1)} %collective-permute-done.4.cross, ...), custom_call_target="tpu_custom_call" | custom-call | flops 5637144576 | bytes 3670016 | tf_op jit(solution)/shard_map/expert_block/pallas_call | solution.py:259
  79.2 9.4 %expert_block.5 = (bf16[32,3584]{1,0:T(8,128)(2,1)S(1)}, bf16[96,3584]{1,0:T(8,128)(2,1)S(1)}, bf16[32,3584]{1,0:T(8,128)(2,1)S(1)}, bf16[96,3584]{1,0:T(8,128)(2,1)S(1)}, f32[8,128]{1,0:T(8,128)}) custom-call(s32[1]{0:T(128)} %bitcast.mine, bf16[64,3712]{1,0:T(8,128)(2,1)S(1)} %get-tuple-element.41.near, bf16[64,3712]{1,0:T(8,128)(2,1)S(1)} %collective-permute-done.4.cross, ...), custom_call_target="tpu_custom_call" | custom-call | flops 5637144576 | bytes 3670016 | tf_op jit(solution)/shard_map/expert_block/pallas_call | solution.py:259
  91.5 9.4 %expert_block.6 = (bf16[32,3584]{1,0:T(8,128)(2,1)S(1)}, bf16[96,3584]{1,0:T(8,128)(2,1)S(1)}, bf16[32,3584]{1,0:T(8,128)(2,1)S(1)}, bf16[96,3584]{1,0:T(8,128)(2,1)S(1)}, f32[8,128]{1,0:T(8,128)}) custom-call(s32[1]{0:T(128)} %bitcast.mine, bf16[64,3712]{1,0:T(8,128)(2,1)S(1)} %get-tuple-element.41.near, bf16[64,3712]{1,0:T(8,128)(2,1)S(1)} %collective-permute-done.4.cross, ...), custom_call_target="tpu_custom_call" | custom-call | flops 5637144576 | bytes 3670016 | tf_op jit(solution)/shard_map/expert_block/pallas_call | solution.py:259
  102.8 4.0 %collective-permute-done.25 = bf16[48,3584]{1,0:T(8,128)(2,1)S(1)} collective-permute-done((bf16[48,3584]{1,0:T(8,128)(2,1)S(1)}, bf16[48,3584]{1,0:T(8,128)(2,1)S(1)}, u32[]{:S(2)}, u32[]{:S(2)}) %collective-permute-start.25) | collective-permute-done | bytes 344096 | tf_op jit(solution)/shard_map/ppermute | solution.py:303
  108.6 9.4 %expert_block.7 = (bf16[32,3584]{1,0:T(8,128)(2,1)S(1)}, bf16[96,3584]{1,0:T(8,128)(2,1)S(1)}, bf16[32,3584]{1,0:T(8,128)(2,1)S(1)}, bf16[96,3584]{1,0:T(8,128)(2,1)S(1)}, f32[8,128]{1,0:T(8,128)}) custom-call(s32[1]{0:T(128)} %bitcast.mine, bf16[64,3712]{1,0:T(8,128)(2,1)S(1)} %get-tuple-element.41.near, bf16[64,3712]{1,0:T(8,128)(2,1)S(1)} %collective-permute-done.4.cross, ...), custom_call_target="tpu_custom_call" | custom-call | flops 5637144576 | bytes 3670016 | tf_op jit(solution)/shard_map/expert_block/pallas_call | solution.py:259
  118.9 3.4 %collective-permute-start.24 = (bf16[16,3584]{1,0:T(8,128)(2,1)S(1)}, bf16[16,3584]{1,0:T(8,128)(2,1)S(1)}, u32[]{:S(2)}, u32[]{:S(2)}) collective-permute-start(bf16[16,3584]{1,0:T(8,128)(2,1)S(1)} %fusion.5), channel_id=1, source_target_pairs={{0,8},{1,9},{2,10},{3,11},{4,12},{5,13},{6,14},{7,15},{8,0},{9,1},... | collective-permute-start | bytes 344072 | tf_op jit(solution)/shard_map/ppermute | solution.py:303
  123.3 7.4 %collective-permute-done.24 = bf16[16,3584]{1,0:T(8,128)(2,1)S(1)} collective-permute-done((bf16[16,3584]{1,0:T(8,128)(2,1)S(1)}, bf16[16,3584]{1,0:T(8,128)(2,1)S(1)}, u32[]{:S(2)}, u32[]{:S(2)}) %collective-permute-start.24) | collective-permute-done | bytes 114720 | tf_op jit(solution)/shard_map/ppermute | solution.py:303
  130.7 2.3 %collective-permute-done.27 = bf16[16,3584]{1,0:T(8,128)(2,1)S(1)} collective-permute-done((bf16[16,3584]{1,0:T(8,128)(2,1)S(1)}, bf16[16,3584]{1,0:T(8,128)(2,1)S(1)}, u32[]{:S(2)}, u32[]{:S(2)}) %collective-permute-start.27) | collective-permute-done | bytes 114720 | tf_op jit(solution)/shard_map/ppermute | solution.py:303
  134.1 6.6 %collective-permute-done.30 = bf16[32,3584]{1,0:T(8,128)(2,1)S(1)} collective-permute-done((bf16[32,3584]{1,0:T(8,128)(2,1)S(1)}, bf16[32,3584]{1,0:T(8,128)(2,1)S(1)}, u32[]{:S(2)}, u32[]{:S(2)}) %collective-permute-start.30) | collective-permute-done | bytes 229408 | tf_op jit(solution)/shard_map/ppermute | solution.py:303
  146.3 6.0 %collective-permute-done.34 = bf16[32,3584]{1,0:T(8,128)(2,1)S(1)} collective-permute-done((bf16[32,3584]{1,0:T(8,128)(2,1)S(1)}, bf16[32,3584]{1,0:T(8,128)(2,1)S(1)}, u32[]{:S(2)}, u32[]{:S(2)}) %collective-permute-start.34) | collective-permute-done | bytes 229408 | tf_op jit(solution)/shard_map/ppermute | solution.py:303
  152.5 6.4 %collective-permute-done.35 = bf16[16,3584]{1,0:T(8,128)(2,1)S(1)} collective-permute-done((bf16[16,3584]{1,0:T(8,128)(2,1)S(1)}, bf16[16,3584]{1,0:T(8,128)(2,1)S(1)}, u32[]{:S(2)}, u32[]{:S(2)}) %collective-permute-start.35) | collective-permute-done | bytes 114720 | tf_op jit(solution)/shard_map/ppermute | solution.py:303
  (141 shorter events, 33.4 us)
Async XLA Ops:
  3.4 26.5 %collective-permute-start.4 = (bf16[64,3712]{1,0:T(8,128)(2,1)S(1)}, bf16[64,3712]{1,0:T(8,128)(2,1)S(1)}, u32[]{:S(2)}, u32[]{:S(2)}) collective-permute-start(bf16[64,3712]{1,0:T(8,128)(2,1)S(1)} %get-tuple-element.41.near), channel_id=1, source_target_pairs={{0,2},{1,3},{2,0},{3,1},{4,6},{5,7},{6,4},{7,5},{8,10},{9,11},{10,... | collective-permute-start | bytes 1425416 | tf_op jit(solution)/shard_map/ppermute | solution.py:303
  6.4 19.7 %collective-permute-start = (bf16[16,3712]{1,0:T(8,128)(2,1)S(1)}, bf16[16,3712]{1,0:T(8,128)(2,1)S(1)}, u32[]{:S(2)}, u32[]{:S(2)}) collective-permute-start(bf16[16,3712]{1,0:T(8,128)(2,1)S(1)} %get-tuple-element.80), channel_id=1, source_target_pairs={{0,8},{1,9},{2,10},{3,11},{4,12},{5,13},{6,14},{7,15},{8,0},{9,1},... | collective-permute-start | bytes 356360 | tf_op jit(solution)/shard_map/ppermute | solution.py:303
  9.1 17.0 %collective-permute-start.1 = (bf16[16,3712]{1,0:T(8,128)(2,1)S(1)}, bf16[16,3712]{1,0:T(8,128)(2,1)S(1)}, u32[]{:S(2)}, u32[]{:S(2)}) collective-permute-start(bf16[16,3712]{1,0:T(8,128)(2,1)S(1)} %get-tuple-element.79), channel_id=1, source_target_pairs={{0,8},{1,9},{2,10},{3,11},{4,12},{5,13},{6,14},{7,15},{8,0},{9,1},... | collective-permute-start | bytes 356360 | tf_op jit(solution)/shard_map/ppermute | solution.py:303
  9.4 19.1 %collective-permute-start.2 = (bf16[16,3712]{1,0:T(8,128)(2,1)S(1)}, bf16[16,3712]{1,0:T(8,128)(2,1)S(1)}, u32[]{:S(2)}, u32[]{:S(2)}) collective-permute-start(bf16[16,3712]{1,0:T(8,128)(2,1)S(1)} %get-tuple-element.78), channel_id=1, source_target_pairs={{0,8},{1,9},{2,10},{3,11},{4,12},{5,13},{6,14},{7,15},{8,0},{9,1},... | collective-permute-start | bytes 356360 | tf_op jit(solution)/shard_map/ppermute | solution.py:303
  12.0 17.9 %collective-permute-start.3 = (bf16[16,3712]{1,0:T(8,128)(2,1)S(1)}, bf16[16,3712]{1,0:T(8,128)(2,1)S(1)}, u32[]{:S(2)}, u32[]{:S(2)}) collective-permute-start(bf16[16,3712]{1,0:T(8,128)(2,1)S(1)} %get-tuple-element.77), channel_id=1, source_target_pairs={{0,8},{1,9},{2,10},{3,11},{4,12},{5,13},{6,14},{7,15},{8,0},{9,1},... | collective-permute-start | bytes 356360 | tf_op jit(solution)/shard_map/ppermute | solution.py:303
  30.7 13.1 %collective-permute-start.9 = (bf16[32,3712]{1,0:T(8,128)(2,1)S(1)}, bf16[32,3712]{1,0:T(8,128)(2,1)S(1)}, u32[]{:S(2)}, u32[]{:S(2)}) collective-permute-start(bf16[32,3712]{1,0:T(8,128)(2,1)S(1)} %pad_maximum_fusion.6), channel_id=1, source_target_pairs={{0,4},{1,5},{2,6},{3,7},{4,0},{5,1},{6,2},{7,3},{8,12},{9,13},{10,... | collective-permute-start | bytes 712712 | tf_op jit(solution)/shard_map/ppermute | solution.py:303
  32.1 16.8 %collective-permute-start.11 = (bf16[32,3712]{1,0:T(8,128)(2,1)S(1)}, bf16[32,3712]{1,0:T(8,128)(2,1)S(1)}, u32[]{:S(2)}, u32[]{:S(2)}) collective-permute-start(bf16[32,3712]{1,0:T(8,128)(2,1)S(1)} %pad_maximum_fusion.7), channel_id=1, source_target_pairs={{0,4},{1,5},{2,6},{3,7},{4,0},{5,1},{6,2},{7,3},{8,12},{9,13},{10,... | collective-permute-start | bytes 712712 | tf_op jit(solution)/shard_map/ppermute | solution.py:303
  32.9 19.0 %collective-permute-start.12 = (bf16[32,3712]{1,0:T(8,128)(2,1)S(1)}, bf16[32,3712]{1,0:T(8,128)(2,1)S(1)}, u32[]{:S(2)}, u32[]{:S(2)}) collective-permute-start(bf16[32,3712]{1,0:T(8,128)(2,1)S(1)} %pad_maximum_fusion.8), channel_id=1, source_target_pairs={{0,4},{1,5},{2,6},{3,7},{4,0},{5,1},{6,2},{7,3},{8,12},{9,13},{10,... | collective-permute-start | bytes 712712 | tf_op jit(solution)/shard_map/ppermute | solution.py:303
  34.4 34.9 %collective-permute-start.5 = (bf16[128,3712]{1,0:T(8,128)(2,1)S(1)}, bf16[128,3712]{1,0:T(8,128)(2,1)S(1)}, u32[]{:S(2)}, u32[]{:S(2)}) collective-permute-start(bf16[128,3712]{1,0:T(8,128)(2,1)S(1)} %pad_maximum_fusion), channel_id=1, source_target_pairs={{0,1},{1,0},{2,3},{3,2},{4,5},{5,4},{6,7},{7,6},{8,9},{9,8},{10,11... | collective-permute-start | bytes 2850824 | tf_op jit(solution)/shard_map/ppermute | solution.py:303
  38.8 13.8 %collective-permute-start.7 = (bf16[48,3712]{1,0:T(8,128)(2,1)S(1)}, bf16[48,3712]{1,0:T(8,128)(2,1)S(1)}, u32[]{:S(2)}, u32[]{:S(2)}) collective-permute-start(bf16[48,3712]{1,0:T(8,128)(2,1)S(1)} %constant_dynamic-update-slice_fusion.z), channel_id=1, source_target_pairs={{0,2},{1,3},{2,0},{3,1},{4,6},{5,7},{6,4},{7,5},{8,10},{9,11},{10,... | collective-permute-start | bytes 1069064 | tf_op jit(solution)/shard_map/ppermute | solution.py:303
  43.9 13.4 %collective-permute-start.10 = (bf16[48,3712]{1,0:T(8,128)(2,1)S(1)}, bf16[48,3712]{1,0:T(8,128)(2,1)S(1)}, u32[]{:S(2)}, u32[]{:S(2)}) collective-permute-start(bf16[48,3712]{1,0:T(8,128)(2,1)S(1)} %constant_dynamic-update-slice_fusion.2.z), channel_id=1, source_target_pairs={{0,2},{1,3},{2,0},{3,1},{4,6},{5,7},{6,4},{7,5},{8,10},{9,11},{10,... | collective-permute-start | bytes 1069064 | tf_op jit(solution)/shard_map/ppermute | solution.py:303
  48.9 16.0 %collective-permute-start.14 = (bf16[48,3712]{1,0:T(8,128)(2,1)S(1)}, bf16[48,3712]{1,0:T(8,128)(2,1)S(1)}, u32[]{:S(2)}, u32[]{:S(2)}) collective-permute-start(bf16[48,3712]{1,0:T(8,128)(2,1)S(1)} %constant_dynamic-update-slice_fusion.4.z), channel_id=1, source_target_pairs={{0,2},{1,3},{2,0},{3,1},{4,6},{5,7},{6,4},{7,5},{8,10},{9,11},{10,... | collective-permute-start | bytes 1069064 | tf_op jit(solution)/shard_map/ppermute | solution.py:303
  52.0 17.2 %collective-permute-start.16 = (bf16[48,3712]{1,0:T(8,128)(2,1)S(1)}, bf16[48,3712]{1,0:T(8,128)(2,1)S(1)}, u32[]{:S(2)}, u32[]{:S(2)}) collective-permute-start(bf16[48,3712]{1,0:T(8,128)(2,1)S(1)} %constant_dynamic-update-slice_fusion.6.z), channel_id=1, source_target_pairs={{0,2},{1,3},{2,0},{3,1},{4,6},{5,7},{6,4},{7,5},{8,10},{9,11},{10,... | collective-permute-start | bytes 1069064 | tf_op jit(solution)/shard_map/ppermute | solution.py:303
  52.6 16.7 %collective-permute-start.8 = (bf16[96,3712]{1,0:T(8,128)(2,1)S(1)}, bf16[96,3712]{1,0:T(8,128)(2,1)S(1)}, u32[]{:S(2)}, u32[]{:S(2)}) collective-permute-start(bf16[96,3712]{1,0:T(8,128)(2,1)S(1)} %pad_maximum_fusion.1), channel_id=1, source_target_pairs={{0,1},{1,0},{2,3},{3,2},{4,5},{5,4},{6,7},{7,6},{8,9},{9,8},{10,11... | collective-permute-start | bytes 2138120 | tf_op jit(solution)/shard_map/ppermute | solution.py:303
  57.3 21.8 %collective-permute-start.13 = (bf16[96,3712]{1,0:T(8,128)(2,1)S(1)}, bf16[96,3712]{1,0:T(8,128)(2,1)S(1)}, u32[]{:S(2)}, u32[]{:S(2)}) collective-permute-start(bf16[96,3712]{1,0:T(8,128)(2,1)S(1)} %pad_maximum_fusion.2), channel_id=1, source_target_pairs={{0,1},{1,0},{2,3},{3,2},{4,5},{5,4},{6,7},{7,6},{8,9},{9,8},{10,11... | collective-permute-start | bytes 2138120 | tf_op jit(solution)/shard_map/ppermute | solution.py:303
  65.0 26.5 %collective-permute-start.15 = (bf16[96,3712]{1,0:T(8,128)(2,1)S(1)}, bf16[96,3712]{1,0:T(8,128)(2,1)S(1)}, u32[]{:S(2)}, u32[]{:S(2)}) collective-permute-start(bf16[96,3712]{1,0:T(8,128)(2,1)S(1)} %pad_maximum_fusion.3), channel_id=1, source_target_pairs={{0,1},{1,0},{2,3},{3,2},{4,5},{5,4},{6,7},{7,6},{8,9},{9,8},{10,11... | collective-permute-start | bytes 2138120 | tf_op jit(solution)/shard_map/ppermute | solution.py:303
  69.2 39.5 %collective-permute-start.18 = (bf16[96,3712]{1,0:T(8,128)(2,1)S(1)}, bf16[96,3712]{1,0:T(8,128)(2,1)S(1)}, u32[]{:S(2)}, u32[]{:S(2)}) collective-permute-start(bf16[96,3712]{1,0:T(8,128)(2,1)S(1)} %pad_maximum_fusion.4), channel_id=1, source_target_pairs={{0,1},{1,0},{2,3},{3,2},{4,5},{5,4},{6,7},{7,6},{8,9},{9,8},{10,11... | collective-permute-start | bytes 2138120 | tf_op jit(solution)/shard_map/ppermute | solution.py:303
  90.9 15.8 %collective-permute-start.25 = (bf16[48,3584]{1,0:T(8,128)(2,1)S(1)}, bf16[48,3584]{1,0:T(8,128)(2,1)S(1)}, u32[]{:S(2)}, u32[]{:S(2)}) collective-permute-start(bf16[48,3584]{1,0:T(8,128)(2,1)S(1)} %slice.276), channel_id=1, source_target_pairs={{0,2},{1,3},{2,0},{3,1},{4,6},{5,7},{6,4},{7,5},{8,10},{9,11},{10,... | collective-permute-start | bytes 1032200 | tf_op jit(solution)/shard_map/ppermute | solution.py:303
  100.9 21.6 %collective-permute-start.28 = (bf16[96,3584]{1,0:T(8,128)(2,1)S(1)}, bf16[96,3584]{1,0:T(8,128)(2,1)S(1)}, u32[]{:S(2)}, u32[]{:S(2)}) collective-permute-start(bf16[96,3584]{1,0:T(8,128)(2,1)S(1)} %get-tuple-element.74), channel_id=1, source_target_pairs={{0,1},{1,0},{2,3},{3,2},{4,5},{5,4},{6,7},{7,6},{8,9},{9,8},{10,11... | collective-permute-start | bytes 2064392 | tf_op jit(solution)/shard_map/ppermute | solution.py:303
  101.0 17.8 %collective-permute-start.23 = (bf16[32,3584]{1,0:T(8,128)(2,1)S(1)}, bf16[32,3584]{1,0:T(8,128)(2,1)S(1)}, u32[]{:S(2)}, u32[]{:S(2)}) collective-permute-start(bf16[32,3584]{1,0:T(8,128)(2,1)S(1)} %slice.281), channel_id=1, source_target_pairs={{0,4},{1,5},{2,6},{3,7},{4,0},{5,1},{6,2},{7,3},{8,12},{9,13},{10,... | collective-permute-start | bytes 688136 | tf_op jit(solution)/shard_map/ppermute | solution.py:303
  106.9 15.4 %collective-permute-start.26 = (bf16[32,3584]{1,0:T(8,128)(2,1)S(1)}, bf16[32,3584]{1,0:T(8,128)(2,1)S(1)}, u32[]{:S(2)}, u32[]{:S(2)}) collective-permute-start(bf16[32,3584]{1,0:T(8,128)(2,1)S(1)} %slice.280), channel_id=1, source_target_pairs={{0,4},{1,5},{2,6},{3,7},{4,0},{5,1},{6,2},{7,3},{8,12},{9,13},{10,... | collective-permute-start | bytes 688136 | tf_op jit(solution)/shard_map/ppermute | solution.py:303
  118.0 15.2 %collective-permute-start.32 = (bf16[96,3584]{1,0:T(8,128)(2,1)S(1)}, bf16[96,3584]{1,0:T(8,128)(2,1)S(1)}, u32[]{:S(2)}, u32[]{:S(2)}) collective-permute-start(bf16[96,3584]{1,0:T(8,128)(2,1)S(1)} %get-tuple-element.76), channel_id=1, source_target_pairs={{0,1},{1,0},{2,3},{3,2},{4,5},{5,4},{6,7},{7,6},{8,9},{9,8},{10,11... | collective-permute-start | bytes 2064392 | tf_op jit(solution)/shard_map/ppermute | solution.py:303
  118.2 27.1 %collective-permute-start.21 = (bf16[128,3584]{1,0:T(8,128)(2,1)S(1)}, bf16[128,3584]{1,0:T(8,128)(2,1)S(1)}, u32[]{:S(2)}, u32[]{:S(2)}) collective-permute-start(bf16[128,3584]{1,0:T(8,128)(2,1)S(1)} %slice_dynamic-update-slice_fusion), channel_id=1, source_target_pairs={{0,1},{1,0},{2,3},{3,2},{4,5},{5,4},{6,7},{7,6},{8,9},{9,8},{10,11... | collective-permute-start | bytes 2752520 | tf_op jit(solution)/shard_map/ppermute | solution.py:303
  145.7 13.3 %collective-permute-start.22 = (bf16[64,3584]{1,0:T(8,128)(2,1)S(1)}, bf16[64,3584]{1,0:T(8,128)(2,1)S(1)}, u32[]{:S(2)}, u32[]{:S(2)}) collective-permute-start(bf16[64,3584]{1,0:T(8,128)(2,1)S(1)} %slice.273), channel_id=1, source_target_pairs={{0,2},{1,3},{2,0},{3,1},{4,6},{5,7},{6,4},{7,5},{8,10},{9,11},{10,... | collective-permute-start | bytes 1376264 | tf_op jit(solution)/shard_map/ppermute | solution.py:303
  (22 other events, 177.5 us)

commit v3 on v2

--- a/solution.py
+++ b/solution.py
@@ -87,7 +87,8 @@
     return combined.astype(jnp.bfloat16)
 
 
-def prepare_kernel(experts, tokens, scores, ids, rows, perm):
+def prepare_kernel(experts, mine, tokens, scores, ids, rows, perm, index):
+    index[0] = mine[0]
     source = lax.broadcasted_iota(jnp.int32, (CHUNK, CHUNK), 0)
     place = lax.broadcasted_iota(jnp.int32, (CHUNK, CHUNK), 1)
     perm[...] = jnp.where((source & 3) * GROUP + (source >> 2) == place, 1.0, 0.0).astype(BF16)
@@ -110,88 +111,169 @@
     ).astype(BF16)
 
 
-def prepare(tokens, scores, ids, experts):
+def prepare(mine, tokens, scores, ids, experts):
     n, width = tokens.shape
+    smem, vmem = pl.BlockSpec(memory_space=pltpu.SMEM), pl.BlockSpec(memory_space=pltpu.VMEM)
     return pl.pallas_call(
         functools.partial(prepare_kernel, experts),
         out_shape=(
             jax.ShapeDtypeStruct((n, width + EXTRA), BF16),
             jax.ShapeDtypeStruct((CHUNK, CHUNK), BF16),
+            jax.ShapeDtypeStruct((1,), jnp.int32),
         ),
-        compiler_params=pltpu.CompilerParams(vmem_limit_bytes=8 * 1024 * 1024),
+        in_specs=[smem, vmem, vmem, vmem],
+        out_specs=(vmem, vmem, smem),
+        compiler_params=pltpu.CompilerParams(vmem_limit_bytes=12 * 1024 * 1024),
         name="prepare",
-    )(tokens, scores, ids)
-
-
-def unpack_chunk(words, scale, zero, at, out, tiles, tile):
+    )(mine, tokens, scores, ids)
+
+
+def unpack_kernel(later, words, scale, zero, *refs):
+    out, done, scales, zeros, held, arrived = refs[later:]
+    at = pl.program_id(0)
     sub = GROUP // WORD
+    tiles, _, tile = out.shape
+
+    def fetch(i):
+        rows = slice(i * GROUP, (i + 1) * GROUP)
+        return pltpu.make_async_copy(words.at[rows], held.at[i], arrived.at[i])
+
+    @pl.when(at == 0)
+    def _():
+        for i in range(held.shape[0]):
+            fetch(i).start()
+        scales[...] = scale[...].astype(F32)
+        zeros[...] = zero[...].astype(F32)
+        done[...] = jnp.zeros(done.shape, F32)
+
+    for i in range(held.shape[0]):
+
+        @pl.when(at == i)
+        def _():
+            fetch(i).wait()
+
     for t in range(tiles):
         cols = slice(t * tile, (t + 1) * tile)
         for g in range(WORD):
-            s = scale[pl.ds(at * WORD + g, 1), cols]
-            z = zero[pl.ds(at * WORD + g, 1), cols]
-            w = words[g * sub : (g + 1) * sub, cols].astype(jnp.int32)
+            s = scales[pl.ds(at * WORD + g, 1), cols]
+            z = zeros[pl.ds(at * WORD + g, 1), cols]
+            w = held[at, g * sub : (g + 1) * sub, cols].astype(jnp.int32)
             for j in range(WORD):
                 code = ((w >> (4 * j)) & 15).astype(F32)
-                out[t, pl.ds(pl.multiple_of(at * CHUNK + j * GROUP + g * sub, sub), sub), :] = (
-                    (code - z) * s
-                ).astype(BF16)
-
-
-def unpack_kernel(pairs, tiles, tile, *refs):
-    ins, outs, scratch = refs[: 3 * pairs], refs[3 * pairs : 4 * pairs], refs[4 * pairs + 1 :]
-    refs[4 * pairs][...] = jnp.zeros(refs[4 * pairs].shape, F32)
-    at = pl.program_id(0)
-
-    @pl.when(at == 0)
-    def _():
-        for p in range(pairs):
-            scratch[2 * p][...] = ins[3 * p + 1][...].astype(F32)
-            scratch[2 * p + 1][...] = ins[3 * p + 2][...].astype(F32)
-
-    for p in range(pairs):
-        unpack_chunk(
-            ins[3 * p], scratch[2 * p], scratch[2 * p + 1], at, outs[p], tiles, tile
-        )
-
-
-def unpack(triples, tile):
-    words, scale, _ = triples[0]
+                begin = pl.multiple_of(at * CHUNK + j * GROUP + g * sub, sub)
+                out[t, pl.ds(begin, sub), :] = ((code - z) * s).astype(BF16)
+
+
+def unpack(words, scale, zero, tile, before=()):
     n, cols = words.shape
-    tiles = cols // tile
-    steps = n // GROUP
-    in_specs, args, scratch = [], [], []
-    for w, s, z in triples:
-        in_specs += [
-            pl.BlockSpec((GROUP, cols), lambda i: (i, 0)),
-            pl.BlockSpec(s.shape, lambda i: (0, 0)),
-            pl.BlockSpec(z.shape, lambda i: (0, 0)),
-        ]
-        args += [w, s, z]
-        scratch += [pltpu.VMEM(s.shape, F32), pltpu.VMEM(z.shape, F32)]
-    return pl.pallas_call(
-        functools.partial(unpack_kernel, len(triples), tiles, tile),
+    tiles, steps = cols // tile, n // GROUP
+    words = pltpu.with_memory_space_constraint(words, pltpu.HBM)
+    resident = pl.BlockSpec(memory_space=pltpu.VMEM)
+    return pl.pallas_call(
+        functools.partial(unpack_kernel, len(before)),
         grid=(steps,),
-        in_specs=in_specs,
-        out_specs=[pl.BlockSpec(memory_space=pltpu.VMEM) for _ in triples]
-        + [pl.BlockSpec((8, 128), lambda i: (0, 0))],
-        out_shape=[pltpu.VMEM((tiles, n * WORD, tile), BF16) for _ in triples]
-        + [jax.ShapeDtypeStruct((8, 128), F32)],
-        scratch_shapes=scratch,
-        compiler_params=pltpu.CompilerParams(vmem_limit_bytes=20 * 1024 * 1024),
+        in_specs=[pl.BlockSpec(memory_space=pl.ANY)] + [resident] * (2 + len(before)),
+        out_specs=[resident] * 2,
+        out_shape=[
+            pltpu.VMEM((tiles, n * WORD, tile), BF16),
+            jax.ShapeDtypeStruct((8, 128), F32),
+        ],
+        scratch_shapes=[
+            pltpu.VMEM(scale.shape, F32),
+            pltpu.VMEM(zero.shape, F32),
+            pltpu.VMEM((steps, GROUP, cols), F32),
+            pltpu.SemaphoreType.DMA((steps,)),
+        ],
+        compiler_params=pltpu.CompilerParams(vmem_limit_bytes=14 * 1024 * 1024),
         cost_estimate=pl.CostEstimate(
-            flops=n * cols * 24 * len(triples),
-            bytes_accessed=n * cols * 4 * len(triples),
-            transcendentals=0,
+            flops=n * cols * 24, bytes_accessed=n * cols * 4, transcendentals=0
         ),
         name="unpack",
-    )(*args)
+    )(words, scale, zero, *before)
+
+
+def pack_kernel(cuts, *refs):
+    out = refs[-1]
+    at = 0
+    for ref, (begin, count) in zip(refs, cuts):
+        out[at : at + count, :] = ref[begin : begin + count, :]
+        at += count
+
+
+def pack(pieces, before=()):
+    resident = pl.BlockSpec(memory_space=pltpu.VMEM)
+    cuts = [(begin, count) for _, begin, count in pieces]
+    rows = sum(count for _, count in cuts)
+    return pl.pallas_call(
+        functools.partial(pack_kernel, cuts),
+        in_specs=[resident] * (len(pieces) + len(before)),
+        out_specs=resident,
+        out_shape=jax.ShapeDtypeStruct((rows, pieces[0][0].shape[1]), BF16),
+        compiler_params=pltpu.CompilerParams(vmem_limit_bytes=4 * 1024 * 1024),
+        cost_estimate=pl.CostEstimate(flops=0, bytes_accessed=rows * 4096, transcendentals=0),
+        name="pack",
+    )(*[p for p, _, _ in pieces], *before)
+
+
+def join_kernel(later, keep, got, *refs):
+    own, crossing = refs[later:]
+    half = own.shape[0]
+    own[...] = keep[:half].astype(F32) + got[:half].astype(F32)
+    crossing[...] = (keep[half:].astype(F32) + got[half:].astype(F32)).astype(BF16)
+
+
+def join(keep, got, before=()):
+    resident = pl.BlockSpec(memory_space=pltpu.VMEM)
+    rows, width = keep.shape
+    return pl.pallas_call(
+        functools.partial(join_kernel, len(before)),
+        in_specs=[resident] * (2 + len(before)),
+        out_specs=[resident] * 2,
+        out_shape=[
+            jax.ShapeDtypeStruct((rows // 2, width), F32),
+            jax.ShapeDtypeStruct((rows // 2, width), BF16),
+        ],
+        compiler_params=pltpu.CompilerParams(vmem_limit_bytes=4 * 1024 * 1024),
+        cost_estimate=pl.CostEstimate(flops=0, bytes_accessed=rows * 4096, transcendentals=0),
+        name="join",
+    )(keep, got, *before)
+
+
+def land_kernel(parts, *refs):
+    leaving, staying = refs[-2:]
+    u = staying.shape[0] // parts
+    for p in range(parts):
+        own, got = refs[2 * p], refs[2 * p + 1]
+        rows = lambda k: own[k * u : (k + 1) * u].astype(F32) + got[k * u : (k + 1) * u].astype(F32)
+        leaving[2 * p * u : (2 * p + 1) * u, :] = rows(0).astype(BF16)
+        leaving[(2 * p + 1) * u : (2 * p + 2) * u, :] = rows(2).astype(BF16)
+        staying[p * u : (p + 1) * u, :] = rows(1)
+
+
+def land(owns, gots, before=()):
+    resident = pl.BlockSpec(memory_space=pltpu.VMEM)
+    rows, width = owns[0].shape
+    parts = len(owns)
+    u = rows // 3
+    pairs = [a for pair in zip(owns, gots) for a in pair]
+    return pl.pallas_call(
+        functools.partial(land_kernel, parts),
+        in_specs=[resident] * (len(pairs) + len(before)),
+        out_specs=[resident] * 2,
+        out_shape=[
+            jax.ShapeDtypeStruct((2 * parts * u, width), BF16),
+            jax.ShapeDtypeStruct((parts * u, width), F32),
+        ],
+        compiler_params=pltpu.CompilerParams(vmem_limit_bytes=4 * 1024 * 1024),
+        cost_estimate=pl.CostEstimate(flops=0, bytes_accessed=rows * 4096, transcendentals=0),
+        name="land",
+    )(*pairs, *before)
 
 
 def expert_kernel(
-    experts, quarter, first, mine, near, cross, other, z, x, c, perm, wg, wu, wd,
-    keep_near, keep_far, send_near, send_far, done, xs, hs, hp, col,
+    experts, quarter, first, later, mine, near, cross, other, z, x, c, perm, wg, wu, wd, *refs
 ):
+    keep_near, keep_far, send_near, send_far, done, xs, hs, hp, col = refs[later:]
     i = pl.program_id(0)
     width = near.shape[1] - EXTRA
     far = z.shape[0]
@@ -247,7 +329,7 @@
             at += ref.shape[0]
 
 
-def expert_block(quarter, mine, near, cross, other, z, x, c, perm, wg, wu, wd, experts):
+def expert_block(quarter, mine, near, cross, other, z, x, c, perm, wg, wu, wd, experts, before):
     far, wide = z.shape
     u = far // 3
     width = wide - EXTRA
@@ -257,11 +339,11 @@
     resident = pl.BlockSpec(memory_space=pltpu.VMEM)
     out = lambda n: pl.BlockSpec((n, otile), lambda i: (0, jnp.maximum(i - first, 0)))
     return pl.pallas_call(
-        functools.partial(expert_kernel, experts, quarter, first),
+        functools.partial(expert_kernel, experts, quarter, first, len(before)),
         grid=(first + second,),
-        in_specs=[pl.BlockSpec(memory_space=pltpu.SMEM)] + [resident] * 10,
+        in_specs=[pl.BlockSpec(memory_space=pltpu.SMEM)] + [resident] * (10 + len(before)),
         out_specs=[out(2 * u), out(6 * u), out(2 * u), out(6 * u)]
-        + [pl.BlockSpec((8, 128), lambda i: (0, 0))],
+        + [pl.BlockSpec(memory_space=pltpu.VMEM)],
         out_shape=[jax.ShapeDtypeStruct((n * u, width), BF16) for n in (2, 6, 2, 6)]
         + [jax.ShapeDtypeStruct((8, 128), F32)],
         scratch_shapes=[
@@ -270,14 +352,14 @@
             pltpu.VMEM((rows, hidden), BF16),
             pltpu.VMEM((rows, 1), F32),
         ],
-        compiler_params=pltpu.CompilerParams(vmem_limit_bytes=16 * 1024 * 1024),
+        compiler_params=pltpu.CompilerParams(vmem_limit_bytes=12 * 1024 * 1024),
         cost_estimate=pl.CostEstimate(
             flops=2 * rows * width * hidden * 3,
             bytes_accessed=rows * width * 4,
             transcendentals=rows * hidden,
         ),
         name="expert_block",
-    )(mine, near, cross, other, z, x, c, perm, wg, wu, wd)
+    )(mine, near, cross, other, z, x, c, perm, wg, wu, wd, *before)
 
 
 def dense(
@@ -302,78 +384,76 @@
     def swap(value, bits):
         return lax.ppermute(value, "ep", [(i, i ^ bits) for i in range(experts)])
 
-    def after(values, *others):
-        return lax.optimization_barrier((values, others))[0]
-
     quarters = range(QUARTERS)
-    rows, perm = prepare(tokens, gate_scores, route_ids, experts)
-    w_gate, w_up, done_in = unpack(
-        [(gate_codes[0], gate_scale[0], gate_zero[0]), (up_codes[0], up_scale[0], up_zero[0])], 256
-    )
-    w_down, done_out = unpack([(down_codes[0], down_scale[0], down_zero[0])], 512)
-
-    mids = [rows[q * u : (q + 1) * u] for q in quarters]
-    twos = [swap(mids[q], 8) for q in quarters]
+    rows, perm, mine = prepare(mine, tokens, gate_scores, route_ids, experts)
+
+    half = n // 2
     cross = swap(rows, 2)
-    twos, cross = after((twos, cross), done_in, done_out)
-    ones = [swap(jnp.concatenate([mids[q], twos[q]]), 4) for q in quarters]
-    other = swap(jnp.concatenate([rows, cross]), 1)
-    z = [jnp.concatenate([ones[q], twos[q]]) for q in quarters]
-    x = [swap(z[q], 2) for q in quarters]
-
-    near, pairs, crossed, planes, back_one = [], [], [], [], []
-    sums = [None] * QUARTERS
-
-    def after_core(q):
-        keep, send = sent[q]
-        pair = keep.astype(F32) + send.astype(F32)
-        crossing = pair[3 * u :].astype(BF16)
-        pairs.append(pair[: 3 * u])
-        crossed.append(swap(crossing, 2))
-        return crossing
-
-    def after_x(q):
-        plane = pairs[q] + crossed[q].astype(F32)
-        leaving = plane[: 2 * u].astype(BF16)
-        planes.append(plane[2 * u :])
-        back_one.append(swap(leaving, 4))
-        return leaving
-
-    def after_one(q):
-        got = back_one[q].astype(F32)
-        leaving = (planes[q] + got[u:]).astype(BF16)
-        sums[q] = got[:u] + swap(leaving, 8).astype(F32)
-        return leaving
-
-    sent, done = [], None
-    for q in quarters:
-        zq, xq = (z[q], x[q]) if done is None else after((z[q], x[q]), done)
-        c = swap(jnp.concatenate([zq, xq]), 1)
-        due = [x[q + 1]] if q + 1 < QUARTERS else []
-        if q == 0:
-            due += [z[i] for i in quarters]
-        if q >= 2:
-            due.append(after_core(q - 2))
-        if q >= 3:
-            due.append(after_x(q - 3))
-        if due:
-            c = after(c, *due)
-        keep_near, keep_far, send_near, send_far, done = expert_block(
-            q, mine, rows, cross, other, zq, xq, c, perm, w_gate, w_up, w_down, experts
+    first = [swap(rows[:half], 4 * k) for k in range(1, 4)]
+    two = swap(rows[half:], 8)
+    w_down, done_down = unpack(down_codes[0], down_scale[0], down_zero[0], 1792)
+    w_gate, done_gate = unpack(gate_codes[0], gate_scale[0], gate_zero[0], 512)
+    w_up, done_up = unpack(up_codes[0], up_scale[0], up_zero[0], 512)
+    unpacked = [done_down, done_gate, done_up]
+
+    z = [pack([(first[k], q * u, u) for k in range(3)], unpacked + [two]) for q in range(2)]
+    onward = pack([(rows, half, half), (two, 0, half)], unpacked)
+    one = swap(onward, 4)
+    other = swap(pack([(rows, 0, n), (cross, 0, n)], unpacked), 1)
+    z += [pack([(one, q * u, u), (two, q * u, u), (one, half + q * u, u)]) for q in range(2)]
+    x = [swap(v, 2) for v in z]
+    both, done, near, back = [], [], [], []
+    own, crossing, crossed = [None] * QUARTERS, [None] * QUARTERS, [None] * QUARTERS
+    leaving, staying = [None] * QUARTERS, [None] * QUARTERS
+
+    def start_core(q, before):
+        both.append(pack([(z[q], 0, 3 * u), (x[q], 0, 3 * u)], before))
+
+    def after_core(q, before):
+        own[q], crossing[q] = join(near[q][1], back[q], before)
+        crossed[q] = swap(crossing[q], 2)
+
+    def after_x(q, before):
+        leaving[q], staying[q] = land([own[q]], [crossed[q]], before)
+
+    def expert(q, before):
+        keep_near, keep_far, send_near, send_far, token = expert_block(
+            q, mine, rows, cross, other, z[q], x[q], swap(both[q], 1), perm,
+            w_gate, w_up, w_down, experts, before,
         )
-        near.append((keep_near, send_near))
-        sent.append((keep_far, swap(send_far, 1)))
-    for q in range(max(QUARTERS - 2, 0), QUARTERS):
-        after_core(q)
-    for q in range(max(QUARTERS - 3, 0), QUARTERS):
-        after_x(q)
-    for q in quarters:
-        after_one(q)
-    sends = [s for _, s in near]
-    got = swap(jnp.concatenate([s[:u] for s in sends] + [s[u:] for s in sends]), 1)
-    kept = [k for k, _ in near]
-    pair = jnp.concatenate([k[:u] for k in kept] + [k[u:] for k in kept]).astype(F32) + got.astype(F32)
-    total = pair[:n] + swap(pair[n:].astype(BF16), 2).astype(F32) + jnp.concatenate(sums)
+        done.append(token)
+        near.append((keep_near, keep_far, send_near))
+        back.append(swap(send_far, 1))
+
+    start_core(0, [z[2], z[3]])
+    expert(0, [])
+    start_core(1, done[-1:])
+    start_core(2, done[-1:])
+    expert(1, [both[2]])
+    start_core(3, done[-1:])
+    after_core(0, done[-1:])
+    expert(2, [both[3], crossing[0]])
+    after_core(1, done[-1:])
+    after_x(0, done[-1:])
+    expert(3, [crossing[1], leaving[0]])
+    after_core(2, done[-1:])
+    after_core(3, [crossing[2]])
+    after_x(1, [crossing[3]])
+    after_x(2, [leaving[1]])
+
+    sends = [s for _, _, s in near]
+    kept = [k for k, _, _ in near]
+    send = pack([(s, 0, u) for s in sends] + [(s, u, u) for s in sends], done[-1:])
+    keep = pack([(k, 0, u) for k in kept] + [(k, u, u) for k in kept], done[-1:])
+    home, away = join(keep, swap(send, 1), [leaving[2]])
+    away = swap(away, 2)
+    after_x(3, [])
+    sums = []
+    for q in range(QUARTERS):
+        got = swap(leaving[q], 4).astype(F32)
+        last = swap((staying[q] + got[u:]).astype(BF16), 8).astype(F32)
+        sums.append(got[:u] + last)
+    total = home + away.astype(F32) + jnp.concatenate(sums)
     return total.astype(BF16)
 
 

time: 160 us -> 147 us (0.919)
  waiting for transfers between devices: 71.5 us -> 54.7 us
  starting transfers between devices: 29.7 us -> 35.8 us
    ppermute x36 -> x33, waiting for transfers between devices: 71.5 us -> 54.7 us  [swap(): return lax.ppermute(value, 'ep', [(i, i ^ bits) for i in range(experts)])]
    ppermute x36 -> x33, starting transfers between devices: 29.7 us -> 35.8 us  [swap(): return lax.ppermute(value, 'ep', [(i, i ^ bits) for i in range(experts)])]
    unnamed x39 -> x16, local copies, waits for them, and re-layouts: 6.87 us -> 5.91 us
    pallas_call x6 -> x28, Pallas kernels: 47.3 us -> 47.5 us  [the longest x4 31.8 us: expert_block(): pl.pallas_call(functools.partial(expert_kernel, experts, quarter, first,...]
  transfers between devices with their start and end apart: 36 -> 33, of which waited for: 17 -> 14; matrix products, arithmetic and copies ran while one was open for 2% -> 0% of each run, Pallas kernels for 30% -> 32%
where the time goes in v3:
time: 147 us; the launch traced here: 146 us
  waiting for transfers between devices  54.7 us (37%)
  Pallas kernels  48.4 us (33%)
  starting transfers between devices  35.8 us (24%)
  local copies, waits for them, and re-layouts  5.94 us (4%)
    ppermute x33, waiting for transfers between devices, swap(): return lax.ppermute(value, 'ep', [(i, i ^ bits) for i in range(experts)])  54.7 us
    ppermute x33, starting transfers between devices, swap(): return lax.ppermute(value, 'ep', [(i, i ^ bits) for i in range(experts)])  35.8 us
    pallas_call x4, Pallas kernels, expert_block(): pl.pallas_call(functools.partial(expert_kernel, experts, quarter, first,...  31.8 us
    pallas_call x3, Pallas kernels, unpack(): pl.pallas_call(functools.partial(unpack_kernel, len(before)), grid=(steps...  14.1 us
    unnamed x16, local copies, waits for them, and re-layouts  5.91 us
  transfers between devices with their start and end apart: 33, of which 14 were waited for; matrix products, arithmetic and copies ran while one was open for 0% of the time, Pallas kernels for 32%

profile of v3, /device:TPU:0, one launch (start us, length us, event | category | flops | bytes accessed | tf_op | source)
XLA Modules:
  0.0 146.4 jit_solution(15369255426848727520)
XLA Ops:
  3.5 4.1 %collective-permute-start.5 = (bf16[32,3712]{1,0:T(8,128)(2,1)S(1)}, bf16[32,3712]{1,0:T(8,128)(2,1)S(1)}, u32[]{:S(2)}, u32[]{:S(2)}) collective-permute-start(bf16[32,3712]{1,0:T(8,128)(2,1)S(1)} %get-tuple-element.100), channel_id=1, source_target_pairs={{0,8},{1,9},{2,10},{3,11},{4,12},{5,13},{6,14},{7,15},{8,0},{9,1},... | collective-permute-start | bytes 712712 | tf_op jit(solution)/shard_map/ppermute | solution.py:385
  9.1 1.6 %collective-permute-start.2 = (bf16[32,3712]{1,0:T(8,128)(2,1)S(1)}, bf16[32,3712]{1,0:T(8,128)(2,1)S(1)}, u32[]{:S(2)}, u32[]{:S(2)}) collective-permute-start(bf16[32,3712]{1,0:T(8,128)(2,1)S(1)} %get-tuple-element.99), channel_id=1, source_target_pairs={{0,4},{1,5},{2,6},{3,7},{4,0},{5,1},{6,2},{7,3},{8,12},{9,13},{10,... | collective-permute-start | bytes 712712 | tf_op jit(solution)/shard_map/ppermute | solution.py:385
  11.0 2.5 %collective-permute-start.4 = (bf16[32,3712]{1,0:T(8,128)(2,1)S(1)}, bf16[32,3712]{1,0:T(8,128)(2,1)S(1)}, u32[]{:S(2)}, u32[]{:S(2)}) collective-permute-start(bf16[32,3712]{1,0:T(8,128)(2,1)S(1)} %get-tuple-element.99), channel_id=1, source_target_pairs={{0,12},{1,13},{2,14},{3,15},{4,8},{5,9},{6,10},{7,11},{8,4},{9,5},... | collective-permute-start | bytes 712712 | tf_op jit(solution)/shard_map/ppermute | solution.py:385
  15.1 5.4 %unpack.3 = (bf16[2,1024,1792]{2,1,0:T(8,128)(2,1)S(1)}, f32[8,128]{1,0:T(8,128)S(1)}) custom-call(f32[256,3584]{1,0:T(8,128)} %bitcast.16, bf16[8,3584]{1,0:T(8,128)(2,1)S(1)} %bitcast.14, bf16[8,3584]{1,0:T(8,128)(2,1)S(1)} %bitcast.15), custom_call_target="tpu_custom_call" | custom-call | flops 22020096 | bytes 3670016 | tf_op jit(solution)/shard_map/unpack/pallas_call | solution.py:172
  22.2 4.4 %unpack.4 = (bf16[2,3584,512]{2,1,0:T(8,128)(2,1)S(1)}, f32[8,128]{1,0:T(8,128)S(1)}) custom-call(f32[896,1024]{1,0:T(8,128)} %bitcast.17, bf16[28,1024]{1,0:T(8,128)(2,1)S(1)} %bitcast.10, bf16[28,1024]{1,0:T(8,128)(2,1)S(1)} %bitcast.11), custom_call_target="tpu_custom_call" | custom-call | flops 22020096 | bytes 3670016 | tf_op jit(solution)/shard_map/unpack/pallas_call | solution.py:172
  26.6 4.4 %unpack.5 = (bf16[2,3584,512]{2,1,0:T(8,128)(2,1)S(1)}, f32[8,128]{1,0:T(8,128)S(1)}) custom-call(f32[896,1024]{1,0:T(8,128)} %bitcast.18, bf16[28,1024]{1,0:T(8,128)(2,1)S(1)} %bitcast.12, bf16[28,1024]{1,0:T(8,128)(2,1)S(1)} %bitcast.13), custom_call_target="tpu_custom_call" | custom-call | flops 22020096 | bytes 3670016 | tf_op jit(solution)/shard_map/unpack/pallas_call | solution.py:172
  31.7 2.9 %collective-permute-done.3.refs_1_ = bf16[32,3712]{1,0:T(8,128)(2,1)S(1)} collective-permute-done((bf16[32,3712]{1,0:T(8,128)(2,1)S(1)}, bf16[32,3712]{1,0:T(8,128)(2,1)S(1)}, u32[]{:S(2)}, u32[]{:S(2)}) %collective-permute-start.3) | collective-permute-done | bytes 237600 | tf_op jit(solution)/shard_map/ppermute | solution.py:385
  34.6 1.9 %collective-permute-start.6 = (bf16[48,3712]{1,0:T(8,128)(2,1)S(1)}, bf16[48,3712]{1,0:T(8,128)(2,1)S(1)}, u32[]{:S(2)}, u32[]{:S(2)}) collective-permute-start(bf16[48,3712]{1,0:T(8,128)(2,1)S(1)} %pack.13.refs_0_.z), channel_id=1, source_target_pairs={{0,2},{1,3},{2,0},{3,1},{4,6},{5,7},{6,4},{7,5},{8,10},{9,11},{10,... | collective-permute-start | bytes 1069064 | tf_op jit(solution)/shard_map/ppermute | solution.py:385
  36.7 7.3 %collective-permute-done.7.refs_0_.refs_2_ = bf16[64,3712]{1,0:T(8,128)(2,1)S(1)} collective-permute-done((bf16[64,3712]{1,0:T(8,128)(2,1)S(1)}, bf16[64,3712]{1,0:T(8,128)(2,1)S(1)}, u32[]{:S(2)}, u32[]{:S(2)}) %collective-permute-start.7) | collective-permute-done | bytes 475168 | tf_op jit(solution)/shard_map/ppermute | solution.py:385
  44.2 1.6 %collective-permute-start.9 = (bf16[48,3712]{1,0:T(8,128)(2,1)S(1)}, bf16[48,3712]{1,0:T(8,128)(2,1)S(1)}, u32[]{:S(2)}, u32[]{:S(2)}) collective-permute-start(bf16[48,3712]{1,0:T(8,128)(2,1)S(1)} %pack.18.refs_0_.z), channel_id=1, source_target_pairs={{0,2},{1,3},{2,0},{3,1},{4,6},{5,7},{6,4},{7,5},{8,10},{9,11},{10,... | collective-permute-start | bytes 1069064 | tf_op jit(solution)/shard_map/ppermute | solution.py:385
  46.3 7.9 %expert_block.4 = (bf16[32,3584]{1,0:T(8,128)(2,1)S(1)}, bf16[96,3584]{1,0:T(8,128)(2,1)S(1)}, bf16[32,3584]{1,0:T(8,128)(2,1)S(1)}, bf16[96,3584]{1,0:T(8,128)(2,1)S(1)}, f32[8,128]{1,0:T(8,128)S(1)}) custom-call(s32[1]{0:T(128)} %get-tuple-element.52.mine, bf16[64,3712]{1,0:T(8,128)(2,1)S(1)} %get-tuple-element.53.refs_0_.near, ...), custom_call_target="tpu_custom_call" | custom-call | flops 5637144576 | bytes 3670016 | tf_op jit(solution)/shard_map/expert_block/pallas_call | solution.py:341
  55.1 1.6 %collective-permute-start.11 = (bf16[48,3712]{1,0:T(8,128)(2,1)S(1)}, bf16[48,3712]{1,0:T(8,128)(2,1)S(1)}, u32[]{:S(2)}, u32[]{:S(2)}) collective-permute-start(bf16[48,3712]{1,0:T(8,128)(2,1)S(1)} %pack.15.refs_2_.refs_0_.z), channel_id=1, source_target_pairs={{0,2},{1,3},{2,0},{3,1},{4,6},{5,7},{6,4},{7,5},{8,10},{9,11},{10,... | collective-permute-start | bytes 1069064 | tf_op jit(solution)/shard_map/ppermute | solution.py:385
  56.7 9.1 %collective-permute-done.11.refs_1_.x = bf16[48,3712]{1,0:T(8,128)(2,1)S(1)} collective-permute-done((bf16[48,3712]{1,0:T(8,128)(2,1)S(1)}, bf16[48,3712]{1,0:T(8,128)(2,1)S(1)}, u32[]{:S(2)}, u32[]{:S(2)}) %collective-permute-start.11) | collective-permute-done | bytes 356384 | tf_op jit(solution)/shard_map/ppermute | solution.py:385
  68.0 7.9 %expert_block.5 = (bf16[32,3584]{1,0:T(8,128)(2,1)S(1)}, bf16[96,3584]{1,0:T(8,128)(2,1)S(1)}, bf16[32,3584]{1,0:T(8,128)(2,1)S(1)}, bf16[96,3584]{1,0:T(8,128)(2,1)S(1)}, f32[8,128]{1,0:T(8,128)S(1)}) custom-call(s32[1]{0:T(128)} %get-tuple-element.52.mine, bf16[64,3712]{1,0:T(8,128)(2,1)S(1)} %get-tuple-element.53.refs_0_.near, ...), custom_call_target="tpu_custom_call" | custom-call | flops 5637144576 | bytes 3670016 | tf_op jit(solution)/shard_map/expert_block/pallas_call | solution.py:341
  77.3 8.1 %expert_block.6 = (bf16[32,3584]{1,0:T(8,128)(2,1)S(1)}, bf16[96,3584]{1,0:T(8,128)(2,1)S(1)}, bf16[32,3584]{1,0:T(8,128)(2,1)S(1)}, bf16[96,3584]{1,0:T(8,128)(2,1)S(1)}, f32[8,128]{1,0:T(8,128)S(1)}) custom-call(s32[1]{0:T(128)} %get-tuple-element.52.mine, bf16[64,3712]{1,0:T(8,128)(2,1)S(1)} %get-tuple-element.53.refs_0_.near, ...), custom_call_target="tpu_custom_call" | custom-call | flops 5637144576 | bytes 3670016 | tf_op jit(solution)/shard_map/expert_block/pallas_call | solution.py:341
  86.0 5.9 %collective-permute-start.24 = (bf16[32,3584]{1,0:T(8,128)(2,1)S(1)}, bf16[32,3584]{1,0:T(8,128)(2,1)S(1)}, u32[]{:S(2)}, u32[]{:S(2)}) collective-permute-start(bf16[32,3584]{1,0:T(8,128)(2,1)S(1)} %get-tuple-element.74.refs_1_), channel_id=1, source_target_pairs={{0,4},{1,5},{2,6},{3,7},{4,0},{5,1},{6,2},{7,3},{8,12},{9,13},{10,... | collective-permute-start | bytes 688136 | tf_op jit(solution)/shard_map/ppermute | solution.py:385
  91.9 5.5 %collective-permute-done.24 = bf16[32,3584]{1,0:T(8,128)(2,1)S(1)} collective-permute-done((bf16[32,3584]{1,0:T(8,128)(2,1)S(1)}, bf16[32,3584]{1,0:T(8,128)(2,1)S(1)}, u32[]{:S(2)}, u32[]{:S(2)}) %collective-permute-start.24) | collective-permute-done | bytes 229408 | tf_op jit(solution)/shard_map/ppermute | solution.py:385
  99.1 7.9 %expert_block.7 = (bf16[32,3584]{1,0:T(8,128)(2,1)S(1)}, bf16[96,3584]{1,0:T(8,128)(2,1)S(1)}, bf16[32,3584]{1,0:T(8,128)(2,1)S(1)}, bf16[96,3584]{1,0:T(8,128)(2,1)S(1)}, f32[8,128]{1,0:T(8,128)S(1)}) custom-call(s32[1]{0:T(128)} %get-tuple-element.52.mine, bf16[64,3712]{1,0:T(8,128)(2,1)S(1)} %get-tuple-element.53.refs_0_.near, ...), custom_call_target="tpu_custom_call" | custom-call | flops 5637144576 | bytes 3670016 | tf_op jit(solution)/shard_map/expert_block/pallas_call | solution.py:341
  107.1 3.7 %collective-permute-start.25 = (bf16[16,3584]{1,0:T(8,128)(2,1)S(1)}, bf16[16,3584]{1,0:T(8,128)(2,1)S(1)}, u32[]{:S(2)}, u32[]{:S(2)}) collective-permute-start(bf16[16,3584]{1,0:T(8,128)(2,1)S(1)} %fusion.4), channel_id=1, source_target_pairs={{0,8},{1,9},{2,10},{3,11},{4,12},{5,13},{6,14},{7,15},{8,0},{9,1},... | collective-permute-start | bytes 344072 | tf_op jit(solution)/shard_map/ppermute | solution.py:385
  112.6 4.6 %collective-permute-done.25 = bf16[16,3584]{1,0:T(8,128)(2,1)S(1)} collective-permute-done((bf16[16,3584]{1,0:T(8,128)(2,1)S(1)}, bf16[16,3584]{1,0:T(8,128)(2,1)S(1)}, u32[]{:S(2)}, u32[]{:S(2)}) %collective-permute-start.25) | collective-permute-done | bytes 114720 | tf_op jit(solution)/shard_map/ppermute | solution.py:385
  117.9 4.3 %collective-permute-done.20.refs_1_ = bf16[48,3584]{1,0:T(8,128)(2,1)S(1)} collective-permute-done((bf16[48,3584]{1,0:T(8,128)(2,1)S(1)}, bf16[48,3584]{1,0:T(8,128)(2,1)S(1)}, u32[]{:S(2)}, u32[]{:S(2)}) %collective-permute-start.20) | collective-permute-done | bytes 344096 | tf_op jit(solution)/shard_map/ppermute | solution.py:385
  124.0 7.0 %collective-permute-done.28 = bf16[32,3584]{1,0:T(8,128)(2,1)S(1)} collective-permute-done((bf16[32,3584]{1,0:T(8,128)(2,1)S(1)}, bf16[32,3584]{1,0:T(8,128)(2,1)S(1)}, u32[]{:S(2)}, u32[]{:S(2)}) %collective-permute-start.28) | collective-permute-done | bytes 229408 | tf_op jit(solution)/shard_map/ppermute | solution.py:385
  132.8 6.2 %collective-permute-done.31 = bf16[32,3584]{1,0:T(8,128)(2,1)S(1)} collective-permute-done((bf16[32,3584]{1,0:T(8,128)(2,1)S(1)}, bf16[32,3584]{1,0:T(8,128)(2,1)S(1)}, u32[]{:S(2)}, u32[]{:S(2)}) %collective-permute-start.31) | collective-permute-done | bytes 229408 | tf_op jit(solution)/shard_map/ppermute | solution.py:385
  140.3 5.1 %collective-permute-done.32 = bf16[16,3584]{1,0:T(8,128)(2,1)S(1)} collective-permute-done((bf16[16,3584]{1,0:T(8,128)(2,1)S(1)}, bf16[16,3584]{1,0:T(8,128)(2,1)S(1)}, u32[]{:S(2)}, u32[]{:S(2)}) %collective-permute-start.32) | collective-permute-done | bytes 114720 | tf_op jit(solution)/shard_map/ppermute | solution.py:385
  (101 shorter events, 25.3 us)
Async XLA Ops:
  3.5 27.5 %collective-permute-start.5 = (bf16[32,3712]{1,0:T(8,128)(2,1)S(1)}, bf16[32,3712]{1,0:T(8,128)(2,1)S(1)}, u32[]{:S(2)}, u32[]{:S(2)}) collective-permute-start(bf16[32,3712]{1,0:T(8,128)(2,1)S(1)} %get-tuple-element.100), channel_id=1, source_target_pairs={{0,8},{1,9},{2,10},{3,11},{4,12},{5,13},{6,14},{7,15},{8,0},{9,1},... | collective-permute-start | bytes 712712 | tf_op jit(solution)/shard_map/ppermute | solution.py:385
  7.6 29.0 %collective-permute-start = (bf16[64,3712]{1,0:T(8,128)(2,1)S(1)}, bf16[64,3712]{1,0:T(8,128)(2,1)S(1)}, u32[]{:S(2)}, u32[]{:S(2)}) collective-permute-start(bf16[64,3712]{1,0:T(8,128)(2,1)S(1)} %get-tuple-element.53.refs_0_.near), channel_id=1, source_target_pairs={{0,2},{1,3},{2,0},{3,1},{4,6},{5,7},{6,4},{7,5},{8,10},{9,11},{10,... | collective-permute-start | bytes 1425416 | tf_op jit(solution)/shard_map/ppermute | solution.py:385
  9.1 22.7 %collective-permute-start.2 = (bf16[32,3712]{1,0:T(8,128)(2,1)S(1)}, bf16[32,3712]{1,0:T(8,128)(2,1)S(1)}, u32[]{:S(2)}, u32[]{:S(2)}) collective-permute-start(bf16[32,3712]{1,0:T(8,128)(2,1)S(1)} %get-tuple-element.99), channel_id=1, source_target_pairs={{0,4},{1,5},{2,6},{3,7},{4,0},{5,1},{6,2},{7,3},{8,12},{9,13},{10,... | collective-permute-start | bytes 712712 | tf_op jit(solution)/shard_map/ppermute | solution.py:385
  10.7 24.0 %collective-permute-start.3 = (bf16[32,3712]{1,0:T(8,128)(2,1)S(1)}, bf16[32,3712]{1,0:T(8,128)(2,1)S(1)}, u32[]{:S(2)}, u32[]{:S(2)}) collective-permute-start(bf16[32,3712]{1,0:T(8,128)(2,1)S(1)} %get-tuple-element.99), channel_id=1, source_target_pairs={{0,8},{1,9},{2,10},{3,11},{4,12},{5,13},{6,14},{7,15},{8,0},{9,1},... | collective-permute-start | bytes 712712 | tf_op jit(solution)/shard_map/ppermute | solution.py:385
  11.0 23.6 %collective-permute-start.4 = (bf16[32,3712]{1,0:T(8,128)(2,1)S(1)}, bf16[32,3712]{1,0:T(8,128)(2,1)S(1)}, u32[]{:S(2)}, u32[]{:S(2)}) collective-permute-start(bf16[32,3712]{1,0:T(8,128)(2,1)S(1)} %get-tuple-element.99), channel_id=1, source_target_pairs={{0,12},{1,13},{2,14},{3,15},{4,8},{5,9},{6,10},{7,11},{8,4},{9,5},... | collective-permute-start | bytes 712712 | tf_op jit(solution)/shard_map/ppermute | solution.py:385
  31.0 13.0 %collective-permute-start.7 = (bf16[64,3712]{1,0:T(8,128)(2,1)S(1)}, bf16[64,3712]{1,0:T(8,128)(2,1)S(1)}, u32[]{:S(2)}, u32[]{:S(2)}) collective-permute-start(bf16[64,3712]{1,0:T(8,128)(2,1)S(1)} %pack.14), channel_id=1, source_target_pairs={{0,4},{1,5},{2,6},{3,7},{4,0},{5,1},{6,2},{7,3},{8,12},{9,13},{10,... | collective-permute-start | bytes 1425416 | tf_op jit(solution)/shard_map/ppermute | solution.py:385
  44.2 10.8 %collective-permute-start.9 = (bf16[48,3712]{1,0:T(8,128)(2,1)S(1)}, bf16[48,3712]{1,0:T(8,128)(2,1)S(1)}, u32[]{:S(2)}, u32[]{:S(2)}) collective-permute-start(bf16[48,3712]{1,0:T(8,128)(2,1)S(1)} %pack.18.refs_0_.z), channel_id=1, source_target_pairs={{0,2},{1,3},{2,0},{3,1},{4,6},{5,7},{6,4},{7,5},{8,10},{9,11},{10,... | collective-permute-start | bytes 1069064 | tf_op jit(solution)/shard_map/ppermute | solution.py:385
  55.0 13.0 %collective-permute-start.10 = (bf16[96,3712]{1,0:T(8,128)(2,1)S(1)}, bf16[96,3712]{1,0:T(8,128)(2,1)S(1)}, u32[]{:S(2)}, u32[]{:S(2)}) collective-permute-start(bf16[96,3712]{1,0:T(8,128)(2,1)S(1)} %pack.19), channel_id=1, source_target_pairs={{0,1},{1,0},{2,3},{3,2},{4,5},{5,4},{6,7},{7,6},{8,9},{9,8},{10,11... | collective-permute-start | bytes 2138120 | tf_op jit(solution)/shard_map/ppermute | solution.py:385
  55.1 10.7 %collective-permute-start.11 = (bf16[48,3712]{1,0:T(8,128)(2,1)S(1)}, bf16[48,3712]{1,0:T(8,128)(2,1)S(1)}, u32[]{:S(2)}, u32[]{:S(2)}) collective-permute-start(bf16[48,3712]{1,0:T(8,128)(2,1)S(1)} %pack.15.refs_2_.refs_0_.z), channel_id=1, source_target_pairs={{0,2},{1,3},{2,0},{3,1},{4,6},{5,7},{6,4},{7,5},{8,10},{9,11},{10,... | collective-permute-start | bytes 1069064 | tf_op jit(solution)/shard_map/ppermute | solution.py:385
  65.9 11.4 %collective-permute-start.12 = (bf16[96,3712]{1,0:T(8,128)(2,1)S(1)}, bf16[96,3712]{1,0:T(8,128)(2,1)S(1)}, u32[]{:S(2)}, u32[]{:S(2)}) collective-permute-start(bf16[96,3712]{1,0:T(8,128)(2,1)S(1)} %pack.20.refs_0_), channel_id=1, source_target_pairs={{0,1},{1,0},{2,3},{3,2},{4,5},{5,4},{6,7},{7,6},{8,9},{9,8},{10,11... | collective-permute-start | bytes 2138120 | tf_op jit(solution)/shard_map/ppermute | solution.py:385
  66.0 9.9 %collective-permute-start.14 = (bf16[96,3584]{1,0:T(8,128)(2,1)S(1)}, bf16[96,3584]{1,0:T(8,128)(2,1)S(1)}, u32[]{:S(2)}, u32[]{:S(2)}) collective-permute-start(bf16[96,3584]{1,0:T(8,128)(2,1)S(1)} %get-tuple-element.66), channel_id=1, source_target_pairs={{0,1},{1,0},{2,3},{3,2},{4,5},{5,4},{6,7},{7,6},{8,9},{9,8},{10,11... | collective-permute-start | bytes 2064392 | tf_op jit(solution)/shard_map/ppermute | solution.py:385
  66.5 10.3 %collective-permute-start.13 = (bf16[48,3712]{1,0:T(8,128)(2,1)S(1)}, bf16[48,3712]{1,0:T(8,128)(2,1)S(1)}, u32[]{:S(2)}, u32[]{:S(2)}) collective-permute-start(bf16[48,3712]{1,0:T(8,128)(2,1)S(1)} %pack.16.refs_3_.refs_0_.z), channel_id=1, source_target_pairs={{0,2},{1,3},{2,0},{3,1},{4,6},{5,7},{6,4},{7,5},{8,10},{9,11},{10,... | collective-permute-start | bytes 1069064 | tf_op jit(solution)/shard_map/ppermute | solution.py:385
  76.1 9.8 %collective-permute-start.17 = (bf16[48,3584]{1,0:T(8,128)(2,1)S(1)}, bf16[48,3584]{1,0:T(8,128)(2,1)S(1)}, u32[]{:S(2)}, u32[]{:S(2)}) collective-permute-start(bf16[48,3584]{1,0:T(8,128)(2,1)S(1)} %get-tuple-element.67.refs_1_), channel_id=1, source_target_pairs={{0,2},{1,3},{2,0},{3,1},{4,6},{5,7},{6,4},{7,5},{8,10},{9,11},{10,... | collective-permute-start | bytes 1032200 | tf_op jit(solution)/shard_map/ppermute | solution.py:385
  76.7 20.8 %collective-permute-start.16 = (bf16[96,3584]{1,0:T(8,128)(2,1)S(1)}, bf16[96,3584]{1,0:T(8,128)(2,1)S(1)}, u32[]{:S(2)}, u32[]{:S(2)}) collective-permute-start(bf16[96,3584]{1,0:T(8,128)(2,1)S(1)} %get-tuple-element.70), channel_id=1, source_target_pairs={{0,1},{1,0},{2,3},{3,2},{4,5},{5,4},{6,7},{7,6},{8,9},{9,8},{10,11... | collective-permute-start | bytes 2064392 | tf_op jit(solution)/shard_map/ppermute | solution.py:385
  76.9 22.2 %collective-permute-start.15 = (bf16[96,3712]{1,0:T(8,128)(2,1)S(1)}, bf16[96,3712]{1,0:T(8,128)(2,1)S(1)}, u32[]{:S(2)}, u32[]{:S(2)}) collective-permute-start(bf16[96,3712]{1,0:T(8,128)(2,1)S(1)} %pack.21.refs_0_), channel_id=1, source_target_pairs={{0,1},{1,0},{2,3},{3,2},{4,5},{5,4},{6,7},{7,6},{8,9},{9,8},{10,11... | collective-permute-start | bytes 2138120 | tf_op jit(solution)/shard_map/ppermute | solution.py:385
  86.0 11.4 %collective-permute-start.24 = (bf16[32,3584]{1,0:T(8,128)(2,1)S(1)}, bf16[32,3584]{1,0:T(8,128)(2,1)S(1)}, u32[]{:S(2)}, u32[]{:S(2)}) collective-permute-start(bf16[32,3584]{1,0:T(8,128)(2,1)S(1)} %get-tuple-element.74.refs_1_), channel_id=1, source_target_pairs={{0,4},{1,5},{2,6},{3,7},{4,0},{5,1},{6,2},{7,3},{8,12},{9,13},{10,... | collective-permute-start | bytes 688136 | tf_op jit(solution)/shard_map/ppermute | solution.py:385
  91.9 19.3 %collective-permute-start.19 = (bf16[96,3584]{1,0:T(8,128)(2,1)S(1)}, bf16[96,3584]{1,0:T(8,128)(2,1)S(1)}, u32[]{:S(2)}, u32[]{:S(2)}) collective-permute-start(bf16[96,3584]{1,0:T(8,128)(2,1)S(1)} %get-tuple-element.82), channel_id=1, source_target_pairs={{0,1},{1,0},{2,3},{3,2},{4,5},{5,4},{6,7},{7,6},{8,9},{9,8},{10,11... | collective-permute-start | bytes 2064392 | tf_op jit(solution)/shard_map/ppermute | solution.py:385
  97.6 14.6 %collective-permute-start.21 = (bf16[48,3584]{1,0:T(8,128)(2,1)S(1)}, bf16[48,3584]{1,0:T(8,128)(2,1)S(1)}, u32[]{:S(2)}, u32[]{:S(2)}) collective-permute-start(bf16[48,3584]{1,0:T(8,128)(2,1)S(1)} %get-tuple-element.72.refs_0_), channel_id=1, source_target_pairs={{0,2},{1,3},{2,0},{3,1},{4,6},{5,7},{6,4},{7,5},{8,10},{9,11},{10,... | collective-permute-start | bytes 1032200 | tf_op jit(solution)/shard_map/ppermute | solution.py:385
  107.1 10.1 %collective-permute-start.25 = (bf16[16,3584]{1,0:T(8,128)(2,1)S(1)}, bf16[16,3584]{1,0:T(8,128)(2,1)S(1)}, u32[]{:S(2)}, u32[]{:S(2)}) collective-permute-start(bf16[16,3584]{1,0:T(8,128)(2,1)S(1)} %fusion.4), channel_id=1, source_target_pairs={{0,8},{1,9},{2,10},{3,11},{4,12},{5,13},{6,14},{7,15},{8,0},{9,1},... | collective-permute-start | bytes 344072 | tf_op jit(solution)/shard_map/ppermute | solution.py:385
  110.9 11.8 %collective-permute-start.18 = (bf16[128,3584]{1,0:T(8,128)(2,1)S(1)}, bf16[128,3584]{1,0:T(8,128)(2,1)S(1)}, u32[]{:S(2)}, u32[]{:S(2)}) collective-permute-start(bf16[128,3584]{1,0:T(8,128)(2,1)S(1)} %pack.23), channel_id=1, source_target_pairs={{0,1},{1,0},{2,3},{3,2},{4,5},{5,4},{6,7},{7,6},{8,9},{9,8},{10,11... | collective-permute-start | bytes 2752520 | tf_op jit(solution)/shard_map/ppermute | solution.py:385
  111.3 10.9 %collective-permute-start.20 = (bf16[48,3584]{1,0:T(8,128)(2,1)S(1)}, bf16[48,3584]{1,0:T(8,128)(2,1)S(1)}, u32[]{:S(2)}, u32[]{:S(2)}) collective-permute-start(bf16[48,3584]{1,0:T(8,128)(2,1)S(1)} %get-tuple-element.84.refs_0_), channel_id=1, source_target_pairs={{0,2},{1,3},{2,0},{3,1},{4,6},{5,7},{6,4},{7,5},{8,10},{9,11},{10,... | collective-permute-start | bytes 1032200 | tf_op jit(solution)/shard_map/ppermute | solution.py:385
  112.2 11.4 %collective-permute-start.26 = (bf16[32,3584]{1,0:T(8,128)(2,1)S(1)}, bf16[32,3584]{1,0:T(8,128)(2,1)S(1)}, u32[]{:S(2)}, u32[]{:S(2)}) collective-permute-start(bf16[32,3584]{1,0:T(8,128)(2,1)S(1)} %get-tuple-element.89.refs_2_), channel_id=1, source_target_pairs={{0,4},{1,5},{2,6},{3,7},{4,0},{5,1},{6,2},{7,3},{8,12},{9,13},{10,... | collective-permute-start | bytes 688136 | tf_op jit(solution)/shard_map/ppermute | solution.py:385
  117.3 13.8 %collective-permute-start.30 = (bf16[48,3584]{1,0:T(8,128)(2,1)S(1)}, bf16[48,3584]{1,0:T(8,128)(2,1)S(1)}, u32[]{:S(2)}, u32[]{:S(2)}) collective-permute-start(bf16[48,3584]{1,0:T(8,128)(2,1)S(1)} %get-tuple-element.88.refs_2_), channel_id=1, source_target_pairs={{0,2},{1,3},{2,0},{3,1},{4,6},{5,7},{6,4},{7,5},{8,10},{9,11},{10,... | collective-permute-start | bytes 1032200 | tf_op jit(solution)/shard_map/ppermute | solution.py:385
  123.0 22.5 %collective-permute-start.23 = (bf16[64,3584]{1,0:T(8,128)(2,1)S(1)}, bf16[64,3584]{1,0:T(8,128)(2,1)S(1)}, u32[]{:S(2)}, u32[]{:S(2)}) collective-permute-start(bf16[64,3584]{1,0:T(8,128)(2,1)S(1)} %get-tuple-element.92), channel_id=1, source_target_pairs={{0,2},{1,3},{2,0},{3,1},{4,6},{5,7},{6,4},{7,5},{8,10},{9,11},{10,... | collective-permute-start | bytes 1376264 | tf_op jit(solution)/shard_map/ppermute | solution.py:385
  (16 other events, 122.3 us)

commit v4 on v3

--- a/solution.py
+++ b/solution.py
@@ -215,59 +215,83 @@
     )(*[p for p, _, _ in pieces], *before)
 
 
-def join_kernel(later, keep, got, *refs):
-    own, crossing = refs[later:]
-    half = own.shape[0]
-    own[...] = keep[:half].astype(F32) + got[:half].astype(F32)
-    crossing[...] = (keep[half:].astype(F32) + got[half:].astype(F32)).astype(BF16)
-
-
-def join(keep, got, before=()):
+def join_kernel(parts, *refs):
+    own, crossing = refs[-2:]
+    half = own.shape[0] // parts
+    for p in range(parts):
+        keep, got = refs[2 * p], refs[2 * p + 1]
+        rows = slice(p * half, (p + 1) * half)
+        own[rows, :] = keep[:half].astype(F32) + got[:half].astype(F32)
+        crossing[rows, :] = (keep[half:].astype(F32) + got[half:].astype(F32)).astype(BF16)
+
+
+def join(keeps, gots, before=()):
     resident = pl.BlockSpec(memory_space=pltpu.VMEM)
-    rows, width = keep.shape
-    return pl.pallas_call(
-        functools.partial(join_kernel, len(before)),
-        in_specs=[resident] * (2 + len(before)),
+    rows, width = keeps[0].shape
+    parts = len(keeps)
+    pairs = [a for pair in zip(keeps, gots) for a in pair]
+    return pl.pallas_call(
+        functools.partial(join_kernel, parts),
+        in_specs=[resident] * (len(pairs) + len(before)),
         out_specs=[resident] * 2,
         out_shape=[
-            jax.ShapeDtypeStruct((rows // 2, width), F32),
-            jax.ShapeDtypeStruct((rows // 2, width), BF16),
+            jax.ShapeDtypeStruct((parts * rows // 2, width), F32),
+            jax.ShapeDtypeStruct((parts * rows // 2, width), BF16),
         ],
         compiler_params=pltpu.CompilerParams(vmem_limit_bytes=4 * 1024 * 1024),
         cost_estimate=pl.CostEstimate(flops=0, bytes_accessed=rows * 4096, transcendentals=0),
         name="join",
-    )(keep, got, *before)
-
-
-def land_kernel(parts, *refs):
+    )(*pairs, *before)
+
+
+def land_kernel(parts, own, got, *refs):
     leaving, staying = refs[-2:]
     u = staying.shape[0] // parts
     for p in range(parts):
-        own, got = refs[2 * p], refs[2 * p + 1]
-        rows = lambda k: own[k * u : (k + 1) * u].astype(F32) + got[k * u : (k + 1) * u].astype(F32)
-        leaving[2 * p * u : (2 * p + 1) * u, :] = rows(0).astype(BF16)
-        leaving[(2 * p + 1) * u : (2 * p + 2) * u, :] = rows(2).astype(BF16)
-        staying[p * u : (p + 1) * u, :] = rows(1)
-
-
-def land(owns, gots, before=()):
+        sums = []
+        for k in range(3):
+            rows = slice((3 * p + k) * u, (3 * p + k + 1) * u)
+            sums.append(own[rows].astype(F32) + got[rows].astype(F32))
+        leaving[p * u : (p + 1) * u, :] = sums[0].astype(BF16)
+        leaving[(parts + p) * u : (parts + p + 1) * u, :] = sums[2].astype(BF16)
+        staying[p * u : (p + 1) * u, :] = sums[1]
+
+
+def land(own, got, parts, before=()):
     resident = pl.BlockSpec(memory_space=pltpu.VMEM)
-    rows, width = owns[0].shape
-    parts = len(owns)
-    u = rows // 3
-    pairs = [a for pair in zip(owns, gots) for a in pair]
+    rows, width = own.shape
     return pl.pallas_call(
         functools.partial(land_kernel, parts),
-        in_specs=[resident] * (len(pairs) + len(before)),
+        in_specs=[resident] * (2 + len(before)),
         out_specs=[resident] * 2,
         out_shape=[
-            jax.ShapeDtypeStruct((2 * parts * u, width), BF16),
-            jax.ShapeDtypeStruct((parts * u, width), F32),
+            jax.ShapeDtypeStruct((2 * rows // 3, width), BF16),
+            jax.ShapeDtypeStruct((rows // 3, width), F32),
         ],
         compiler_params=pltpu.CompilerParams(vmem_limit_bytes=4 * 1024 * 1024),
         cost_estimate=pl.CostEstimate(flops=0, bytes_accessed=rows * 4096, transcendentals=0),
         name="land",
-    )(*pairs, *before)
+    )(own, got, *before)
+
+
+def pass_kernel(staying, got, *refs):
+    u = staying.shape[0]
+    refs[-1][...] = (staying[...] + got[u:].astype(F32)).astype(BF16)
+
+
+def pass_on(staying, got, before=()):
+    resident = pl.BlockSpec(memory_space=pltpu.VMEM)
+    return pl.pallas_call(
+        pass_kernel,
+        in_specs=[resident] * (2 + len(before)),
+        out_specs=resident,
+        out_shape=jax.ShapeDtypeStruct(staying.shape, BF16),
+        compiler_params=pltpu.CompilerParams(vmem_limit_bytes=4 * 1024 * 1024),
+        cost_estimate=pl.CostEstimate(
+            flops=0, bytes_accessed=staying.shape[0] * 4096, transcendentals=0
+        ),
+        name="pass_on",
+    )(staying, got, *before)
 
 
 def expert_kernel(
@@ -401,59 +425,61 @@
     one = swap(onward, 4)
     other = swap(pack([(rows, 0, n), (cross, 0, n)], unpacked), 1)
     z += [pack([(one, q * u, u), (two, q * u, u), (one, half + q * u, u)]) for q in range(2)]
-    x = [swap(v, 2) for v in z]
-    both, done, near, back = [], [], [], []
-    own, crossing, crossed = [None] * QUARTERS, [None] * QUARTERS, [None] * QUARTERS
-    leaving, staying = [None] * QUARTERS, [None] * QUARTERS
-
-    def start_core(q, before):
-        both.append(pack([(z[q], 0, 3 * u), (x[q], 0, 3 * u)], before))
-
-    def after_core(q, before):
-        own[q], crossing[q] = join(near[q][1], back[q], before)
-        crossed[q] = swap(crossing[q], 2)
-
-    def after_x(q, before):
-        leaving[q], staying[q] = land([own[q]], [crossed[q]], before)
-
-    def expert(q, before):
+    two_x = swap(pack([(cross, 3 * u, u)], unpacked), 8)
+    x = [swap(v, 2) for v in z[:3]]
+    done, near, far, sent = [], [], [], []
+
+    def expert(q, ahead, before):
+        both = pack([(z[q], 0, 3 * u), (x[q], 0, 3 * u)], done[-1:] + ahead)
         keep_near, keep_far, send_near, send_far, token = expert_block(
-            q, mine, rows, cross, other, z[q], x[q], swap(both[q], 1), perm,
+            q, mine, rows, cross, other, z[q], x[q], swap(both, 1), perm,
             w_gate, w_up, w_down, experts, before,
         )
         done.append(token)
-        near.append((keep_near, keep_far, send_near))
-        back.append(swap(send_far, 1))
-
-    start_core(0, [z[2], z[3]])
-    expert(0, [])
-    start_core(1, done[-1:])
-    start_core(2, done[-1:])
-    expert(1, [both[2]])
-    start_core(3, done[-1:])
-    after_core(0, done[-1:])
-    expert(2, [both[3], crossing[0]])
-    after_core(1, done[-1:])
-    after_x(0, done[-1:])
-    expert(3, [crossing[1], leaving[0]])
-    after_core(2, done[-1:])
-    after_core(3, [crossing[2]])
-    after_x(1, [crossing[3]])
-    after_x(2, [leaving[1]])
-
-    sends = [s for _, _, s in near]
-    kept = [k for k, _, _ in near]
+        near.append((keep_near, send_near))
+        far.append(keep_far)
+        sent.append(send_far)
+
+    def after_core(q, before):
+        own, crossing = join([far[q]], [swap(sent[q], 1)], before)
+        return own, crossing, swap(crossing, 2)
+
+    expert(0, [z[2], z[3]], [])
+    onward_x = pack([(cross, 3 * u, u), (two_x, 0, u)], done[-1:])
+    one_x = swap(onward_x, 4)
+    leaving_0, staying_0 = land(far[0], swap(sent[0], 1), 2, done[-1:])
+    expert(1, [onward_x], [leaving_0])
+    x.append(pack([(one_x, 0, u), (two_x, 0, u), (one_x, u, u)], done[-1:]))
+    own_1, crossing_1, crossed_1 = after_core(1, done[-1:])
+    expert(2, [x[3]], [crossing_1])
+    got_0 = swap(leaving_0, 4)
+    passed_0 = pass_on(staying_0, got_0, done[-1:])
+    leaving_1, staying_1 = land(own_1, crossed_1, 1, done[-1:])
+    own_2, crossing_2, crossed_2 = after_core(2, done[-1:])
+    expert(3, [passed_0, leaving_1], [crossing_2])
+    got_1 = swap(leaving_1, 4)
+    passed_1 = pass_on(staying_1, got_1, done[-1:])
+    leaving_2, staying_2 = land(own_2, crossed_2, 1, done[-1:])
+    sent[3] = pack([(sent[3], 0, 6 * u)], [passed_1, leaving_2])
+    own_3, crossing_3, crossed_3 = after_core(3, done[-1:])
+    leaving_3, staying_3 = land(own_3, crossed_3, 1)
+
+    sends = [s for _, s in near]
+    kept = [k for k, _ in near]
     send = pack([(s, 0, u) for s in sends] + [(s, u, u) for s in sends], done[-1:])
     keep = pack([(k, 0, u) for k in kept] + [(k, u, u) for k in kept], done[-1:])
-    home, away = join(keep, swap(send, 1), [leaving[2]])
-    away = swap(away, 2)
-    after_x(3, [])
-    sums = []
-    for q in range(QUARTERS):
-        got = swap(leaving[q], 4).astype(F32)
-        last = swap((staying[q] + got[u:]).astype(BF16), 8).astype(F32)
-        sums.append(got[:u] + last)
-    total = home + away.astype(F32) + jnp.concatenate(sums)
+    last_0 = swap(passed_0, 8)
+    sum_0 = got_0[: 2 * u].astype(F32) + last_0.astype(F32)
+    pair = keep.astype(F32) + swap(send, 1).astype(F32)
+    away = jnp.concatenate([pair[n : n + u] + sum_0[u:], pair[n + u :]]).astype(BF16)
+    over = [swap(away[:half], 2), swap(away[half:], 2)]
+    got_2, got_3 = swap(leaving_2, 4), swap(leaving_3, 4)
+    passed_2 = pass_on(staying_2, got_2, [crossing_3])
+    passed_3 = pass_on(staying_3, got_3, [over[0]])
+    sums = [sum_0[:u]]
+    for got, passed in ((got_1, passed_1), (got_2, passed_2), (got_3, passed_3)):
+        sums.append(got[:u].astype(F32) + swap(passed, 8).astype(F32))
+    total = pair[:n] + jnp.concatenate(over).astype(F32) + jnp.concatenate(sums)
     return total.astype(BF16)
 
 

time: 147 us -> 130 us (0.88)
  waiting for transfers between devices: 54.7 us -> 37.5 us
  local copies, waits for them, and re-layouts: 5.94 us -> 4.32 us
    ppermute x33 -> x34, waiting for transfers between devices: 54.7 us -> 37.5 us  [swap(): return lax.ppermute(value, 'ep', [(i, i ^ bits) for i in range(experts)])]
    unnamed x16, local copies, waits for them, and re-layouts: 5.91 us -> 4.24 us
    ppermute x33 -> x34, starting transfers between devices: 35.8 us -> 36.9 us  [swap(): return lax.ppermute(value, 'ep', [(i, i ^ bits) for i in range(experts)])]
  transfers between devices with their start and end apart: 33 -> 34, of which waited for: 14 -> 15; matrix products, arithmetic and copies ran while one was open for 0% -> 0% of each run, Pallas kernels for 32% -> 37%
where the time goes in v4:
time: 130 us; the launch traced here: 129 us
  Pallas kernels  48.8 us (38%)
  waiting for transfers between devices  37.5 us (29%)
  starting transfers between devices  36.9 us (28%)
  local copies, waits for them, and re-layouts  4.32 us (3%)
  other arithmetic  1.41 us (1%)
    ppermute x34, waiting for transfers between devices, swap(): return lax.ppermute(value, 'ep', [(i, i ^ bits) for i in range(experts)])  37.5 us
    ppermute x34, starting transfers between devices, swap(): return lax.ppermute(value, 'ep', [(i, i ^ bits) for i in range(experts)])  36.9 us
    pallas_call x4, Pallas kernels, expert_block(): pl.pallas_call(functools.partial(expert_kernel, experts, quarter, first,...  32.1 us
    pallas_call x3, Pallas kernels, unpack(): pl.pallas_call(functools.partial(unpack_kernel, len(before)), grid=(steps...  14.2 us
    unnamed x16, local copies, waits for them, and re-layouts  4.24 us
  transfers between devices with their start and end apart: 34, of which 15 were waited for; matrix products, arithmetic and copies ran while one was open for 0% of the time, Pallas kernels for 37%

profile of v4, /device:TPU:0, one launch (start us, length us, event | category | flops | bytes accessed | tf_op | source)
XLA Modules:
  0.0 129.4 jit_solution(6141267400835256387)
XLA Ops:
  3.5 4.1 %collective-permute-start.5 = (bf16[32,3712]{1,0:T(8,128)(2,1)S(1)}, bf16[32,3712]{1,0:T(8,128)(2,1)S(1)}, u32[]{:S(2)}, u32[]{:S(2)}) collective-permute-start(bf16[32,3712]{1,0:T(8,128)(2,1)S(1)} %get-tuple-element.93), channel_id=1, source_target_pairs={{0,8},{1,9},{2,10},{3,11},{4,12},{5,13},{6,14},{7,15},{8,0},{9,1},... | collective-permute-start | bytes 712712 | tf_op jit(solution)/shard_map/ppermute | solution.py:409
  9.1 1.6 %collective-permute-start.2 = (bf16[32,3712]{1,0:T(8,128)(2,1)S(1)}, bf16[32,3712]{1,0:T(8,128)(2,1)S(1)}, u32[]{:S(2)}, u32[]{:S(2)}) collective-permute-start(bf16[32,3712]{1,0:T(8,128)(2,1)S(1)} %get-tuple-element.94), channel_id=1, source_target_pairs={{0,4},{1,5},{2,6},{3,7},{4,0},{5,1},{6,2},{7,3},{8,12},{9,13},{10,... | collective-permute-start | bytes 712712 | tf_op jit(solution)/shard_map/ppermute | solution.py:409
  11.0 2.5 %collective-permute-start.4 = (bf16[32,3712]{1,0:T(8,128)(2,1)S(1)}, bf16[32,3712]{1,0:T(8,128)(2,1)S(1)}, u32[]{:S(2)}, u32[]{:S(2)}) collective-permute-start(bf16[32,3712]{1,0:T(8,128)(2,1)S(1)} %get-tuple-element.94), channel_id=1, source_target_pairs={{0,12},{1,13},{2,14},{3,15},{4,8},{5,9},{6,10},{7,11},{8,4},{9,5},... | collective-permute-start | bytes 712712 | tf_op jit(solution)/shard_map/ppermute | solution.py:409
  15.1 5.4 %unpack.3 = (bf16[2,1024,1792]{2,1,0:T(8,128)(2,1)S(1)}, f32[8,128]{1,0:T(8,128)S(1)}) custom-call(f32[256,3584]{1,0:T(8,128)} %bitcast.16, bf16[8,3584]{1,0:T(8,128)(2,1)S(1)} %bitcast.14, bf16[8,3584]{1,0:T(8,128)(2,1)S(1)} %bitcast.15), custom_call_target="tpu_custom_call" | custom-call | flops 22020096 | bytes 3670016 | tf_op jit(solution)/shard_map/unpack/pallas_call | solution.py:172
  20.6 4.4 %unpack.4 = (bf16[2,3584,512]{2,1,0:T(8,128)(2,1)S(1)}, f32[8,128]{1,0:T(8,128)S(1)}) custom-call(f32[896,1024]{1,0:T(8,128)} %bitcast.17, bf16[28,1024]{1,0:T(8,128)(2,1)S(1)} %bitcast.10, bf16[28,1024]{1,0:T(8,128)(2,1)S(1)} %bitcast.11), custom_call_target="tpu_custom_call" | custom-call | flops 22020096 | bytes 3670016 | tf_op jit(solution)/shard_map/unpack/pallas_call | solution.py:172
  25.0 4.4 %unpack.5 = (bf16[2,3584,512]{2,1,0:T(8,128)(2,1)S(1)}, f32[8,128]{1,0:T(8,128)S(1)}) custom-call(f32[896,1024]{1,0:T(8,128)} %bitcast.18, bf16[28,1024]{1,0:T(8,128)(2,1)S(1)} %bitcast.12, bf16[28,1024]{1,0:T(8,128)(2,1)S(1)} %bitcast.13), custom_call_target="tpu_custom_call" | custom-call | flops 22020096 | bytes 3670016 | tf_op jit(solution)/shard_map/unpack/pallas_call | solution.py:172
  30.1 4.5 %collective-permute-done.3.refs_1_ = bf16[32,3712]{1,0:T(8,128)(2,1)S(1)} collective-permute-done((bf16[32,3712]{1,0:T(8,128)(2,1)S(1)}, bf16[32,3712]{1,0:T(8,128)(2,1)S(1)}, u32[]{:S(2)}, u32[]{:S(2)}) %collective-permute-start.3) | collective-permute-done | bytes 237600 | tf_op jit(solution)/shard_map/ppermute | solution.py:409
  34.7 1.9 %collective-permute-start.6 = (bf16[48,3712]{1,0:T(8,128)(2,1)S(1)}, bf16[48,3712]{1,0:T(8,128)(2,1)S(1)}, u32[]{:S(2)}, u32[]{:S(2)}) collective-permute-start(bf16[48,3712]{1,0:T(8,128)(2,1)S(1)} %pack.17.refs_0_.z), channel_id=1, source_target_pairs={{0,2},{1,3},{2,0},{3,1},{4,6},{5,7},{6,4},{7,5},{8,10},{9,11},{10,... | collective-permute-start | bytes 1069064 | tf_op jit(solution)/shard_map/ppermute | solution.py:409
  36.7 7.2 %collective-permute-done.7.refs_0_.refs_2_ = bf16[64,3712]{1,0:T(8,128)(2,1)S(1)} collective-permute-done((bf16[64,3712]{1,0:T(8,128)(2,1)S(1)}, bf16[64,3712]{1,0:T(8,128)(2,1)S(1)}, u32[]{:S(2)}, u32[]{:S(2)}) %collective-permute-start.7) | collective-permute-done | bytes 475168 | tf_op jit(solution)/shard_map/ppermute | solution.py:409
  44.2 1.6 %collective-permute-start.9 = (bf16[48,3712]{1,0:T(8,128)(2,1)S(1)}, bf16[48,3712]{1,0:T(8,128)(2,1)S(1)}, u32[]{:S(2)}, u32[]{:S(2)}) collective-permute-start(bf16[48,3712]{1,0:T(8,128)(2,1)S(1)} %pack.22.refs_0_.z), channel_id=1, source_target_pairs={{0,2},{1,3},{2,0},{3,1},{4,6},{5,7},{6,4},{7,5},{8,10},{9,11},{10,... | collective-permute-start | bytes 1069064 | tf_op jit(solution)/shard_map/ppermute | solution.py:409
  45.8 7.8 %collective-permute-start.10 = (bf16[16,3712]{1,0:T(8,128)(2,1)S(1)}, bf16[16,3712]{1,0:T(8,128)(2,1)S(1)}, u32[]{:S(2)}, u32[]{:S(2)}) collective-permute-start(bf16[16,3712]{1,0:T(8,128)(2,1)S(1)} %pack.23), channel_id=1, source_target_pairs={{0,8},{1,9},{2,10},{3,11},{4,12},{5,13},{6,14},{7,15},{8,0},{9,1},... | collective-permute-start | bytes 356360 | tf_op jit(solution)/shard_map/ppermute | solution.py:409
  53.7 8.0 %expert_block.4 = (bf16[32,3584]{1,0:T(8,128)(2,1)S(1)}, bf16[96,3584]{1,0:T(8,128)(2,1)S(1)}, bf16[32,3584]{1,0:T(8,128)(2,1)S(1)}, bf16[96,3584]{1,0:T(8,128)(2,1)S(1)}, f32[8,128]{1,0:T(8,128)S(1)}) custom-call(s32[1]{0:T(128)} %get-tuple-element.48.mine, bf16[64,3712]{1,0:T(8,128)(2,1)S(1)} %get-tuple-element.49.refs_0_.near, ...), custom_call_target="tpu_custom_call" | custom-call | flops 5637144576 | bytes 3670016 | tf_op jit(solution)/shard_map/expert_block/pallas_call | solution.py:365
  63.0 2.0 %collective-permute-done.12.got = bf16[96,3584]{1,0:T(8,128)(2,1)S(1)} collective-permute-done((bf16[96,3584]{1,0:T(8,128)(2,1)S(1)}, bf16[96,3584]{1,0:T(8,128)(2,1)S(1)}, u32[]{:S(2)}, u32[]{:S(2)}) %collective-permute-start.12) | collective-permute-done | bytes 688160 | tf_op jit(solution)/shard_map/ppermute | solution.py:409
  65.2 8.0 %expert_block.5 = (bf16[32,3584]{1,0:T(8,128)(2,1)S(1)}, bf16[96,3584]{1,0:T(8,128)(2,1)S(1)}, bf16[32,3584]{1,0:T(8,128)(2,1)S(1)}, bf16[96,3584]{1,0:T(8,128)(2,1)S(1)}, f32[8,128]{1,0:T(8,128)S(1)}) custom-call(s32[1]{0:T(128)} %get-tuple-element.48.mine, bf16[64,3712]{1,0:T(8,128)(2,1)S(1)} %get-tuple-element.49.refs_0_.near, ...), custom_call_target="tpu_custom_call" | custom-call | flops 5637144576 | bytes 3670016 | tf_op jit(solution)/shard_map/expert_block/pallas_call | solution.py:365
  73.9 2.6 %collective-permute-done.16.refs_1_ = bf16[96,3584]{1,0:T(8,128)(2,1)S(1)} collective-permute-done((bf16[96,3584]{1,0:T(8,128)(2,1)S(1)}, bf16[96,3584]{1,0:T(8,128)(2,1)S(1)}, u32[]{:S(2)}, u32[]{:S(2)}) %collective-permute-start.16) | collective-permute-done | bytes 688160 | tf_op jit(solution)/shard_map/ppermute | solution.py:409
  77.3 8.2 %expert_block.6 = (bf16[32,3584]{1,0:T(8,128)(2,1)S(1)}, bf16[96,3584]{1,0:T(8,128)(2,1)S(1)}, bf16[32,3584]{1,0:T(8,128)(2,1)S(1)}, bf16[96,3584]{1,0:T(8,128)(2,1)S(1)}, f32[8,128]{1,0:T(8,128)S(1)}) custom-call(s32[1]{0:T(128)} %get-tuple-element.48.mine, bf16[64,3712]{1,0:T(8,128)(2,1)S(1)} %get-tuple-element.49.refs_0_.near, ...), custom_call_target="tpu_custom_call" | custom-call | flops 5637144576 | bytes 3670016 | tf_op jit(solution)/shard_map/expert_block/pallas_call | solution.py:365
  91.0 8.0 %expert_block.7 = (bf16[32,3584]{1,0:T(8,128)(2,1)S(1)}, bf16[96,3584]{1,0:T(8,128)(2,1)S(1)}, bf16[32,3584]{1,0:T(8,128)(2,1)S(1)}, bf16[96,3584]{1,0:T(8,128)(2,1)S(1)}, f32[8,128]{1,0:T(8,128)S(1)}) custom-call(s32[1]{0:T(128)} %get-tuple-element.48.mine, bf16[64,3712]{1,0:T(8,128)(2,1)S(1)} %get-tuple-element.49.refs_0_.near, ...), custom_call_target="tpu_custom_call" | custom-call | flops 5637144576 | bytes 3670016 | tf_op jit(solution)/shard_map/expert_block/pallas_call | solution.py:365
  101.8 1.8 %collective-permute-start.26 = (bf16[16,3584]{1,0:T(8,128)(2,1)S(1)}, bf16[16,3584]{1,0:T(8,128)(2,1)S(1)}, u32[]{:S(2)}, u32[]{:S(2)}) collective-permute-start(bf16[16,3584]{1,0:T(8,128)(2,1)S(1)} %pass_on.5.refs_1_), channel_id=1, source_target_pairs={{0,8},{1,9},{2,10},{3,11},{4,12},{5,13},{6,14},{7,15},{8,0},{9,1},... | collective-permute-start | bytes 344072 | tf_op jit(solution)/shard_map/ppermute | solution.py:409
  104.6 5.4 %collective-permute-done.28.got = bf16[32,3584]{1,0:T(8,128)(2,1)S(1)} collective-permute-done((bf16[32,3584]{1,0:T(8,128)(2,1)S(1)}, bf16[32,3584]{1,0:T(8,128)(2,1)S(1)}, u32[]{:S(2)}, u32[]{:S(2)}) %collective-permute-start.28) | collective-permute-done | bytes 229408 | tf_op jit(solution)/shard_map/ppermute | solution.py:409
  110.5 1.9 %collective-permute-start.23 = (bf16[32,3584]{1,0:T(8,128)(2,1)S(1)}, bf16[32,3584]{1,0:T(8,128)(2,1)S(1)}, u32[]{:S(2)}, u32[]{:S(2)}) collective-permute-start(bf16[32,3584]{1,0:T(8,128)(2,1)S(1)} %pad_maximum_fusion), channel_id=1, source_target_pairs={{0,2},{1,3},{2,0},{3,1},{4,6},{5,7},{6,4},{7,5},{8,10},{9,11},{10,... | collective-permute-start | bytes 688136 | tf_op jit(solution)/shard_map/ppermute | solution.py:409
  112.4 2.4 %collective-permute-done.31.got = bf16[48,3584]{1,0:T(8,128)(2,1)S(1)} collective-permute-done((bf16[48,3584]{1,0:T(8,128)(2,1)S(1)}, bf16[48,3584]{1,0:T(8,128)(2,1)S(1)}, u32[]{:S(2)}, u32[]{:S(2)}) %collective-permute-start.31) | collective-permute-done | bytes 344096 | tf_op jit(solution)/shard_map/ppermute | solution.py:409
  116.3 2.2 %collective-permute-done.23.refs_0_ = bf16[32,3584]{1,0:T(8,128)(2,1)S(1)} collective-permute-done((bf16[32,3584]{1,0:T(8,128)(2,1)S(1)}, bf16[32,3584]{1,0:T(8,128)(2,1)S(1)}, u32[]{:S(2)}, u32[]{:S(2)}) %collective-permute-start.23) | collective-permute-done | bytes 229408 | tf_op jit(solution)/shard_map/ppermute | solution.py:409
  118.5 2.5 %collective-permute-done.32.got = bf16[32,3584]{1,0:T(8,128)(2,1)S(1)} collective-permute-done((bf16[32,3584]{1,0:T(8,128)(2,1)S(1)}, bf16[32,3584]{1,0:T(8,128)(2,1)S(1)}, u32[]{:S(2)}, u32[]{:S(2)}) %collective-permute-start.32) | collective-permute-done | bytes 229408 | tf_op jit(solution)/shard_map/ppermute | solution.py:409
  123.6 4.4 %collective-permute-done.33 = bf16[16,3584]{1,0:T(8,128)(2,1)S(1)} collective-permute-done((bf16[16,3584]{1,0:T(8,128)(2,1)S(1)}, bf16[16,3584]{1,0:T(8,128)(2,1)S(1)}, u32[]{:S(2)}, u32[]{:S(2)}) %collective-permute-start.33) | collective-permute-done | bytes 114720 | tf_op jit(solution)/shard_map/ppermute | solution.py:409
  (106 shorter events, 26.2 us)
Async XLA Ops:
  3.5 25.9 %collective-permute-start.5 = (bf16[32,3712]{1,0:T(8,128)(2,1)S(1)}, bf16[32,3712]{1,0:T(8,128)(2,1)S(1)}, u32[]{:S(2)}, u32[]{:S(2)}) collective-permute-start(bf16[32,3712]{1,0:T(8,128)(2,1)S(1)} %get-tuple-element.93), channel_id=1, source_target_pairs={{0,8},{1,9},{2,10},{3,11},{4,12},{5,13},{6,14},{7,15},{8,0},{9,1},... | collective-permute-start | bytes 712712 | tf_op jit(solution)/shard_map/ppermute | solution.py:409
  7.6 29.0 %collective-permute-start = (bf16[64,3712]{1,0:T(8,128)(2,1)S(1)}, bf16[64,3712]{1,0:T(8,128)(2,1)S(1)}, u32[]{:S(2)}, u32[]{:S(2)}) collective-permute-start(bf16[64,3712]{1,0:T(8,128)(2,1)S(1)} %get-tuple-element.49.refs_0_.near), channel_id=1, source_target_pairs={{0,2},{1,3},{2,0},{3,1},{4,6},{5,7},{6,4},{7,5},{8,10},{9,11},{10,... | collective-permute-start | bytes 1425416 | tf_op jit(solution)/shard_map/ppermute | solution.py:409
  9.1 21.1 %collective-permute-start.2 = (bf16[32,3712]{1,0:T(8,128)(2,1)S(1)}, bf16[32,3712]{1,0:T(8,128)(2,1)S(1)}, u32[]{:S(2)}, u32[]{:S(2)}) collective-permute-start(bf16[32,3712]{1,0:T(8,128)(2,1)S(1)} %get-tuple-element.94), channel_id=1, source_target_pairs={{0,4},{1,5},{2,6},{3,7},{4,0},{5,1},{6,2},{7,3},{8,12},{9,13},{10,... | collective-permute-start | bytes 712712 | tf_op jit(solution)/shard_map/ppermute | solution.py:409
  10.7 24.0 %collective-permute-start.3 = (bf16[32,3712]{1,0:T(8,128)(2,1)S(1)}, bf16[32,3712]{1,0:T(8,128)(2,1)S(1)}, u32[]{:S(2)}, u32[]{:S(2)}) collective-permute-start(bf16[32,3712]{1,0:T(8,128)(2,1)S(1)} %get-tuple-element.94), channel_id=1, source_target_pairs={{0,8},{1,9},{2,10},{3,11},{4,12},{5,13},{6,14},{7,15},{8,0},{9,1},... | collective-permute-start | bytes 712712 | tf_op jit(solution)/shard_map/ppermute | solution.py:409
  11.0 23.7 %collective-permute-start.4 = (bf16[32,3712]{1,0:T(8,128)(2,1)S(1)}, bf16[32,3712]{1,0:T(8,128)(2,1)S(1)}, u32[]{:S(2)}, u32[]{:S(2)}) collective-permute-start(bf16[32,3712]{1,0:T(8,128)(2,1)S(1)} %get-tuple-element.94), channel_id=1, source_target_pairs={{0,12},{1,13},{2,14},{3,15},{4,8},{5,9},{6,10},{7,11},{8,4},{9,5},... | collective-permute-start | bytes 712712 | tf_op jit(solution)/shard_map/ppermute | solution.py:409
  29.4 14.6 %collective-permute-start.7 = (bf16[64,3712]{1,0:T(8,128)(2,1)S(1)}, bf16[64,3712]{1,0:T(8,128)(2,1)S(1)}, u32[]{:S(2)}, u32[]{:S(2)}) collective-permute-start(bf16[64,3712]{1,0:T(8,128)(2,1)S(1)} %pack.18), channel_id=1, source_target_pairs={{0,4},{1,5},{2,6},{3,7},{4,0},{5,1},{6,2},{7,3},{8,12},{9,13},{10,... | collective-permute-start | bytes 1425416 | tf_op jit(solution)/shard_map/ppermute | solution.py:409
  34.7 9.3 %collective-permute-start.6 = (bf16[48,3712]{1,0:T(8,128)(2,1)S(1)}, bf16[48,3712]{1,0:T(8,128)(2,1)S(1)}, u32[]{:S(2)}, u32[]{:S(2)}) collective-permute-start(bf16[48,3712]{1,0:T(8,128)(2,1)S(1)} %pack.17.refs_0_.z), channel_id=1, source_target_pairs={{0,2},{1,3},{2,0},{3,1},{4,6},{5,7},{6,4},{7,5},{8,10},{9,11},{10,... | collective-permute-start | bytes 1069064 | tf_op jit(solution)/shard_map/ppermute | solution.py:409
  36.7 17.0 %collective-permute-start.1 = (bf16[128,3712]{1,0:T(8,128)(2,1)S(1)}, bf16[128,3712]{1,0:T(8,128)(2,1)S(1)}, u32[]{:S(2)}, u32[]{:S(2)}) collective-permute-start(bf16[128,3712]{1,0:T(8,128)(2,1)S(1)} %pack.16), channel_id=1, source_target_pairs={{0,1},{1,0},{2,3},{3,2},{4,5},{5,4},{6,7},{7,6},{8,9},{9,8},{10,11... | collective-permute-start | bytes 2850824 | tf_op jit(solution)/shard_map/ppermute | solution.py:409
  44.1 9.6 %collective-permute-start.8 = (bf16[96,3712]{1,0:T(8,128)(2,1)S(1)}, bf16[96,3712]{1,0:T(8,128)(2,1)S(1)}, u32[]{:S(2)}, u32[]{:S(2)}) collective-permute-start(bf16[96,3712]{1,0:T(8,128)(2,1)S(1)} %pack.21), channel_id=1, source_target_pairs={{0,1},{1,0},{2,3},{3,2},{4,5},{5,4},{6,7},{7,6},{8,9},{9,8},{10,11... | collective-permute-start | bytes 2138120 | tf_op jit(solution)/shard_map/ppermute | solution.py:409
  44.2 17.5 %collective-permute-start.9 = (bf16[48,3712]{1,0:T(8,128)(2,1)S(1)}, bf16[48,3712]{1,0:T(8,128)(2,1)S(1)}, u32[]{:S(2)}, u32[]{:S(2)}) collective-permute-start(bf16[48,3712]{1,0:T(8,128)(2,1)S(1)} %pack.22.refs_0_.z), channel_id=1, source_target_pairs={{0,2},{1,3},{2,0},{3,1},{4,6},{5,7},{6,4},{7,5},{8,10},{9,11},{10,... | collective-permute-start | bytes 1069064 | tf_op jit(solution)/shard_map/ppermute | solution.py:409
  45.8 15.8 %collective-permute-start.10 = (bf16[16,3712]{1,0:T(8,128)(2,1)S(1)}, bf16[16,3712]{1,0:T(8,128)(2,1)S(1)}, u32[]{:S(2)}, u32[]{:S(2)}) collective-permute-start(bf16[16,3712]{1,0:T(8,128)(2,1)S(1)} %pack.23), channel_id=1, source_target_pairs={{0,8},{1,9},{2,10},{3,11},{4,12},{5,13},{6,14},{7,15},{8,0},{9,1},... | collective-permute-start | bytes 356360 | tf_op jit(solution)/shard_map/ppermute | solution.py:409
  62.3 10.9 %collective-permute-start.13 = (bf16[48,3712]{1,0:T(8,128)(2,1)S(1)}, bf16[48,3712]{1,0:T(8,128)(2,1)S(1)}, u32[]{:S(2)}, u32[]{:S(2)}) collective-permute-start(bf16[48,3712]{1,0:T(8,128)(2,1)S(1)} %pack.19.refs_2_.refs_0_.z), channel_id=1, source_target_pairs={{0,2},{1,3},{2,0},{3,1},{4,6},{5,7},{6,4},{7,5},{8,10},{9,11},{10,... | collective-permute-start | bytes 1069064 | tf_op jit(solution)/shard_map/ppermute | solution.py:409
  62.9 10.3 %collective-permute-start.14 = (bf16[32,3712]{1,0:T(8,128)(2,1)S(1)}, bf16[32,3712]{1,0:T(8,128)(2,1)S(1)}, u32[]{:S(2)}, u32[]{:S(2)}) collective-permute-start(bf16[32,3712]{1,0:T(8,128)(2,1)S(1)} %pack.24.refs_3_), channel_id=1, source_target_pairs={{0,4},{1,5},{2,6},{3,7},{4,0},{5,1},{6,2},{7,3},{8,12},{9,13},{10,... | collective-permute-start | bytes 712712 | tf_op jit(solution)/shard_map/ppermute | solution.py:409
  73.9 12.6 %collective-permute-start.17 = (bf16[64,3584]{1,0:T(8,128)(2,1)S(1)}, bf16[64,3584]{1,0:T(8,128)(2,1)S(1)}, u32[]{:S(2)}, u32[]{:S(2)}) collective-permute-start(bf16[64,3584]{1,0:T(8,128)(2,1)S(1)} %get-tuple-element.61.refs_0_), channel_id=1, source_target_pairs={{0,4},{1,5},{2,6},{3,7},{4,0},{5,1},{6,2},{7,3},{8,12},{9,13},{10,... | collective-permute-start | bytes 1376264 | tf_op jit(solution)/shard_map/ppermute | solution.py:409
  76.7 10.2 %collective-permute-start.18 = (bf16[48,3584]{1,0:T(8,128)(2,1)S(1)}, bf16[48,3584]{1,0:T(8,128)(2,1)S(1)}, u32[]{:S(2)}, u32[]{:S(2)}) collective-permute-start(bf16[48,3584]{1,0:T(8,128)(2,1)S(1)} %get-tuple-element.66.refs_0_), channel_id=1, source_target_pairs={{0,2},{1,3},{2,0},{3,1},{4,6},{5,7},{6,4},{7,5},{8,10},{9,11},{10,... | collective-permute-start | bytes 1032200 | tf_op jit(solution)/shard_map/ppermute | solution.py:409
  87.6 14.2 %collective-permute-start.22 = (bf16[32,3584]{1,0:T(8,128)(2,1)S(1)}, bf16[32,3584]{1,0:T(8,128)(2,1)S(1)}, u32[]{:S(2)}, u32[]{:S(2)}) collective-permute-start(bf16[32,3584]{1,0:T(8,128)(2,1)S(1)} %pass_on.4.refs_3_), channel_id=1, source_target_pairs={{0,8},{1,9},{2,10},{3,11},{4,12},{5,13},{6,14},{7,15},{8,0},{9,1},... | collective-permute-start | bytes 688136 | tf_op jit(solution)/shard_map/ppermute | solution.py:409
  88.7 12.2 %collective-permute-start.25 = (bf16[32,3584]{1,0:T(8,128)(2,1)S(1)}, bf16[32,3584]{1,0:T(8,128)(2,1)S(1)}, u32[]{:S(2)}, u32[]{:S(2)}) collective-permute-start(bf16[32,3584]{1,0:T(8,128)(2,1)S(1)} %get-tuple-element.71.refs_4_), channel_id=1, source_target_pairs={{0,4},{1,5},{2,6},{3,7},{4,0},{5,1},{6,2},{7,3},{8,12},{9,13},{10,... | collective-permute-start | bytes 688136 | tf_op jit(solution)/shard_map/ppermute | solution.py:409
  90.4 10.2 %collective-permute-start.27 = (bf16[48,3584]{1,0:T(8,128)(2,1)S(1)}, bf16[48,3584]{1,0:T(8,128)(2,1)S(1)}, u32[]{:S(2)}, u32[]{:S(2)}) collective-permute-start(bf16[48,3584]{1,0:T(8,128)(2,1)S(1)} %get-tuple-element.74.refs_0_), channel_id=1, source_target_pairs={{0,2},{1,3},{2,0},{3,1},{4,6},{5,7},{6,4},{7,5},{8,10},{9,11},{10,... | collective-permute-start | bytes 1032200 | tf_op jit(solution)/shard_map/ppermute | solution.py:409
  100.6 9.3 %collective-permute-start.28 = (bf16[32,3584]{1,0:T(8,128)(2,1)S(1)}, bf16[32,3584]{1,0:T(8,128)(2,1)S(1)}, u32[]{:S(2)}, u32[]{:S(2)}) collective-permute-start(bf16[32,3584]{1,0:T(8,128)(2,1)S(1)} %get-tuple-element.83.refs_2_), channel_id=1, source_target_pairs={{0,4},{1,5},{2,6},{3,7},{4,0},{5,1},{6,2},{7,3},{8,12},{9,13},{10,... | collective-permute-start | bytes 688136 | tf_op jit(solution)/shard_map/ppermute | solution.py:409
  101.2 8.9 %collective-permute-start.21 = (bf16[128,3584]{1,0:T(8,128)(2,1)S(1)}, bf16[128,3584]{1,0:T(8,128)(2,1)S(1)}, u32[]{:S(2)}, u32[]{:S(2)}) collective-permute-start(bf16[128,3584]{1,0:T(8,128)(2,1)S(1)} %pack.30), channel_id=1, source_target_pairs={{0,1},{1,0},{2,3},{3,2},{4,5},{5,4},{6,7},{7,6},{8,9},{9,8},{10,11... | collective-permute-start | bytes 2752520 | tf_op jit(solution)/shard_map/ppermute | solution.py:409
  101.8 14.5 %collective-permute-start.26 = (bf16[16,3584]{1,0:T(8,128)(2,1)S(1)}, bf16[16,3584]{1,0:T(8,128)(2,1)S(1)}, u32[]{:S(2)}, u32[]{:S(2)}) collective-permute-start(bf16[16,3584]{1,0:T(8,128)(2,1)S(1)} %pass_on.5.refs_1_), channel_id=1, source_target_pairs={{0,8},{1,9},{2,10},{3,11},{4,12},{5,13},{6,14},{7,15},{8,0},{9,1},... | collective-permute-start | bytes 344072 | tf_op jit(solution)/shard_map/ppermute | solution.py:409
  103.8 11.0 %collective-permute-start.31 = (bf16[48,3584]{1,0:T(8,128)(2,1)S(1)}, bf16[48,3584]{1,0:T(8,128)(2,1)S(1)}, u32[]{:S(2)}, u32[]{:S(2)}) collective-permute-start(bf16[48,3584]{1,0:T(8,128)(2,1)S(1)} %get-tuple-element.87.refs_0_), channel_id=1, source_target_pairs={{0,2},{1,3},{2,0},{3,1},{4,6},{5,7},{6,4},{7,5},{8,10},{9,11},{10,... | collective-permute-start | bytes 1032200 | tf_op jit(solution)/shard_map/ppermute | solution.py:409
  110.0 12.3 %collective-permute-start.30 = (bf16[16,3584]{1,0:T(8,128)(2,1)S(1)}, bf16[16,3584]{1,0:T(8,128)(2,1)S(1)}, u32[]{:S(2)}, u32[]{:S(2)}) collective-permute-start(bf16[16,3584]{1,0:T(8,128)(2,1)S(1)} %pass_on.6), channel_id=1, source_target_pairs={{0,8},{1,9},{2,10},{3,11},{4,12},{5,13},{6,14},{7,15},{8,0},{9,1},... | collective-permute-start | bytes 344072 | tf_op jit(solution)/shard_map/ppermute | solution.py:409
  110.5 8.0 %collective-permute-start.23 = (bf16[32,3584]{1,0:T(8,128)(2,1)S(1)}, bf16[32,3584]{1,0:T(8,128)(2,1)S(1)}, u32[]{:S(2)}, u32[]{:S(2)}) collective-permute-start(bf16[32,3584]{1,0:T(8,128)(2,1)S(1)} %pad_maximum_fusion), channel_id=1, source_target_pairs={{0,2},{1,3},{2,0},{3,1},{4,6},{5,7},{6,4},{7,5},{8,10},{9,11},{10,... | collective-permute-start | bytes 688136 | tf_op jit(solution)/shard_map/ppermute | solution.py:409
  (17 other events, 103.5 us)

commit v5 on v4

--- a/solution.py
+++ b/solution.py
@@ -87,28 +87,43 @@
     return combined.astype(jnp.bfloat16)
 
 
-def prepare_kernel(experts, mine, tokens, scores, ids, rows, perm, index):
+def prepare_kernel(
+    experts, mine, all_tokens, all_scores, all_ids, rows, perm, index, tokens, scores, ids, arrived
+):
     index[0] = mine[0]
+    fetches = [
+        pltpu.make_async_copy(source, held, arrived.at[i])
+        for i, (source, held) in enumerate(
+            ((all_tokens, tokens), (all_scores, scores), (all_ids, ids))
+        )
+    ]
+    for fetch in fetches:
+        fetch.start()
     source = lax.broadcasted_iota(jnp.int32, (CHUNK, CHUNK), 0)
     place = lax.broadcasted_iota(jnp.int32, (CHUNK, CHUNK), 1)
     perm[...] = jnp.where((source & 3) * GROUP + (source >> 2) == place, 1.0, 0.0).astype(BF16)
     width = tokens.shape[1]
+    for fetch in fetches:
+        fetch.wait()
     for at in range(0, width, CHUNK):
         rows[:, at : at + CHUNK] = jnp.dot(
             tokens[:, at : at + CHUNK], perm[...], preferred_element_type=F32
         ).astype(BF16)
-    weights = route_scale * scores[...] / jnp.sum(scores[...], axis=1, keepdims=True)
-    lane = lax.broadcasted_iota(jnp.int32, (tokens.shape[0], EXTRA), 1)
-    spread = jnp.zeros((tokens.shape[0], EXTRA), F32)
-    for k in range(ids.shape[1]):
-        spread += jnp.where(lane % experts == ids[:, k : k + 1], weights[:, k : k + 1], 0.0)
+    weights = route_scale * scores[...] / jnp.sum(scores[...], axis=0, keepdims=True)
+    n = tokens.shape[0]
+    lane = lax.broadcasted_iota(jnp.int32, (EXTRA, n), 0)
+    spread = jnp.zeros((EXTRA, n), F32)
+    for k in range(ids.shape[0]):
+        spread += jnp.where(lane % experts == ids[k : k + 1, :], weights[k : k + 1, :], 0.0)
     high = spread.astype(BF16).astype(F32)
     mid = (spread - high).astype(BF16).astype(F32)
     low = spread - high - mid
     part = lane // experts
-    rows[:, width:] = jnp.where(
+    spread = jnp.where(
         part == 0, high, jnp.where(part == 1, mid, jnp.where(part == 2, low, 0.0))
-    ).astype(BF16)
+    )
+    square = jnp.concatenate([spread, jnp.zeros((EXTRA, EXTRA - n), F32)], axis=1)
+    rows[:, width:] = square.T[:n].astype(BF16)
 
 
 def prepare(mine, tokens, scores, ids, experts):
@@ -121,11 +136,17 @@
             jax.ShapeDtypeStruct((CHUNK, CHUNK), BF16),
             jax.ShapeDtypeStruct((1,), jnp.int32),
         ),
-        in_specs=[smem, vmem, vmem, vmem],
+        in_specs=[smem] + [pl.BlockSpec(memory_space=pl.ANY)] * 3,
         out_specs=(vmem, vmem, smem),
-        compiler_params=pltpu.CompilerParams(vmem_limit_bytes=12 * 1024 * 1024),
+        scratch_shapes=[
+            pltpu.VMEM(tokens.shape, BF16),
+            pltpu.VMEM(scores.shape[::-1], F32),
+            pltpu.VMEM(ids.shape[::-1], jnp.int32),
+            pltpu.SemaphoreType.DMA((3,)),
+        ],
+        compiler_params=pltpu.CompilerParams(vmem_limit_bytes=8 * 1024 * 1024),
         name="prepare",
-    )(mine, tokens, scores, ids)
+    )(mine, *[pltpu.with_memory_space_constraint(a, pltpu.HBM) for a in (tokens, scores.T, ids.T)])
 
 
 def unpack_kernel(later, words, scale, zero, *refs):
@@ -295,61 +316,48 @@
 
 
 def expert_kernel(
-    experts, quarter, first, later, mine, near, cross, other, z, x, c, perm, wg, wu, wd, *refs
+    experts, quarter, later, mine, near, cross, other, z, x, c, perm, wg, wu, wd, *refs
 ):
-    keep_near, keep_far, send_near, send_far, done, xs, hs, hp, col = refs[later:]
-    i = pl.program_id(0)
-    width = near.shape[1] - EXTRA
+    keep_near, keep_far, send_near, send_far, done, xs, hs, hp = refs[later:]
+    n, width = near.shape[0], near.shape[1] - EXTRA
     far = z.shape[0]
     u = far // 3
-
-    @pl.when(i == 0)
-    def _():
-        done[...] = jnp.zeros(done.shape, F32)
-        mine_at = quarter * u
-        n = near.shape[0]
-        at = 0
-        for ref, begin, count in (
-            (near, mine_at, u),
-            (cross, mine_at, u),
-            (z, 0, far),
-            (x, 0, far),
-            (other, mine_at, u),
-            (other, n + mine_at, u),
-            (c, 0, 2 * far),
-        ):
-            xs[at : at + count, :] = ref[begin : begin + count, :width]
-            parts = ref[begin : begin + count, width:].astype(F32)
-            lane = lax.broadcasted_iota(jnp.int32, parts.shape, 1)
-            parts = jnp.where(lane % experts == mine[0], parts, 0.0)
-            col[at : at + count, :] = jnp.sum(parts, axis=1, keepdims=True)
-            at += count
-
-    @pl.when(i < first)
-    def _():
-        gate = jnp.dot(xs[...], wg[i], preferred_element_type=F32)
-        up = jnp.dot(xs[...], wu[i], preferred_element_type=F32)
-        hs[i] = (gate / (1.0 + jnp.exp(-gate)) * up).astype(BF16)
-
-    @pl.when(i == first)
-    def _():
-        tile = hs.shape[2]
-        each = CHUNK // tile
-        for c in range(first // each):
-            total = None
-            for b in range(each):
-                part = jnp.dot(
-                    hs[c * each + b], perm[b * tile : (b + 1) * tile, :], preferred_element_type=F32
-                )
-                total = part if total is None else total + part
-            hp[:, c * CHUNK : (c + 1) * CHUNK] = total.astype(BF16)
-
-    @pl.when(i >= first)
-    def _():
-        answer = (jnp.dot(hp[...], wd[i - first], preferred_element_type=F32) * col[...]).astype(BF16)
+    tiles, _, tile = wg.shape
+
+    done[...] = jnp.zeros(done.shape, F32)
+    mine_at = quarter * u
+    weights = []
+    at = 0
+    for ref, begin, count in (
+        (near, mine_at, u),
+        (cross, mine_at, u),
+        (z, 0, far),
+        (x, 0, far),
+        (other, mine_at, u),
+        (other, n + mine_at, u),
+        (c, 0, 2 * far),
+    ):
+        xs[at : at + count, :] = ref[begin : begin + count, :width]
+        parts = ref[begin : begin + count, width:].astype(F32)
+        lane = lax.broadcasted_iota(jnp.int32, parts.shape, 1)
+        parts = jnp.where(lane % experts == mine[0], parts, 0.0)
+        weights.append(jnp.sum(parts, axis=1, keepdims=True))
+        at += count
+    weights = jnp.concatenate(weights, axis=0)
+
+    for t in range(tiles):
+        gate = jnp.dot(xs[...], wg[t], preferred_element_type=F32)
+        up = jnp.dot(xs[...], wu[t], preferred_element_type=F32)
+        hs[:, t * tile : (t + 1) * tile] = (gate / (1.0 + jnp.exp(-gate)) * up).astype(BF16)
+    for begin in range(0, hs.shape[1], CHUNK):
+        cols = slice(begin, begin + CHUNK)
+        hp[:, cols] = jnp.dot(hs[:, cols], perm[...], preferred_element_type=F32).astype(BF16)
+    for t in range(wd.shape[0]):
+        cols = slice(t * wd.shape[2], (t + 1) * wd.shape[2])
+        answer = (jnp.dot(hp[...], wd[t], preferred_element_type=F32) * weights).astype(BF16)
         at = 0
         for ref in (keep_near, keep_far, send_near, send_far):
-            ref[...] = answer[at : at + ref.shape[0]]
+            ref[:, cols] = answer[at : at + ref.shape[0]]
             at += ref.shape[0]
 
 
@@ -357,26 +365,21 @@
     far, wide = z.shape
     u = far // 3
     width = wide - EXTRA
-    first, _, tile = wg.shape
-    second, hidden, otile = wd.shape
+    hidden = wd.shape[1]
     rows = 16 * u
     resident = pl.BlockSpec(memory_space=pltpu.VMEM)
-    out = lambda n: pl.BlockSpec((n, otile), lambda i: (0, jnp.maximum(i - first, 0)))
-    return pl.pallas_call(
-        functools.partial(expert_kernel, experts, quarter, first, len(before)),
-        grid=(first + second,),
+    return pl.pallas_call(
+        functools.partial(expert_kernel, experts, quarter, len(before)),
         in_specs=[pl.BlockSpec(memory_space=pltpu.SMEM)] + [resident] * (10 + len(before)),
-        out_specs=[out(2 * u), out(6 * u), out(2 * u), out(6 * u)]
-        + [pl.BlockSpec(memory_space=pltpu.VMEM)],
+        out_specs=[resident] * 5,
         out_shape=[jax.ShapeDtypeStruct((n * u, width), BF16) for n in (2, 6, 2, 6)]
         + [jax.ShapeDtypeStruct((8, 128), F32)],
         scratch_shapes=[
             pltpu.VMEM((rows, width), BF16),
-            pltpu.VMEM((first, rows, tile), BF16),
             pltpu.VMEM((rows, hidden), BF16),
-            pltpu.VMEM((rows, 1), F32),
+            pltpu.VMEM((rows, hidden), BF16),
         ],
-        compiler_params=pltpu.CompilerParams(vmem_limit_bytes=12 * 1024 * 1024),
+        compiler_params=pltpu.CompilerParams(vmem_limit_bytes=14 * 1024 * 1024),
         cost_estimate=pl.CostEstimate(
             flops=2 * rows * width * hidden * 3,
             bytes_accessed=rows * width * 4,
@@ -414,19 +417,18 @@
     half = n // 2
     cross = swap(rows, 2)
     first = [swap(rows[:half], 4 * k) for k in range(1, 4)]
-    two = swap(rows[half:], 8)
     w_down, done_down = unpack(down_codes[0], down_scale[0], down_zero[0], 1792)
     w_gate, done_gate = unpack(gate_codes[0], gate_scale[0], gate_zero[0], 512)
     w_up, done_up = unpack(up_codes[0], up_scale[0], up_zero[0], 512)
     unpacked = [done_down, done_gate, done_up]
 
-    z = [pack([(first[k], q * u, u) for k in range(3)], unpacked + [two]) for q in range(2)]
+    z = [pack([(first[k], q * u, u) for k in range(3)], unpacked) for q in range(2)]
+    two = swap(pack([(rows, half, half)], z), 8)
     onward = pack([(rows, half, half), (two, 0, half)], unpacked)
     one = swap(onward, 4)
     other = swap(pack([(rows, 0, n), (cross, 0, n)], unpacked), 1)
-    z += [pack([(one, q * u, u), (two, q * u, u), (one, half + q * u, u)]) for q in range(2)]
     two_x = swap(pack([(cross, 3 * u, u)], unpacked), 8)
-    x = [swap(v, 2) for v in z[:3]]
+    x = [swap(v, 2) for v in z]
     done, near, far, sent = [], [], [], []
 
     def expert(q, ahead, before):
@@ -444,11 +446,16 @@
         own, crossing = join([far[q]], [swap(sent[q], 1)], before)
         return own, crossing, swap(crossing, 2)
 
-    expert(0, [z[2], z[3]], [])
+    expert(0, [onward], [])
+    z += [
+        pack([(one, q * u, u), (two, q * u, u), (one, half + q * u, u)], done[-1:])
+        for q in range(2)
+    ]
+    x.append(swap(z[2], 2))
     onward_x = pack([(cross, 3 * u, u), (two_x, 0, u)], done[-1:])
     one_x = swap(onward_x, 4)
     leaving_0, staying_0 = land(far[0], swap(sent[0], 1), 2, done[-1:])
-    expert(1, [onward_x], [leaving_0])
+    expert(1, [onward_x, z[2], z[3]], [leaving_0])
     x.append(pack([(one_x, 0, u), (two_x, 0, u), (one_x, u, u)], done[-1:]))
     own_1, crossing_1, crossed_1 = after_core(1, done[-1:])
     expert(2, [x[3]], [crossing_1])

time: 130 us -> 127 us (0.977)
  waiting for transfers between devices: 37.5 us -> 42.7 us
  Pallas kernels: 48.8 us -> 46 us
  local copies, waits for them, and re-layouts: 4.32 us -> 1.71 us
  starting transfers between devices: 36.9 us -> 35 us
    ppermute x34, waiting for transfers between devices: 37.5 us -> 42.7 us  [swap(): return lax.ppermute(value, 'ep', [(i, i ^ bits) for i in range(experts)])]
    pallas_call x4, Pallas kernels: 32.1 us -> 28.2 us  [expert_block(): pl.pallas_call(functools.partial(expert_kernel, experts, quarter, len(bef...]
    unnamed x16 -> x12, local copies, waits for them, and re-layouts: 4.24 us -> 1.65 us
    ppermute x34, starting transfers between devices: 36.9 us -> 35 us  [swap(): return lax.ppermute(value, 'ep', [(i, i ^ bits) for i in range(experts)])]
  transfers between devices with their start and end apart: 34 -> 34, of which waited for: 15 -> 16; matrix products, arithmetic and copies ran while one was open for 0% -> 0% of each run, Pallas kernels for 37% -> 35%
where the time goes in v5:
time: 127 us
  Pallas kernels  46 us (36%)
  waiting for transfers between devices  42.7 us (34%)
  starting transfers between devices  35 us (28%)
  local copies, waits for them, and re-layouts  1.71 us (1%)
  other arithmetic  1.34 us (1%)
    ppermute x34, waiting for transfers between devices, swap(): return lax.ppermute(value, 'ep', [(i, i ^ bits) for i in range(experts)])  42.7 us
    ppermute x34, starting transfers between devices, swap(): return lax.ppermute(value, 'ep', [(i, i ^ bits) for i in range(experts)])  35 us
    pallas_call x4, Pallas kernels, expert_block(): pl.pallas_call(functools.partial(expert_kernel, experts, quarter, len(bef...  28.2 us
    pallas_call x3, Pallas kernels, unpack(): pl.pallas_call(functools.partial(unpack_kernel, len(before)), grid=(steps...  14.3 us
  transfers between devices with their start and end apart: 34, of which 16 were waited for; matrix products, arithmetic and copies ran while one was open for 0% of the time, Pallas kernels for 35%

profile of v5, /device:TPU:0, one launch (start us, length us, event | category | flops | bytes accessed | tf_op | source)
XLA Modules:
  0.0 127.1 jit_solution(9649967921737490289)
XLA Ops:
  0.0 1.8 %prepare.1 = (bf16[64,3712]{1,0:T(8,128)(2,1)S(1)}, bf16[512,512]{1,0:T(8,128)(2,1)S(1)}, s32[1]{0:T(128)}) custom-call(s32[1]{0:T(128)} %bitcast.mine, bf16[64,3584]{1,0:T(8,128)(2,1)} %all_tokens.1, f32[8,64]{1,0:T(8,128)} %bitcast.21, s32[8,64]{1,0:T(8,128)} %bitcast.22), custom_call_target="tpu_custom_call" | custom-call | tf_op jit(solution)/shard_map/prepare/pallas_call | solution.py:132
  1.9 3.0 %collective-permute-start = (bf16[64,3712]{1,0:T(8,128)(2,1)S(1)}, bf16[64,3712]{1,0:T(8,128)(2,1)S(1)}, u32[]{:S(2)}, u32[]{:S(2)}) collective-permute-start(bf16[64,3712]{1,0:T(8,128)(2,1)S(1)} %get-tuple-element.49.refs_0_.near), channel_id=1, source_target_pairs={{0,2},{1,3},{2,0},{3,1},{4,6},{5,7},{6,4},{7,5},{8,10},{9,11},{10,... | collective-permute-start | bytes 1425416 | tf_op jit(solution)/shard_map/ppermute | solution.py:412
  6.5 2.6 %collective-permute-start.3 = (bf16[32,3712]{1,0:T(8,128)(2,1)S(1)}, bf16[32,3712]{1,0:T(8,128)(2,1)S(1)}, u32[]{:S(2)}, u32[]{:S(2)}) collective-permute-start(bf16[32,3712]{1,0:T(8,128)(2,1)S(1)} %slice.41), channel_id=1, source_target_pairs={{0,8},{1,9},{2,10},{3,11},{4,12},{5,13},{6,14},{7,15},{8,0},{9,1},... | collective-permute-start | bytes 712712 | tf_op jit(solution)/shard_map/ppermute | solution.py:412
  11.0 5.4 %unpack.3 = (bf16[2,1024,1792]{2,1,0:T(8,128)(2,1)S(1)}, f32[8,128]{1,0:T(8,128)S(1)}) custom-call(f32[256,3584]{1,0:T(8,128)} %bitcast.18, bf16[8,3584]{1,0:T(8,128)(2,1)S(1)} %bitcast.16, bf16[8,3584]{1,0:T(8,128)(2,1)S(1)} %bitcast.17), custom_call_target="tpu_custom_call" | custom-call | flops 22020096 | bytes 3670016 | tf_op jit(solution)/shard_map/unpack/pallas_call | solution.py:193
  16.4 4.4 %unpack.4 = (bf16[2,3584,512]{2,1,0:T(8,128)(2,1)S(1)}, f32[8,128]{1,0:T(8,128)S(1)}) custom-call(f32[896,1024]{1,0:T(8,128)} %bitcast.19, bf16[28,1024]{1,0:T(8,128)(2,1)S(1)} %bitcast.12, bf16[28,1024]{1,0:T(8,128)(2,1)S(1)} %bitcast.13), custom_call_target="tpu_custom_call" | custom-call | flops 22020096 | bytes 3670016 | tf_op jit(solution)/shard_map/unpack/pallas_call | solution.py:193
  20.8 4.6 %unpack.5 = (bf16[2,3584,512]{2,1,0:T(8,128)(2,1)S(1)}, f32[8,128]{1,0:T(8,128)S(1)}) custom-call(f32[896,1024]{1,0:T(8,128)} %bitcast.20, bf16[28,1024]{1,0:T(8,128)(2,1)S(1)} %bitcast.14, bf16[28,1024]{1,0:T(8,128)(2,1)S(1)} %bitcast.15), custom_call_target="tpu_custom_call" | custom-call | flops 22020096 | bytes 3670016 | tf_op jit(solution)/shard_map/unpack/pallas_call | solution.py:193
  27.0 5.0 %collective-permute-start.6 = (bf16[32,3712]{1,0:T(8,128)(2,1)S(1)}, bf16[32,3712]{1,0:T(8,128)(2,1)S(1)}, u32[]{:S(2)}, u32[]{:S(2)}) collective-permute-start(bf16[32,3712]{1,0:T(8,128)(2,1)S(1)} %pack.20), channel_id=1, source_target_pairs={{0,8},{1,9},{2,10},{3,11},{4,12},{5,13},{6,14},{7,15},{8,0},{9,1},... | collective-permute-start | bytes 712712 | tf_op jit(solution)/shard_map/ppermute | solution.py:412
  32.2 9.0 %collective-permute-done.6.refs_1_ = bf16[32,3712]{1,0:T(8,128)(2,1)S(1)} collective-permute-done((bf16[32,3712]{1,0:T(8,128)(2,1)S(1)}, bf16[32,3712]{1,0:T(8,128)(2,1)S(1)}, u32[]{:S(2)}, u32[]{:S(2)}) %collective-permute-start.6) | collective-permute-done | bytes 237600 | tf_op jit(solution)/shard_map/ppermute | solution.py:412
  42.9 2.0 %collective-permute-start.9 = (bf16[16,3712]{1,0:T(8,128)(2,1)S(1)}, bf16[16,3712]{1,0:T(8,128)(2,1)S(1)}, u32[]{:S(2)}, u32[]{:S(2)}) collective-permute-start(bf16[16,3712]{1,0:T(8,128)(2,1)S(1)} %pack.23), channel_id=1, source_target_pairs={{0,8},{1,9},{2,10},{3,11},{4,12},{5,13},{6,14},{7,15},{8,0},{9,1},... | collective-permute-start | bytes 356360 | tf_op jit(solution)/shard_map/ppermute | solution.py:412
  44.9 7.0 %expert_block.4 = (bf16[32,3584]{1,0:T(8,128)(2,1)S(1)}, bf16[96,3584]{1,0:T(8,128)(2,1)S(1)}, bf16[32,3584]{1,0:T(8,128)(2,1)S(1)}, bf16[96,3584]{1,0:T(8,128)(2,1)S(1)}, f32[8,128]{1,0:T(8,128)S(1)}) custom-call(s32[1]{0:T(128)} %get-tuple-element.48.mine, bf16[64,3712]{1,0:T(8,128)(2,1)S(1)} %get-tuple-element.49.refs_0_.near, ...), custom_call_target="tpu_custom_call" | custom-call | flops 5637144576 | bytes 3670016 | tf_op jit(solution)/shard_map/expert_block/pallas_call | solution.py:371
  51.9 6.5 %collective-permute-done.10.refs_0_.refs_2_ = bf16[64,3712]{1,0:T(8,128)(2,1)S(1)} collective-permute-done((bf16[64,3712]{1,0:T(8,128)(2,1)S(1)}, bf16[64,3712]{1,0:T(8,128)(2,1)S(1)}, u32[]{:S(2)}, u32[]{:S(2)}) %collective-permute-start.10) | collective-permute-done | bytes 475168 | tf_op jit(solution)/shard_map/ppermute | solution.py:412
  59.8 2.0 %collective-permute-done.12.got = bf16[96,3584]{1,0:T(8,128)(2,1)S(1)} collective-permute-done((bf16[96,3584]{1,0:T(8,128)(2,1)S(1)}, bf16[96,3584]{1,0:T(8,128)(2,1)S(1)}, u32[]{:S(2)}, u32[]{:S(2)}) %collective-permute-start.12) | collective-permute-done | bytes 688160 | tf_op jit(solution)/shard_map/ppermute | solution.py:412
  62.0 7.0 %expert_block.5 = (bf16[32,3584]{1,0:T(8,128)(2,1)S(1)}, bf16[96,3584]{1,0:T(8,128)(2,1)S(1)}, bf16[32,3584]{1,0:T(8,128)(2,1)S(1)}, bf16[96,3584]{1,0:T(8,128)(2,1)S(1)}, f32[8,128]{1,0:T(8,128)S(1)}) custom-call(s32[1]{0:T(128)} %get-tuple-element.48.mine, bf16[64,3712]{1,0:T(8,128)(2,1)S(1)} %get-tuple-element.49.refs_0_.near, ...), custom_call_target="tpu_custom_call" | custom-call | flops 5637144576 | bytes 3670016 | tf_op jit(solution)/shard_map/expert_block/pallas_call | solution.py:371
  73.5 7.2 %expert_block.6 = (bf16[32,3584]{1,0:T(8,128)(2,1)S(1)}, bf16[96,3584]{1,0:T(8,128)(2,1)S(1)}, bf16[32,3584]{1,0:T(8,128)(2,1)S(1)}, bf16[96,3584]{1,0:T(8,128)(2,1)S(1)}, f32[8,128]{1,0:T(8,128)S(1)}) custom-call(s32[1]{0:T(128)} %get-tuple-element.48.mine, bf16[64,3712]{1,0:T(8,128)(2,1)S(1)} %get-tuple-element.49.refs_0_.near, ...), custom_call_target="tpu_custom_call" | custom-call | flops 5637144576 | bytes 3670016 | tf_op jit(solution)/shard_map/expert_block/pallas_call | solution.py:371
  80.8 1.8 %collective-permute-done.17.got = bf16[64,3584]{1,0:T(8,128)(2,1)S(1)} collective-permute-done((bf16[64,3584]{1,0:T(8,128)(2,1)S(1)}, bf16[64,3584]{1,0:T(8,128)(2,1)S(1)}, u32[]{:S(2)}, u32[]{:S(2)}) %collective-permute-start.17) | collective-permute-done | bytes 458784 | tf_op jit(solution)/shard_map/ppermute | solution.py:412
  87.4 7.0 %expert_block.7 = (bf16[32,3584]{1,0:T(8,128)(2,1)S(1)}, bf16[96,3584]{1,0:T(8,128)(2,1)S(1)}, bf16[32,3584]{1,0:T(8,128)(2,1)S(1)}, bf16[96,3584]{1,0:T(8,128)(2,1)S(1)}, f32[8,128]{1,0:T(8,128)S(1)}) custom-call(s32[1]{0:T(128)} %get-tuple-element.48.mine, bf16[64,3712]{1,0:T(8,128)(2,1)S(1)} %get-tuple-element.49.refs_0_.near, ...), custom_call_target="tpu_custom_call" | custom-call | flops 5637144576 | bytes 3670016 | tf_op jit(solution)/shard_map/expert_block/pallas_call | solution.py:371
  94.4 2.4 %collective-permute-done.27.got = bf16[48,3584]{1,0:T(8,128)(2,1)S(1)} collective-permute-done((bf16[48,3584]{1,0:T(8,128)(2,1)S(1)}, bf16[48,3584]{1,0:T(8,128)(2,1)S(1)}, u32[]{:S(2)}, u32[]{:S(2)}) %collective-permute-start.27) | collective-permute-done | bytes 344096 | tf_op jit(solution)/shard_map/ppermute | solution.py:412
  101.7 3.0 %collective-permute-done.28.got = bf16[32,3584]{1,0:T(8,128)(2,1)S(1)} collective-permute-done((bf16[32,3584]{1,0:T(8,128)(2,1)S(1)}, bf16[32,3584]{1,0:T(8,128)(2,1)S(1)}, u32[]{:S(2)}, u32[]{:S(2)}) %collective-permute-start.28) | collective-permute-done | bytes 229408 | tf_op jit(solution)/shard_map/ppermute | solution.py:412
  104.8 1.9 %collective-permute-start.30 = (bf16[16,3584]{1,0:T(8,128)(2,1)S(1)}, bf16[16,3584]{1,0:T(8,128)(2,1)S(1)}, u32[]{:S(2)}, u32[]{:S(2)}) collective-permute-start(bf16[16,3584]{1,0:T(8,128)(2,1)S(1)} %pass_on.6), channel_id=1, source_target_pairs={{0,8},{1,9},{2,10},{3,11},{4,12},{5,13},{6,14},{7,15},{8,0},{9,1},... | collective-permute-start | bytes 344072 | tf_op jit(solution)/shard_map/ppermute | solution.py:412
  107.9 4.2 %collective-permute-done.31.got = bf16[48,3584]{1,0:T(8,128)(2,1)S(1)} collective-permute-done((bf16[48,3584]{1,0:T(8,128)(2,1)S(1)}, bf16[48,3584]{1,0:T(8,128)(2,1)S(1)}, u32[]{:S(2)}, u32[]{:S(2)}) %collective-permute-start.31) | collective-permute-done | bytes 344096 | tf_op jit(solution)/shard_map/ppermute | solution.py:412
  112.9 3.3 %collective-permute-done.23.refs_0_ = bf16[32,3584]{1,0:T(8,128)(2,1)S(1)} collective-permute-done((bf16[32,3584]{1,0:T(8,128)(2,1)S(1)}, bf16[32,3584]{1,0:T(8,128)(2,1)S(1)}, u32[]{:S(2)}, u32[]{:S(2)}) %collective-permute-start.23) | collective-permute-done | bytes 229408 | tf_op jit(solution)/shard_map/ppermute | solution.py:412
  116.2 2.0 %collective-permute-done.32.got = bf16[32,3584]{1,0:T(8,128)(2,1)S(1)} collective-permute-done((bf16[32,3584]{1,0:T(8,128)(2,1)S(1)}, bf16[32,3584]{1,0:T(8,128)(2,1)S(1)}, u32[]{:S(2)}, u32[]{:S(2)}) %collective-permute-start.32) | collective-permute-done | bytes 229408 | tf_op jit(solution)/shard_map/ppermute | solution.py:412
  118.3 1.8 %collective-permute-start.33 = (bf16[16,3584]{1,0:T(8,128)(2,1)S(1)}, bf16[16,3584]{1,0:T(8,128)(2,1)S(1)}, u32[]{:S(2)}, u32[]{:S(2)}) collective-permute-start(bf16[16,3584]{1,0:T(8,128)(2,1)S(1)} %pass_on.7), channel_id=1, source_target_pairs={{0,8},{1,9},{2,10},{3,11},{4,12},{5,13},{6,14},{7,15},{8,0},{9,1},... | collective-permute-start | bytes 344072 | tf_op jit(solution)/shard_map/ppermute | solution.py:412
  120.7 4.5 %collective-permute-done.33 = bf16[16,3584]{1,0:T(8,128)(2,1)S(1)} collective-permute-done((bf16[16,3584]{1,0:T(8,128)(2,1)S(1)}, bf16[16,3584]{1,0:T(8,128)(2,1)S(1)}, u32[]{:S(2)}, u32[]{:S(2)}) %collective-permute-start.33) | collective-permute-done | bytes 114720 | tf_op jit(solution)/shard_map/ppermute | solution.py:412
  (103 shorter events, 27.3 us)
Async XLA Ops:
  1.9 30.2 %collective-permute-start = (bf16[64,3712]{1,0:T(8,128)(2,1)S(1)}, bf16[64,3712]{1,0:T(8,128)(2,1)S(1)}, u32[]{:S(2)}, u32[]{:S(2)}) collective-permute-start(bf16[64,3712]{1,0:T(8,128)(2,1)S(1)} %get-tuple-element.49.refs_0_.near), channel_id=1, source_target_pairs={{0,2},{1,3},{2,0},{3,1},{4,6},{5,7},{6,4},{7,5},{8,10},{9,11},{10,... | collective-permute-start | bytes 1425416 | tf_op jit(solution)/shard_map/ppermute | solution.py:412
  4.9 20.5 %collective-permute-start.2 = (bf16[32,3712]{1,0:T(8,128)(2,1)S(1)}, bf16[32,3712]{1,0:T(8,128)(2,1)S(1)}, u32[]{:S(2)}, u32[]{:S(2)}) collective-permute-start(bf16[32,3712]{1,0:T(8,128)(2,1)S(1)} %slice.41), channel_id=1, source_target_pairs={{0,4},{1,5},{2,6},{3,7},{4,0},{5,1},{6,2},{7,3},{8,12},{9,13},{10,... | collective-permute-start | bytes 712712 | tf_op jit(solution)/shard_map/ppermute | solution.py:412
  6.5 19.8 %collective-permute-start.3 = (bf16[32,3712]{1,0:T(8,128)(2,1)S(1)}, bf16[32,3712]{1,0:T(8,128)(2,1)S(1)}, u32[]{:S(2)}, u32[]{:S(2)}) collective-permute-start(bf16[32,3712]{1,0:T(8,128)(2,1)S(1)} %slice.41), channel_id=1, source_target_pairs={{0,8},{1,9},{2,10},{3,11},{4,12},{5,13},{6,14},{7,15},{8,0},{9,1},... | collective-permute-start | bytes 712712 | tf_op jit(solution)/shard_map/ppermute | solution.py:412
  9.1 17.2 %collective-permute-start.4 = (bf16[32,3712]{1,0:T(8,128)(2,1)S(1)}, bf16[32,3712]{1,0:T(8,128)(2,1)S(1)}, u32[]{:S(2)}, u32[]{:S(2)}) collective-permute-start(bf16[32,3712]{1,0:T(8,128)(2,1)S(1)} %slice.41), channel_id=1, source_target_pairs={{0,12},{1,13},{2,14},{3,15},{4,8},{5,9},{6,10},{7,11},{8,4},{9,5},... | collective-permute-start | bytes 712712 | tf_op jit(solution)/shard_map/ppermute | solution.py:412
  26.4 14.9 %collective-permute-start.5 = (bf16[48,3712]{1,0:T(8,128)(2,1)S(1)}, bf16[48,3712]{1,0:T(8,128)(2,1)S(1)}, u32[]{:S(2)}, u32[]{:S(2)}) collective-permute-start(bf16[48,3712]{1,0:T(8,128)(2,1)S(1)} %pack.18.refs_1_.refs_0_.z), channel_id=1, source_target_pairs={{0,2},{1,3},{2,0},{3,1},{4,6},{5,7},{6,4},{7,5},{8,10},{9,11},{10,... | collective-permute-start | bytes 1069064 | tf_op jit(solution)/shard_map/ppermute | solution.py:412
  27.0 14.2 %collective-permute-start.6 = (bf16[32,3712]{1,0:T(8,128)(2,1)S(1)}, bf16[32,3712]{1,0:T(8,128)(2,1)S(1)}, u32[]{:S(2)}, u32[]{:S(2)}) collective-permute-start(bf16[32,3712]{1,0:T(8,128)(2,1)S(1)} %pack.20), channel_id=1, source_target_pairs={{0,8},{1,9},{2,10},{3,11},{4,12},{5,13},{6,14},{7,15},{8,0},{9,1},... | collective-permute-start | bytes 712712 | tf_op jit(solution)/shard_map/ppermute | solution.py:412
  32.1 12.8 %collective-permute-start.1 = (bf16[128,3712]{1,0:T(8,128)(2,1)S(1)}, bf16[128,3712]{1,0:T(8,128)(2,1)S(1)}, u32[]{:S(2)}, u32[]{:S(2)}) collective-permute-start(bf16[128,3712]{1,0:T(8,128)(2,1)S(1)} %pack.17), channel_id=1, source_target_pairs={{0,1},{1,0},{2,3},{3,2},{4,5},{5,4},{6,7},{7,6},{8,9},{9,8},{10,11... | collective-permute-start | bytes 2850824 | tf_op jit(solution)/shard_map/ppermute | solution.py:412
  41.4 17.1 %collective-permute-start.8 = (bf16[48,3712]{1,0:T(8,128)(2,1)S(1)}, bf16[48,3712]{1,0:T(8,128)(2,1)S(1)}, u32[]{:S(2)}, u32[]{:S(2)}) collective-permute-start(bf16[48,3712]{1,0:T(8,128)(2,1)S(1)} %pack.19.refs_2_.refs_0_.z), channel_id=1, source_target_pairs={{0,2},{1,3},{2,0},{3,1},{4,6},{5,7},{6,4},{7,5},{8,10},{9,11},{10,... | collective-permute-start | bytes 1069064 | tf_op jit(solution)/shard_map/ppermute | solution.py:412
  42.9 15.5 %collective-permute-start.10 = (bf16[64,3712]{1,0:T(8,128)(2,1)S(1)}, bf16[64,3712]{1,0:T(8,128)(2,1)S(1)}, u32[]{:S(2)}, u32[]{:S(2)}) collective-permute-start(bf16[64,3712]{1,0:T(8,128)(2,1)S(1)} %pack.21.refs_2_), channel_id=1, source_target_pairs={{0,4},{1,5},{2,6},{3,7},{4,0},{5,1},{6,2},{7,3},{8,12},{9,13},{10,... | collective-permute-start | bytes 1425416 | tf_op jit(solution)/shard_map/ppermute | solution.py:412
  42.9 15.5 %collective-permute-start.9 = (bf16[16,3712]{1,0:T(8,128)(2,1)S(1)}, bf16[16,3712]{1,0:T(8,128)(2,1)S(1)}, u32[]{:S(2)}, u32[]{:S(2)}) collective-permute-start(bf16[16,3712]{1,0:T(8,128)(2,1)S(1)} %pack.23), channel_id=1, source_target_pairs={{0,8},{1,9},{2,10},{3,11},{4,12},{5,13},{6,14},{7,15},{8,0},{9,1},... | collective-permute-start | bytes 356360 | tf_op jit(solution)/shard_map/ppermute | solution.py:412
  59.2 9.8 %collective-permute-start.14 = (bf16[32,3712]{1,0:T(8,128)(2,1)S(1)}, bf16[32,3712]{1,0:T(8,128)(2,1)S(1)}, u32[]{:S(2)}, u32[]{:S(2)}) collective-permute-start(bf16[32,3712]{1,0:T(8,128)(2,1)S(1)} %pack.24.refs_3_), channel_id=1, source_target_pairs={{0,4},{1,5},{2,6},{3,7},{4,0},{5,1},{6,2},{7,3},{8,12},{9,13},{10,... | collective-permute-start | bytes 712712 | tf_op jit(solution)/shard_map/ppermute | solution.py:412
  59.3 10.2 %collective-permute-start.13 = (bf16[48,3712]{1,0:T(8,128)(2,1)S(1)}, bf16[48,3712]{1,0:T(8,128)(2,1)S(1)}, u32[]{:S(2)}, u32[]{:S(2)}) collective-permute-start(bf16[48,3712]{1,0:T(8,128)(2,1)S(1)} %pack.25.refs_4_.refs_0_.z), channel_id=1, source_target_pairs={{0,2},{1,3},{2,0},{3,1},{4,6},{5,7},{6,4},{7,5},{8,10},{9,11},{10,... | collective-permute-start | bytes 1069064 | tf_op jit(solution)/shard_map/ppermute | solution.py:412
  70.1 12.5 %collective-permute-start.17 = (bf16[64,3584]{1,0:T(8,128)(2,1)S(1)}, bf16[64,3584]{1,0:T(8,128)(2,1)S(1)}, u32[]{:S(2)}, u32[]{:S(2)}) collective-permute-start(bf16[64,3584]{1,0:T(8,128)(2,1)S(1)} %get-tuple-element.61.refs_0_), channel_id=1, source_target_pairs={{0,4},{1,5},{2,6},{3,7},{4,0},{5,1},{6,2},{7,3},{8,12},{9,13},{10,... | collective-permute-start | bytes 1376264 | tf_op jit(solution)/shard_map/ppermute | solution.py:412
  72.9 10.2 %collective-permute-start.18 = (bf16[48,3584]{1,0:T(8,128)(2,1)S(1)}, bf16[48,3584]{1,0:T(8,128)(2,1)S(1)}, u32[]{:S(2)}, u32[]{:S(2)}) collective-permute-start(bf16[48,3584]{1,0:T(8,128)(2,1)S(1)} %get-tuple-element.66.refs_0_), channel_id=1, source_target_pairs={{0,2},{1,3},{2,0},{3,1},{4,6},{5,7},{6,4},{7,5},{8,10},{9,11},{10,... | collective-permute-start | bytes 1032200 | tf_op jit(solution)/shard_map/ppermute | solution.py:412
  83.8 15.7 %collective-permute-start.22 = (bf16[32,3584]{1,0:T(8,128)(2,1)S(1)}, bf16[32,3584]{1,0:T(8,128)(2,1)S(1)}, u32[]{:S(2)}, u32[]{:S(2)}) collective-permute-start(bf16[32,3584]{1,0:T(8,128)(2,1)S(1)} %pass_on.4.refs_3_), channel_id=1, source_target_pairs={{0,8},{1,9},{2,10},{3,11},{4,12},{5,13},{6,14},{7,15},{8,0},{9,1},... | collective-permute-start | bytes 688136 | tf_op jit(solution)/shard_map/ppermute | solution.py:412
  85.4 13.2 %collective-permute-start.25 = (bf16[32,3584]{1,0:T(8,128)(2,1)S(1)}, bf16[32,3584]{1,0:T(8,128)(2,1)S(1)}, u32[]{:S(2)}, u32[]{:S(2)}) collective-permute-start(bf16[32,3584]{1,0:T(8,128)(2,1)S(1)} %get-tuple-element.71.refs_4_), channel_id=1, source_target_pairs={{0,4},{1,5},{2,6},{3,7},{4,0},{5,1},{6,2},{7,3},{8,12},{9,13},{10,... | collective-permute-start | bytes 688136 | tf_op jit(solution)/shard_map/ppermute | solution.py:412
  86.8 10.0 %collective-permute-start.27 = (bf16[48,3584]{1,0:T(8,128)(2,1)S(1)}, bf16[48,3584]{1,0:T(8,128)(2,1)S(1)}, u32[]{:S(2)}, u32[]{:S(2)}) collective-permute-start(bf16[48,3584]{1,0:T(8,128)(2,1)S(1)} %get-tuple-element.74.refs_0_), channel_id=1, source_target_pairs={{0,2},{1,3},{2,0},{3,1},{4,6},{5,7},{6,4},{7,5},{8,10},{9,11},{10,... | collective-permute-start | bytes 1032200 | tf_op jit(solution)/shard_map/ppermute | solution.py:412
  96.9 7.9 %collective-permute-start.28 = (bf16[32,3584]{1,0:T(8,128)(2,1)S(1)}, bf16[32,3584]{1,0:T(8,128)(2,1)S(1)}, u32[]{:S(2)}, u32[]{:S(2)}) collective-permute-start(bf16[32,3584]{1,0:T(8,128)(2,1)S(1)} %get-tuple-element.83.refs_2_), channel_id=1, source_target_pairs={{0,4},{1,5},{2,6},{3,7},{4,0},{5,1},{6,2},{7,3},{8,12},{9,13},{10,... | collective-permute-start | bytes 688136 | tf_op jit(solution)/shard_map/ppermute | solution.py:412
  98.9 7.7 %collective-permute-start.21 = (bf16[128,3584]{1,0:T(8,128)(2,1)S(1)}, bf16[128,3584]{1,0:T(8,128)(2,1)S(1)}, u32[]{:S(2)}, u32[]{:S(2)}) collective-permute-start(bf16[128,3584]{1,0:T(8,128)(2,1)S(1)} %pack.32), channel_id=1, source_target_pairs={{0,1},{1,0},{2,3},{3,2},{4,5},{5,4},{6,7},{7,6},{8,9},{9,8},{10,11... | collective-permute-start | bytes 2752520 | tf_op jit(solution)/shard_map/ppermute | solution.py:412
  99.5 13.4 %collective-permute-start.26 = (bf16[16,3584]{1,0:T(8,128)(2,1)S(1)}, bf16[16,3584]{1,0:T(8,128)(2,1)S(1)}, u32[]{:S(2)}, u32[]{:S(2)}) collective-permute-start(bf16[16,3584]{1,0:T(8,128)(2,1)S(1)} %pass_on.5.refs_1_), channel_id=1, source_target_pairs={{0,8},{1,9},{2,10},{3,11},{4,12},{5,13},{6,14},{7,15},{8,0},{9,1},... | collective-permute-start | bytes 344072 | tf_op jit(solution)/shard_map/ppermute | solution.py:412
  101.1 11.0 %collective-permute-start.31 = (bf16[48,3584]{1,0:T(8,128)(2,1)S(1)}, bf16[48,3584]{1,0:T(8,128)(2,1)S(1)}, u32[]{:S(2)}, u32[]{:S(2)}) collective-permute-start(bf16[48,3584]{1,0:T(8,128)(2,1)S(1)} %get-tuple-element.87.refs_0_), channel_id=1, source_target_pairs={{0,2},{1,3},{2,0},{3,1},{4,6},{5,7},{6,4},{7,5},{8,10},{9,11},{10,... | collective-permute-start | bytes 1032200 | tf_op jit(solution)/shard_map/ppermute | solution.py:412
  104.8 15.3 %collective-permute-start.30 = (bf16[16,3584]{1,0:T(8,128)(2,1)S(1)}, bf16[16,3584]{1,0:T(8,128)(2,1)S(1)}, u32[]{:S(2)}, u32[]{:S(2)}) collective-permute-start(bf16[16,3584]{1,0:T(8,128)(2,1)S(1)} %pass_on.6), channel_id=1, source_target_pairs={{0,8},{1,9},{2,10},{3,11},{4,12},{5,13},{6,14},{7,15},{8,0},{9,1},... | collective-permute-start | bytes 344072 | tf_op jit(solution)/shard_map/ppermute | solution.py:412
  107.0 9.2 %collective-permute-start.23 = (bf16[32,3584]{1,0:T(8,128)(2,1)S(1)}, bf16[32,3584]{1,0:T(8,128)(2,1)S(1)}, u32[]{:S(2)}, u32[]{:S(2)}) collective-permute-start(bf16[32,3584]{1,0:T(8,128)(2,1)S(1)} %pad_maximum_fusion), channel_id=1, source_target_pairs={{0,2},{1,3},{2,0},{3,1},{4,6},{5,7},{6,4},{7,5},{8,10},{9,11},{10,... | collective-permute-start | bytes 688136 | tf_op jit(solution)/shard_map/ppermute | solution.py:412
  118.3 7.0 %collective-permute-start.33 = (bf16[16,3584]{1,0:T(8,128)(2,1)S(1)}, bf16[16,3584]{1,0:T(8,128)(2,1)S(1)}, u32[]{:S(2)}, u32[]{:S(2)}) collective-permute-start(bf16[16,3584]{1,0:T(8,128)(2,1)S(1)} %pass_on.7), channel_id=1, source_target_pairs={{0,8},{1,9},{2,10},{3,11},{4,12},{5,13},{6,14},{7,15},{8,0},{9,1},... | collective-permute-start | bytes 344072 | tf_op jit(solution)/shard_map/ppermute | solution.py:412
  (16 other events, 93.5 us)

commit v6 on v5

--- a/solution.py
+++ b/solution.py
@@ -417,15 +417,15 @@
     half = n // 2
     cross = swap(rows, 2)
     first = [swap(rows[:half], 4 * k) for k in range(1, 4)]
+    one = swap(rows[half:], 4)
     w_down, done_down = unpack(down_codes[0], down_scale[0], down_zero[0], 1792)
     w_gate, done_gate = unpack(gate_codes[0], gate_scale[0], gate_zero[0], 512)
     w_up, done_up = unpack(up_codes[0], up_scale[0], up_zero[0], 512)
     unpacked = [done_down, done_gate, done_up]
 
-    z = [pack([(first[k], q * u, u) for k in range(3)], unpacked) for q in range(2)]
-    two = swap(pack([(rows, half, half)], z), 8)
-    onward = pack([(rows, half, half), (two, 0, half)], unpacked)
-    one = swap(onward, 4)
+    z = [pack([(first[k], q * u, u) for k in range(3)], unpacked + [one]) for q in range(2)]
+    onward = [pack([(rows, half + q * u, u), (one, q * u, u)], z) for q in range(2)]
+    two = [swap(v, 8) for v in onward]
     other = swap(pack([(rows, 0, n), (cross, 0, n)], unpacked), 1)
     two_x = swap(pack([(cross, 3 * u, u)], unpacked), 8)
     x = [swap(v, 2) for v in z]
@@ -446,19 +446,17 @@
         own, crossing = join([far[q]], [swap(sent[q], 1)], before)
         return own, crossing, swap(crossing, 2)
 
-    expert(0, [onward], [])
-    z += [
-        pack([(one, q * u, u), (two, q * u, u), (one, half + q * u, u)], done[-1:])
-        for q in range(2)
-    ]
+    z.append(pack([(one, 0, u), (two[0], 0, u), (two[0], u, u)]))
+    expert(0, [z[2]], [])
     x.append(swap(z[2], 2))
     onward_x = pack([(cross, 3 * u, u), (two_x, 0, u)], done[-1:])
     one_x = swap(onward_x, 4)
     leaving_0, staying_0 = land(far[0], swap(sent[0], 1), 2, done[-1:])
-    expert(1, [onward_x, z[2], z[3]], [leaving_0])
+    expert(1, [onward_x], [leaving_0, onward[1]])
+    z.append(pack([(one, u, u), (two[1], 0, u), (two[1], u, u)], done[-1:]))
     x.append(pack([(one_x, 0, u), (two_x, 0, u), (one_x, u, u)], done[-1:]))
     own_1, crossing_1, crossed_1 = after_core(1, done[-1:])
-    expert(2, [x[3]], [crossing_1])
+    expert(2, [x[3], z[3]], [crossing_1])
     got_0 = swap(leaving_0, 4)
     passed_0 = pass_on(staying_0, got_0, done[-1:])
     leaving_1, staying_1 = land(own_1, crossed_1, 1, done[-1:])

time: 127 us -> 125 us (0.984)
  starting transfers between devices: 35 us -> 32.7 us
    ppermute x34 -> x35, starting transfers between devices: 35 us -> 32.7 us  [swap(): return lax.ppermute(value, 'ep', [(i, i ^ bits) for i in range(experts)])]
    ppermute x34 -> x35, waiting for transfers between devices: 42.7 us -> 42.9 us  [swap(): return lax.ppermute(value, 'ep', [(i, i ^ bits) for i in range(experts)])]
  transfers between devices with their start and end apart: 34 -> 35, of which waited for: 16 -> 18; matrix products, arithmetic and copies ran while one was open for 0% -> 0% of each run, Pallas kernels for 35% -> 35%
where the time goes in v6:
time: 125 us
  Pallas kernels  45.6 us (36%)
  waiting for transfers between devices  42.9 us (34%)
  starting transfers between devices  32.7 us (26%)
  local copies, waits for them, and re-layouts  1.73 us (1%)
  other arithmetic  1.35 us (1%)
    ppermute x35, waiting for transfers between devices, swap(): return lax.ppermute(value, 'ep', [(i, i ^ bits) for i in range(experts)])  42.9 us
    ppermute x35, starting transfers between devices, swap(): return lax.ppermute(value, 'ep', [(i, i ^ bits) for i in range(experts)])  32.7 us
    pallas_call x4, Pallas kernels, expert_block(): pl.pallas_call(functools.partial(expert_kernel, experts, quarter, len(bef...  27.8 us
    pallas_call x3, Pallas kernels, unpack(): pl.pallas_call(functools.partial(unpack_kernel, len(before)), grid=(steps...  14.3 us
  transfers between devices with their start and end apart: 35, of which 18 were waited for; matrix products, arithmetic and copies ran while one was open for 0% of the time, Pallas kernels for 35%

profile of v6, /device:TPU:0, one launch (start us, length us, event | category | flops | bytes accessed | tf_op | source)
XLA Modules:
  0.0 124.8 jit_solution(7065371078311823052)
XLA Ops:
  0.0 1.8 %prepare.1 = (bf16[64,3712]{1,0:T(8,128)(2,1)S(1)}, bf16[512,512]{1,0:T(8,128)(2,1)S(1)}, s32[1]{0:T(128)}) custom-call(s32[1]{0:T(128)} %bitcast.mine, bf16[64,3584]{1,0:T(8,128)(2,1)} %all_tokens.1, f32[8,64]{1,0:T(8,128)} %bitcast.21, s32[8,64]{1,0:T(8,128)} %bitcast.22), custom_call_target="tpu_custom_call" | custom-call | tf_op jit(solution)/shard_map/prepare/pallas_call | solution.py:132
  1.9 3.0 %collective-permute-start = (bf16[64,3712]{1,0:T(8,128)(2,1)S(1)}, bf16[64,3712]{1,0:T(8,128)(2,1)S(1)}, u32[]{:S(2)}, u32[]{:S(2)}) collective-permute-start(bf16[64,3712]{1,0:T(8,128)(2,1)S(1)} %get-tuple-element.49.refs_0_.near), channel_id=1, source_target_pairs={{0,2},{1,3},{2,0},{3,1},{4,6},{5,7},{6,4},{7,5},{8,10},{9,11},{10,... | collective-permute-start | bytes 1425416 | tf_op jit(solution)/shard_map/ppermute | solution.py:412
  7.0 2.6 %collective-permute-start.3 = (bf16[32,3712]{1,0:T(8,128)(2,1)S(1)}, bf16[32,3712]{1,0:T(8,128)(2,1)S(1)}, u32[]{:S(2)}, u32[]{:S(2)}) collective-permute-start(bf16[32,3712]{1,0:T(8,128)(2,1)S(1)} %get-tuple-element.94), channel_id=1, source_target_pairs={{0,8},{1,9},{2,10},{3,11},{4,12},{5,13},{6,14},{7,15},{8,0},{9,1},... | collective-permute-start | bytes 712712 | tf_op jit(solution)/shard_map/ppermute | solution.py:412
  12.6 5.4 %unpack.3 = (bf16[2,1024,1792]{2,1,0:T(8,128)(2,1)S(1)}, f32[8,128]{1,0:T(8,128)S(1)}) custom-call(f32[256,3584]{1,0:T(8,128)} %bitcast.18, bf16[8,3584]{1,0:T(8,128)(2,1)S(1)} %bitcast.16, bf16[8,3584]{1,0:T(8,128)(2,1)S(1)} %bitcast.17), custom_call_target="tpu_custom_call" | custom-call | flops 22020096 | bytes 3670016 | tf_op jit(solution)/shard_map/unpack/pallas_call | solution.py:193
  18.0 4.4 %unpack.4 = (bf16[2,3584,512]{2,1,0:T(8,128)(2,1)S(1)}, f32[8,128]{1,0:T(8,128)S(1)}) custom-call(f32[896,1024]{1,0:T(8,128)} %bitcast.19, bf16[28,1024]{1,0:T(8,128)(2,1)S(1)} %bitcast.12, bf16[28,1024]{1,0:T(8,128)(2,1)S(1)} %bitcast.13), custom_call_target="tpu_custom_call" | custom-call | flops 22020096 | bytes 3670016 | tf_op jit(solution)/shard_map/unpack/pallas_call | solution.py:193
  22.4 4.6 %unpack.5 = (bf16[2,3584,512]{2,1,0:T(8,128)(2,1)S(1)}, f32[8,128]{1,0:T(8,128)S(1)}) custom-call(f32[896,1024]{1,0:T(8,128)} %bitcast.20, bf16[28,1024]{1,0:T(8,128)(2,1)S(1)} %bitcast.14, bf16[28,1024]{1,0:T(8,128)(2,1)S(1)} %bitcast.15), custom_call_target="tpu_custom_call" | custom-call | flops 22020096 | bytes 3670016 | tf_op jit(solution)/shard_map/unpack/pallas_call | solution.py:193
  27.0 2.6 %collective-permute-done.4.refs_2_ = bf16[32,3712]{1,0:T(8,128)(2,1)S(1)} collective-permute-done((bf16[32,3712]{1,0:T(8,128)(2,1)S(1)}, bf16[32,3712]{1,0:T(8,128)(2,1)S(1)}, u32[]{:S(2)}, u32[]{:S(2)}) %collective-permute-start.4) | collective-permute-done | bytes 237600 | tf_op jit(solution)/shard_map/ppermute | solution.py:412
  30.3 3.0 %collective-permute-start.7 = (bf16[32,3712]{1,0:T(8,128)(2,1)S(1)}, bf16[32,3712]{1,0:T(8,128)(2,1)S(1)}, u32[]{:S(2)}, u32[]{:S(2)}) collective-permute-start(bf16[32,3712]{1,0:T(8,128)(2,1)S(1)} %pack.20), channel_id=1, source_target_pairs={{0,8},{1,9},{2,10},{3,11},{4,12},{5,13},{6,14},{7,15},{8,0},{9,1},... | collective-permute-start | bytes 712712 | tf_op jit(solution)/shard_map/ppermute | solution.py:412
  33.5 8.7 %collective-permute-done.7.refs_1_.refs_2_ = bf16[32,3712]{1,0:T(8,128)(2,1)S(1)} collective-permute-done((bf16[32,3712]{1,0:T(8,128)(2,1)S(1)}, bf16[32,3712]{1,0:T(8,128)(2,1)S(1)}, u32[]{:S(2)}, u32[]{:S(2)}) %collective-permute-start.7) | collective-permute-done | bytes 237600 | tf_op jit(solution)/shard_map/ppermute | solution.py:412
  44.6 6.9 %expert_block.4 = (bf16[32,3584]{1,0:T(8,128)(2,1)S(1)}, bf16[96,3584]{1,0:T(8,128)(2,1)S(1)}, bf16[32,3584]{1,0:T(8,128)(2,1)S(1)}, bf16[96,3584]{1,0:T(8,128)(2,1)S(1)}, f32[8,128]{1,0:T(8,128)S(1)}) custom-call(s32[1]{0:T(128)} %get-tuple-element.48.mine, bf16[64,3712]{1,0:T(8,128)(2,1)S(1)} %get-tuple-element.49.refs_0_.near, ...), custom_call_target="tpu_custom_call" | custom-call | flops 5637144576 | bytes 3670016 | tf_op jit(solution)/shard_map/expert_block/pallas_call | solution.py:371
  55.4 2.0 %collective-permute-start.14 = (bf16[32,3712]{1,0:T(8,128)(2,1)S(1)}, bf16[32,3712]{1,0:T(8,128)(2,1)S(1)}, u32[]{:S(2)}, u32[]{:S(2)}) collective-permute-start(bf16[32,3712]{1,0:T(8,128)(2,1)S(1)} %pack.24.refs_3_), channel_id=1, source_target_pairs={{0,4},{1,5},{2,6},{3,7},{4,0},{5,1},{6,2},{7,3},{8,12},{9,13},{10,... | collective-permute-start | bytes 712712 | tf_op jit(solution)/shard_map/ppermute | solution.py:412
  57.6 6.9 %expert_block.5 = (bf16[32,3584]{1,0:T(8,128)(2,1)S(1)}, bf16[96,3584]{1,0:T(8,128)(2,1)S(1)}, bf16[32,3584]{1,0:T(8,128)(2,1)S(1)}, bf16[96,3584]{1,0:T(8,128)(2,1)S(1)}, f32[8,128]{1,0:T(8,128)S(1)}) custom-call(s32[1]{0:T(128)} %get-tuple-element.48.mine, bf16[64,3712]{1,0:T(8,128)(2,1)S(1)} %get-tuple-element.49.refs_0_.near, ...), custom_call_target="tpu_custom_call" | custom-call | flops 5637144576 | bytes 3670016 | tf_op jit(solution)/shard_map/expert_block/pallas_call | solution.py:371
  64.5 2.6 %collective-permute-done.15.refs_1_.refs_2_ = bf16[32,3712]{1,0:T(8,128)(2,1)S(1)} collective-permute-done((bf16[32,3712]{1,0:T(8,128)(2,1)S(1)}, bf16[32,3712]{1,0:T(8,128)(2,1)S(1)}, u32[]{:S(2)}, u32[]{:S(2)}) %collective-permute-start.15) | collective-permute-done | bytes 237600 | tf_op jit(solution)/shard_map/ppermute | solution.py:412
  68.7 2.6 %collective-permute-done.17.refs_1_ = bf16[96,3584]{1,0:T(8,128)(2,1)S(1)} collective-permute-done((bf16[96,3584]{1,0:T(8,128)(2,1)S(1)}, bf16[96,3584]{1,0:T(8,128)(2,1)S(1)}, u32[]{:S(2)}, u32[]{:S(2)}) %collective-permute-start.17) | collective-permute-done | bytes 688160 | tf_op jit(solution)/shard_map/ppermute | solution.py:412
  72.5 7.1 %expert_block.6 = (bf16[32,3584]{1,0:T(8,128)(2,1)S(1)}, bf16[96,3584]{1,0:T(8,128)(2,1)S(1)}, bf16[32,3584]{1,0:T(8,128)(2,1)S(1)}, bf16[96,3584]{1,0:T(8,128)(2,1)S(1)}, f32[8,128]{1,0:T(8,128)S(1)}) custom-call(s32[1]{0:T(128)} %get-tuple-element.48.mine, bf16[64,3712]{1,0:T(8,128)(2,1)S(1)} %get-tuple-element.49.refs_0_.near, ...), custom_call_target="tpu_custom_call" | custom-call | flops 5637144576 | bytes 3670016 | tf_op jit(solution)/shard_map/expert_block/pallas_call | solution.py:371
  82.8 2.2 %collective-permute-start.26 = (bf16[32,3584]{1,0:T(8,128)(2,1)S(1)}, bf16[32,3584]{1,0:T(8,128)(2,1)S(1)}, u32[]{:S(2)}, u32[]{:S(2)}) collective-permute-start(bf16[32,3584]{1,0:T(8,128)(2,1)S(1)} %get-tuple-element.71.refs_4_), channel_id=1, source_target_pairs={{0,4},{1,5},{2,6},{3,7},{4,0},{5,1},{6,2},{7,3},{8,12},{9,13},{10,... | collective-permute-start | bytes 688136 | tf_op jit(solution)/shard_map/ppermute | solution.py:412
  86.2 6.9 %expert_block.7 = (bf16[32,3584]{1,0:T(8,128)(2,1)S(1)}, bf16[96,3584]{1,0:T(8,128)(2,1)S(1)}, bf16[32,3584]{1,0:T(8,128)(2,1)S(1)}, bf16[96,3584]{1,0:T(8,128)(2,1)S(1)}, f32[8,128]{1,0:T(8,128)S(1)}) custom-call(s32[1]{0:T(128)} %get-tuple-element.48.mine, bf16[64,3712]{1,0:T(8,128)(2,1)S(1)} %get-tuple-element.49.refs_0_.near, ...), custom_call_target="tpu_custom_call" | custom-call | flops 5637144576 | bytes 3670016 | tf_op jit(solution)/shard_map/expert_block/pallas_call | solution.py:371
  93.1 2.2 %collective-permute-done.28.got = bf16[48,3584]{1,0:T(8,128)(2,1)S(1)} collective-permute-done((bf16[48,3584]{1,0:T(8,128)(2,1)S(1)}, bf16[48,3584]{1,0:T(8,128)(2,1)S(1)}, u32[]{:S(2)}, u32[]{:S(2)}) %collective-permute-start.28) | collective-permute-done | bytes 344096 | tf_op jit(solution)/shard_map/ppermute | solution.py:412
  96.4 2.6 %collective-permute-start.27 = (bf16[16,3584]{1,0:T(8,128)(2,1)S(1)}, bf16[16,3584]{1,0:T(8,128)(2,1)S(1)}, u32[]{:S(2)}, u32[]{:S(2)}) collective-permute-start(bf16[16,3584]{1,0:T(8,128)(2,1)S(1)} %pass_on.5.refs_1_), channel_id=1, source_target_pairs={{0,8},{1,9},{2,10},{3,11},{4,12},{5,13},{6,14},{7,15},{8,0},{9,1},... | collective-permute-start | bytes 344072 | tf_op jit(solution)/shard_map/ppermute | solution.py:412
  100.1 4.7 %collective-permute-done.29.got = bf16[32,3584]{1,0:T(8,128)(2,1)S(1)} collective-permute-done((bf16[32,3584]{1,0:T(8,128)(2,1)S(1)}, bf16[32,3584]{1,0:T(8,128)(2,1)S(1)}, u32[]{:S(2)}, u32[]{:S(2)}) %collective-permute-start.29) | collective-permute-done | bytes 229408 | tf_op jit(solution)/shard_map/ppermute | solution.py:412
  106.3 3.9 %collective-permute-done.32.got = bf16[48,3584]{1,0:T(8,128)(2,1)S(1)} collective-permute-done((bf16[48,3584]{1,0:T(8,128)(2,1)S(1)}, bf16[48,3584]{1,0:T(8,128)(2,1)S(1)}, u32[]{:S(2)}, u32[]{:S(2)}) %collective-permute-start.32) | collective-permute-done | bytes 344096 | tf_op jit(solution)/shard_map/ppermute | solution.py:412
  111.1 2.8 %collective-permute-done.24.refs_0_ = bf16[32,3584]{1,0:T(8,128)(2,1)S(1)} collective-permute-done((bf16[32,3584]{1,0:T(8,128)(2,1)S(1)}, bf16[32,3584]{1,0:T(8,128)(2,1)S(1)}, u32[]{:S(2)}, u32[]{:S(2)}) %collective-permute-start.24) | collective-permute-done | bytes 229408 | tf_op jit(solution)/shard_map/ppermute | solution.py:412
  113.9 2.5 %collective-permute-done.33.got = bf16[32,3584]{1,0:T(8,128)(2,1)S(1)} collective-permute-done((bf16[32,3584]{1,0:T(8,128)(2,1)S(1)}, bf16[32,3584]{1,0:T(8,128)(2,1)S(1)}, u32[]{:S(2)}, u32[]{:S(2)}) %collective-permute-start.33) | collective-permute-done | bytes 229408 | tf_op jit(solution)/shard_map/ppermute | solution.py:412
  118.7 4.8 %collective-permute-done.34 = bf16[16,3584]{1,0:T(8,128)(2,1)S(1)} collective-permute-done((bf16[16,3584]{1,0:T(8,128)(2,1)S(1)}, bf16[16,3584]{1,0:T(8,128)(2,1)S(1)}, u32[]{:S(2)}, u32[]{:S(2)}) %collective-permute-start.34) | collective-permute-done | bytes 114720 | tf_op jit(solution)/shard_map/ppermute | solution.py:412
  (105 shorter events, 27.4 us)
Async XLA Ops:
  1.9 31.5 %collective-permute-start = (bf16[64,3712]{1,0:T(8,128)(2,1)S(1)}, bf16[64,3712]{1,0:T(8,128)(2,1)S(1)}, u32[]{:S(2)}, u32[]{:S(2)}) collective-permute-start(bf16[64,3712]{1,0:T(8,128)(2,1)S(1)} %get-tuple-element.49.refs_0_.near), channel_id=1, source_target_pairs={{0,2},{1,3},{2,0},{3,1},{4,6},{5,7},{6,4},{7,5},{8,10},{9,11},{10,... | collective-permute-start | bytes 1425416 | tf_op jit(solution)/shard_map/ppermute | solution.py:412
  4.9 22.1 %collective-permute-start.5 = (bf16[32,3712]{1,0:T(8,128)(2,1)S(1)}, bf16[32,3712]{1,0:T(8,128)(2,1)S(1)}, u32[]{:S(2)}, u32[]{:S(2)}) collective-permute-start(bf16[32,3712]{1,0:T(8,128)(2,1)S(1)} %get-tuple-element.93), channel_id=1, source_target_pairs={{0,4},{1,5},{2,6},{3,7},{4,0},{5,1},{6,2},{7,3},{8,12},{9,13},{10,... | collective-permute-start | bytes 712712 | tf_op jit(solution)/shard_map/ppermute | solution.py:412
  6.5 20.5 %collective-permute-start.2 = (bf16[32,3712]{1,0:T(8,128)(2,1)S(1)}, bf16[32,3712]{1,0:T(8,128)(2,1)S(1)}, u32[]{:S(2)}, u32[]{:S(2)}) collective-permute-start(bf16[32,3712]{1,0:T(8,128)(2,1)S(1)} %get-tuple-element.94), channel_id=1, source_target_pairs={{0,4},{1,5},{2,6},{3,7},{4,0},{5,1},{6,2},{7,3},{8,12},{9,13},{10,... | collective-permute-start | bytes 712712 | tf_op jit(solution)/shard_map/ppermute | solution.py:412
  7.0 20.0 %collective-permute-start.3 = (bf16[32,3712]{1,0:T(8,128)(2,1)S(1)}, bf16[32,3712]{1,0:T(8,128)(2,1)S(1)}, u32[]{:S(2)}, u32[]{:S(2)}) collective-permute-start(bf16[32,3712]{1,0:T(8,128)(2,1)S(1)} %get-tuple-element.94), channel_id=1, source_target_pairs={{0,8},{1,9},{2,10},{3,11},{4,12},{5,13},{6,14},{7,15},{8,0},{9,1},... | collective-permute-start | bytes 712712 | tf_op jit(solution)/shard_map/ppermute | solution.py:412
  9.6 20.0 %collective-permute-start.4 = (bf16[32,3712]{1,0:T(8,128)(2,1)S(1)}, bf16[32,3712]{1,0:T(8,128)(2,1)S(1)}, u32[]{:S(2)}, u32[]{:S(2)}) collective-permute-start(bf16[32,3712]{1,0:T(8,128)(2,1)S(1)} %get-tuple-element.94), channel_id=1, source_target_pairs={{0,12},{1,13},{2,14},{3,15},{4,8},{5,9},{6,10},{7,11},{8,4},{9,5},... | collective-permute-start | bytes 712712 | tf_op jit(solution)/shard_map/ppermute | solution.py:412
  29.6 12.6 %collective-permute-start.6 = (bf16[48,3712]{1,0:T(8,128)(2,1)S(1)}, bf16[48,3712]{1,0:T(8,128)(2,1)S(1)}, u32[]{:S(2)}, u32[]{:S(2)}) collective-permute-start(bf16[48,3712]{1,0:T(8,128)(2,1)S(1)} %pack.18.refs_2_.refs_0_.z), channel_id=1, source_target_pairs={{0,2},{1,3},{2,0},{3,1},{4,6},{5,7},{6,4},{7,5},{8,10},{9,11},{10,... | collective-permute-start | bytes 1069064 | tf_op jit(solution)/shard_map/ppermute | solution.py:412
  30.3 11.9 %collective-permute-start.7 = (bf16[32,3712]{1,0:T(8,128)(2,1)S(1)}, bf16[32,3712]{1,0:T(8,128)(2,1)S(1)}, u32[]{:S(2)}, u32[]{:S(2)}) collective-permute-start(bf16[32,3712]{1,0:T(8,128)(2,1)S(1)} %pack.20), channel_id=1, source_target_pairs={{0,8},{1,9},{2,10},{3,11},{4,12},{5,13},{6,14},{7,15},{8,0},{9,1},... | collective-permute-start | bytes 712712 | tf_op jit(solution)/shard_map/ppermute | solution.py:412
  33.4 11.2 %collective-permute-start.1 = (bf16[128,3712]{1,0:T(8,128)(2,1)S(1)}, bf16[128,3712]{1,0:T(8,128)(2,1)S(1)}, u32[]{:S(2)}, u32[]{:S(2)}) collective-permute-start(bf16[128,3712]{1,0:T(8,128)(2,1)S(1)} %pack.17), channel_id=1, source_target_pairs={{0,1},{1,0},{2,3},{3,2},{4,5},{5,4},{6,7},{7,6},{8,9},{9,8},{10,11... | collective-permute-start | bytes 2850824 | tf_op jit(solution)/shard_map/ppermute | solution.py:412
  42.4 10.7 %collective-permute-start.9 = (bf16[48,3712]{1,0:T(8,128)(2,1)S(1)}, bf16[48,3712]{1,0:T(8,128)(2,1)S(1)}, u32[]{:S(2)}, u32[]{:S(2)}) collective-permute-start(bf16[48,3712]{1,0:T(8,128)(2,1)S(1)} %pack.19.refs_3_.refs_0_.z), channel_id=1, source_target_pairs={{0,2},{1,3},{2,0},{3,1},{4,6},{5,7},{6,4},{7,5},{8,10},{9,11},{10,... | collective-permute-start | bytes 1069064 | tf_op jit(solution)/shard_map/ppermute | solution.py:412
  44.0 7.7 %collective-permute-start.10 = (bf16[16,3712]{1,0:T(8,128)(2,1)S(1)}, bf16[16,3712]{1,0:T(8,128)(2,1)S(1)}, u32[]{:S(2)}, u32[]{:S(2)}) collective-permute-start(bf16[16,3712]{1,0:T(8,128)(2,1)S(1)} %pack.23), channel_id=1, source_target_pairs={{0,8},{1,9},{2,10},{3,11},{4,12},{5,13},{6,14},{7,15},{8,0},{9,1},... | collective-permute-start | bytes 356360 | tf_op jit(solution)/shard_map/ppermute | solution.py:412
  53.8 13.3 %collective-permute-start.15 = (bf16[32,3712]{1,0:T(8,128)(2,1)S(1)}, bf16[32,3712]{1,0:T(8,128)(2,1)S(1)}, u32[]{:S(2)}, u32[]{:S(2)}) collective-permute-start(bf16[32,3712]{1,0:T(8,128)(2,1)S(1)} %pack.26.refs_1_), channel_id=1, source_target_pairs={{0,8},{1,9},{2,10},{3,11},{4,12},{5,13},{6,14},{7,15},{8,0},{9,1},... | collective-permute-start | bytes 712712 | tf_op jit(solution)/shard_map/ppermute | solution.py:412
  54.7 13.4 %collective-permute-start.13 = (bf16[48,3712]{1,0:T(8,128)(2,1)S(1)}, bf16[48,3712]{1,0:T(8,128)(2,1)S(1)}, u32[]{:S(2)}, u32[]{:S(2)}) collective-permute-start(bf16[48,3712]{1,0:T(8,128)(2,1)S(1)} %pack.21.refs_2_.refs_0_.z), channel_id=1, source_target_pairs={{0,2},{1,3},{2,0},{3,1},{4,6},{5,7},{6,4},{7,5},{8,10},{9,11},{10,... | collective-permute-start | bytes 1069064 | tf_op jit(solution)/shard_map/ppermute | solution.py:412
  55.4 12.5 %collective-permute-start.14 = (bf16[32,3712]{1,0:T(8,128)(2,1)S(1)}, bf16[32,3712]{1,0:T(8,128)(2,1)S(1)}, u32[]{:S(2)}, u32[]{:S(2)}) collective-permute-start(bf16[32,3712]{1,0:T(8,128)(2,1)S(1)} %pack.24.refs_3_), channel_id=1, source_target_pairs={{0,4},{1,5},{2,6},{3,7},{4,0},{5,1},{6,2},{7,3},{8,12},{9,13},{10,... | collective-permute-start | bytes 712712 | tf_op jit(solution)/shard_map/ppermute | solution.py:412
  68.7 12.5 %collective-permute-start.18 = (bf16[64,3584]{1,0:T(8,128)(2,1)S(1)}, bf16[64,3584]{1,0:T(8,128)(2,1)S(1)}, u32[]{:S(2)}, u32[]{:S(2)}) collective-permute-start(bf16[64,3584]{1,0:T(8,128)(2,1)S(1)} %get-tuple-element.61.refs_0_), channel_id=1, source_target_pairs={{0,4},{1,5},{2,6},{3,7},{4,0},{5,1},{6,2},{7,3},{8,12},{9,13},{10,... | collective-permute-start | bytes 1376264 | tf_op jit(solution)/shard_map/ppermute | solution.py:412
  71.5 10.2 %collective-permute-start.19 = (bf16[48,3584]{1,0:T(8,128)(2,1)S(1)}, bf16[48,3584]{1,0:T(8,128)(2,1)S(1)}, u32[]{:S(2)}, u32[]{:S(2)}) collective-permute-start(bf16[48,3584]{1,0:T(8,128)(2,1)S(1)} %get-tuple-element.66.refs_0_), channel_id=1, source_target_pairs={{0,2},{1,3},{2,0},{3,1},{4,6},{5,7},{6,4},{7,5},{8,10},{9,11},{10,... | collective-permute-start | bytes 1032200 | tf_op jit(solution)/shard_map/ppermute | solution.py:412
  82.3 14.0 %collective-permute-start.23 = (bf16[32,3584]{1,0:T(8,128)(2,1)S(1)}, bf16[32,3584]{1,0:T(8,128)(2,1)S(1)}, u32[]{:S(2)}, u32[]{:S(2)}) collective-permute-start(bf16[32,3584]{1,0:T(8,128)(2,1)S(1)} %pass_on.4.refs_3_), channel_id=1, source_target_pairs={{0,8},{1,9},{2,10},{3,11},{4,12},{5,13},{6,14},{7,15},{8,0},{9,1},... | collective-permute-start | bytes 688136 | tf_op jit(solution)/shard_map/ppermute | solution.py:412
  82.8 12.7 %collective-permute-start.26 = (bf16[32,3584]{1,0:T(8,128)(2,1)S(1)}, bf16[32,3584]{1,0:T(8,128)(2,1)S(1)}, u32[]{:S(2)}, u32[]{:S(2)}) collective-permute-start(bf16[32,3584]{1,0:T(8,128)(2,1)S(1)} %get-tuple-element.71.refs_4_), channel_id=1, source_target_pairs={{0,4},{1,5},{2,6},{3,7},{4,0},{5,1},{6,2},{7,3},{8,12},{9,13},{10,... | collective-permute-start | bytes 688136 | tf_op jit(solution)/shard_map/ppermute | solution.py:412
  85.2 10.2 %collective-permute-start.28 = (bf16[48,3584]{1,0:T(8,128)(2,1)S(1)}, bf16[48,3584]{1,0:T(8,128)(2,1)S(1)}, u32[]{:S(2)}, u32[]{:S(2)}) collective-permute-start(bf16[48,3584]{1,0:T(8,128)(2,1)S(1)} %get-tuple-element.74.refs_0_), channel_id=1, source_target_pairs={{0,2},{1,3},{2,0},{3,1},{4,6},{5,7},{6,4},{7,5},{8,10},{9,11},{10,... | collective-permute-start | bytes 1032200 | tf_op jit(solution)/shard_map/ppermute | solution.py:412
  95.4 9.3 %collective-permute-start.29 = (bf16[32,3584]{1,0:T(8,128)(2,1)S(1)}, bf16[32,3584]{1,0:T(8,128)(2,1)S(1)}, u32[]{:S(2)}, u32[]{:S(2)}) collective-permute-start(bf16[32,3584]{1,0:T(8,128)(2,1)S(1)} %get-tuple-element.83.refs_2_), channel_id=1, source_target_pairs={{0,4},{1,5},{2,6},{3,7},{4,0},{5,1},{6,2},{7,3},{8,12},{9,13},{10,... | collective-permute-start | bytes 688136 | tf_op jit(solution)/shard_map/ppermute | solution.py:412
  95.8 9.2 %collective-permute-start.22 = (bf16[128,3584]{1,0:T(8,128)(2,1)S(1)}, bf16[128,3584]{1,0:T(8,128)(2,1)S(1)}, u32[]{:S(2)}, u32[]{:S(2)}) collective-permute-start(bf16[128,3584]{1,0:T(8,128)(2,1)S(1)} %pack.32), channel_id=1, source_target_pairs={{0,1},{1,0},{2,3},{3,2},{4,5},{5,4},{6,7},{7,6},{8,9},{9,8},{10,11... | collective-permute-start | bytes 2752520 | tf_op jit(solution)/shard_map/ppermute | solution.py:412
  96.4 14.7 %collective-permute-start.27 = (bf16[16,3584]{1,0:T(8,128)(2,1)S(1)}, bf16[16,3584]{1,0:T(8,128)(2,1)S(1)}, u32[]{:S(2)}, u32[]{:S(2)}) collective-permute-start(bf16[16,3584]{1,0:T(8,128)(2,1)S(1)} %pass_on.5.refs_1_), channel_id=1, source_target_pairs={{0,8},{1,9},{2,10},{3,11},{4,12},{5,13},{6,14},{7,15},{8,0},{9,1},... | collective-permute-start | bytes 344072 | tf_op jit(solution)/shard_map/ppermute | solution.py:412
  99.3 11.0 %collective-permute-start.32 = (bf16[48,3584]{1,0:T(8,128)(2,1)S(1)}, bf16[48,3584]{1,0:T(8,128)(2,1)S(1)}, u32[]{:S(2)}, u32[]{:S(2)}) collective-permute-start(bf16[48,3584]{1,0:T(8,128)(2,1)S(1)} %get-tuple-element.87.refs_0_), channel_id=1, source_target_pairs={{0,2},{1,3},{2,0},{3,1},{4,6},{5,7},{6,4},{7,5},{8,10},{9,11},{10,... | collective-permute-start | bytes 1032200 | tf_op jit(solution)/shard_map/ppermute | solution.py:412
  104.8 13.0 %collective-permute-start.31 = (bf16[16,3584]{1,0:T(8,128)(2,1)S(1)}, bf16[16,3584]{1,0:T(8,128)(2,1)S(1)}, u32[]{:S(2)}, u32[]{:S(2)}) collective-permute-start(bf16[16,3584]{1,0:T(8,128)(2,1)S(1)} %pass_on.6), channel_id=1, source_target_pairs={{0,8},{1,9},{2,10},{3,11},{4,12},{5,13},{6,14},{7,15},{8,0},{9,1},... | collective-permute-start | bytes 344072 | tf_op jit(solution)/shard_map/ppermute | solution.py:412
  105.4 8.6 %collective-permute-start.24 = (bf16[32,3584]{1,0:T(8,128)(2,1)S(1)}, bf16[32,3584]{1,0:T(8,128)(2,1)S(1)}, u32[]{:S(2)}, u32[]{:S(2)}) collective-permute-start(bf16[32,3584]{1,0:T(8,128)(2,1)S(1)} %pad_maximum_fusion), channel_id=1, source_target_pairs={{0,2},{1,3},{2,0},{3,1},{4,6},{5,7},{6,4},{7,5},{8,10},{9,11},{10,... | collective-permute-start | bytes 688136 | tf_op jit(solution)/shard_map/ppermute | solution.py:412
  (17 other events, 106.0 us)
